TPU v7x, 32 devices: a whole 2x2x4 slice. The times are simulated.
32 devices in a mesh: row: 4 (over x, core), col: 8 (over z, y).
Axes of the slice: x: 2, y: 2, z: 4, core: 2. Of those that a mesh axis runs over, the one named last changes fastest.
Arguments:
- tokens: bfloat16 [4096, 16384], P('row', 'col'), may hold values from -6 to 6
- up_weight: bfloat16 [16384, 28672], P('row', 'col'), may hold values from -0.0625 to 0.0625
Outputs:
- projected: bfloat16 [4096, 28672], P('row', 'col')
All inputs are finite; a program needn't handle non-finite values.
Results may differ from a plain program's by a relative error of at most 0.001.
Values may be sent and summed in bfloat16 or wider, within the bound.
No kernel may reach another device: no remote copies, remote signals or barrier semaphores. Data moves between devices by JAX's collectives and lax.ppermute only.
A program may use at most 192 MiB of HBM per device.

v0:
```python
import jax
import jax.numpy as jnp
from jax import lax
from jax.sharding import PartitionSpec as P


def from_root(value, axis, source):
    kept = jnp.where(lax.axis_index(axis) == source, value, 0).astype(value.dtype)
    return lax.psum(kept, axis)


def from_behind(x, axis, by):
    count = lax.axis_size(axis)
    return lax.ppermute(x, axis, [(i, (i + by) % count) for i in range(count)])


def body(tokens, up_weight):
    row_index = lax.axis_index("row")
    col_count = lax.axis_size("col")
    pieces_list = []
    for position in range(4):
        pieces_list.append(from_root(tokens, "col", (2 * row_index + position) % col_count))
    gathered = jnp.concatenate(pieces_list, axis=1)
    split_at = up_weight.shape[0]
    own_part = jnp.dot(gathered[:, :split_at], up_weight, preferred_element_type=jnp.float32)
    following = from_behind(up_weight, "row", -1)
    next_part = jnp.dot(gathered[:, split_at:], following, preferred_element_type=jnp.float32)
    return (own_part + next_part).astype(jnp.bfloat16)


def solution(mesh):
    placed = (P("row", "col"), P("row", "col"))
    return jax.shard_map(
        body, mesh=mesh, in_specs=placed, out_specs=P("row", "col"), check_vma=False
    )
```

profile of v0, /device:TPU:1, one launch (start us, length us, event | category | flops | bytes accessed | tf_op | source)
XLA Modules:
  0.0 609.3 jit_solution(7907942922101117124)
XLA Ops:
  6.5 0.0 all-reduce.3.cloned.1.call-start
  6.5 0.1 collective-permute-start
  6.6 7.6 %broadcast_select_fusion.1 = (bf16[1024,2048]{1,0:T(8,128)(2,1)}, bf16[1024,2048]{1,0:T(8,128)(2,1)}, bf16[1024,2048]{1,0:T(8,128)(2,1)}, bf16[1024,2048]{1,0:T(8,128)(2,1)}) fusion(bf16[1024,2048]{1,0:T(8,128)(2,1)} %param.2, pred[]{:T(512)S(6)} %eq.19, pred[]{:T(512)S(6)} %eq.18, pred[]{:T(512)S(6)} %eq.17, pred[]{:T(512)S(6)} %eq.20), kind=kLoop, calls=%fused_computation.10 | loop fusion | flops 8388608 | bytes 20971524 | tf_op jit(solution)/shard_map/jit(_where)/select_n | solution.py:8
  14.2 0.0 all-reduce.3.cloned.1.call-update
  14.2 514.9 %all-reduce.3.cloned.1.call-done = (bf16[1024,2048]{1,0:T(8,128)(2,1)}, bf16[1024,2048]{1,0:T(8,128)(2,1)}, bf16[1024,2048]{1,0:T(8,128)(2,1)}, bf16[1024,2048]{1,0:T(8,128)(2,1)}) async-done(((bf16[1024,2048]{1,0:T(8,128)(2,1)}, bf16[1024,2048]{1,0:T(8,128)(2,1)}, bf16[1024,2048]{1,0:T(8,128)(2,1)}, bf16[1024,2048]{1,0:T(8,128)(2,1)}), (bf16[1024,2048]{1,0:T(8,128)(2,1)}, bf16[1024,2048]{1,0:T(8,128)(2,1)}, ...) | async-done | bytes 16777232 | tf_op jit(solution)/shard_map/psum | solution.py:9
  529.1 0.0 copy-start
  529.1 0.0 copy-start.1
  529.1 37.6 %fusion = f32[1024,3584]{1,0:T(8,128)} fusion(bf16[4096,3584]{1,0:T(8,128)(2,1)} %param.3, bf16[1024,2048]{1,0:T(8,128)(2,1)} %get-tuple-element.5, bf16[1024,2048]{1,0:T(8,128)(2,1)} %get-tuple-element.6), kind=kOutput, calls=%fused_computation.1 | convolution fusion | flops 30081548288 | bytes 52428800 | tf_op jit(solution)/shard_map/dot_general | solution.py:25
  566.8 0.0 collective-permute-done
  566.8 0.0 copy-done
  566.8 0.0 copy-done.1
  566.8 35.7 %add_convert_fusion = bf16[1024,3584]{1,0:T(8,128)(2,1)} fusion(f32[1024,3584]{1,0:T(8,128)} %fusion, bf16[4096,3584]{1,0:T(8,128)(2,1)} %collective-permute-done, bf16[1024,2048]{1,0:T(8,128)(2,1)S(1)} %copy-done, bf16[1024,2048]{1,0:T(8,128)(2,1)S(1)} %copy-done.1), kind=kOutput, calls=%fused_computation | convolution fusion | flops 30088888320 | bytes 59768832 | tf_op jit(solution)/shard_map/dot_general | solution.py:27
Async XLA Ops:
  6.5 522.6 %all-reduce.3.cloned.1.call-start = ((), (), s32[]{:S(2)}) async-start(), calls=%async_computation | async-start | bytes 33554432 | tf_op jit(solution)/shard_map/psum | solution.py:9
  6.5 560.2 %collective-permute-start = (bf16[4096,3584]{1,0:T(8,128)(2,1)}, bf16[4096,3584]{1,0:T(8,128)(2,1)}, u32[]{:S(2)}, u32[]{:S(2)}) collective-permute-start(bf16[4096,3584]{1,0:T(8,128)(2,1)} %param.3), channel_id=1, source_target_pairs={{0,24},{8,0},{16,8},{24,16},{1,25},{9,1},{17,9},{25,17},{2,26},{10... | collective-permute-start | bytes 88080392 | tf_op jit(solution)/shard_map/ppermute | solution.py:14
  529.1 37.7 %copy-start = (bf16[1024,2048]{1,0:T(8,128)(2,1)S(1)}, bf16[1024,2048]{1,0:T(8,128)(2,1)}, u32[]{:S(2)}) copy-start(bf16[1024,2048]{1,0:T(8,128)(2,1)} %get-tuple-element.7) | copy-start | bytes 12582916
  529.1 37.7 %copy-start.1 = (bf16[1024,2048]{1,0:T(8,128)(2,1)S(1)}, bf16[1024,2048]{1,0:T(8,128)(2,1)}, u32[]{:S(2)}) copy-start(bf16[1024,2048]{1,0:T(8,128)(2,1)} %get-tuple-element.8) | copy-start | bytes 12582916
Sparse Core Ops, SparseCore 0:
  14.3 514.7 all-reduce.2
where the time goes:
time: 610 us; the launch traced here: 609 us
  waiting for transfers between devices  515 us (84%)
  matrix products  73.4 us (12%)
  between operations  13.4 us (2%)
  other arithmetic  7.58 us (1%)
    psum x1, waiting for transfers between devices, from_root(): return lax.psum(kept, axis)  515 us
    dot_general x1, matrix products, body(): jnp.dot(gathered[:, :split_at], up_weight, preferred_element_type=jnp.flo...  37.6 us
    dot_general x1, matrix products, body(): jnp.dot(gathered[:, split_at:], following, preferred_element_type=jnp.flo...  35.7 us
  transfers between devices with their start and end apart: 2, of which 1 were waited for; matrix products, arithmetic and copies ran while one was open for 7% of the time, Pallas kernels for 0%

commit v1 on v0

v1 whole, which is shorter than its diff:
```python
import functools

import jax
import jax.numpy as jnp
from jax import lax
from jax.experimental import pallas as pl
from jax.experimental.pallas import tpu as pltpu
from jax.sharding import PartitionSpec as P

AXES = ("row", "col")
PIECES = 8
STREAM = (0, 1, 1, 1, 0, 1, 1, 1, 0, 1, 1, 0, 0, 0, 0, 0)
SUB = 2
BACK_STEPS = 3
MIB = 1024 * 1024
CHOOSE_VMEM = 4 * MIB
PRODUCT_VMEM = 12 * MIB
ANYWHERE = pl.BlockSpec(memory_space=pl.ANY)
NO_COST = pl.CostEstimate(flops=0, bytes_accessed=0, transcendentals=0)
TOKEN = jax.ShapeDtypeStruct((8, 128), jnp.float32)


def through(sources, scratch, out, sems):
    if len(sources) == 1:
        half = out.shape[0] // 2
        sources = [sources[0].at[pl.ds(0, half)], sources[0].at[pl.ds(half, half)]]
    inward, outward, at = [], [], 0
    for i, source in enumerate(sources):
        rows = pl.ds(at, source.shape[0])
        inward.append(pltpu.make_async_copy(source, scratch.at[rows], sems.at[2 * i]))
        outward.append(pltpu.make_async_copy(scratch.at[rows], out.at[rows], sems.at[2 * i + 1]))
        at += source.shape[0]
    for c in inward:
        c.start()
    for i, c in enumerate(outward):
        inward[i].wait()
        c.start()
    for c in outward:
        c.wait()


def choose_kernel(options, parts, which_of, start, size, *refs):
    out, _, scratch, sems = refs[-4:]
    index = which_of(lax.axis_index("row"), lax.axis_index("col"))
    for value in range(options):
        sources = refs[value * parts:(value + 1) * parts]
        if parts == 1 and sources[0].shape[0] != size:
            sources = [sources[0].at[pl.ds(start, size)]]

        @pl.when(index == value)
        def _(sources=sources):
            through(sources, scratch, out, sems)


def choose(which_of, options, start, size, tokens, into=None):
    parts = len(options[0])
    width, dtype = options[0][0].shape[1], options[0][0].dtype
    args = [a for option in options for a in option] + list(tokens)
    aliases = {}
    if into is not None:
        aliases = {len(args): 0}
        args.append(into)
    return pl.pallas_call(
        functools.partial(choose_kernel, len(options), parts, which_of, start, size),
        out_shape=(jax.ShapeDtypeStruct((size, width), dtype), TOKEN),
        in_specs=[ANYWHERE] * len(args),
        out_specs=(ANYWHERE, ANYWHERE),
        scratch_shapes=[pltpu.VMEM((size, width), dtype), pltpu.SemaphoreType.DMA((2 * max(parts, 2),))],
        input_output_aliases=aliases,
        compiler_params=pltpu.CompilerParams(vmem_limit_bytes=CHOOSE_VMEM),
        cost_estimate=NO_COST,
    )(*args)


def load_kernel(x, *refs):
    out, _, sem = refs[-3:]
    copy = pltpu.make_async_copy(x, out, sem)
    copy.start()
    copy.wait()


def load(x, tokens):
    return pl.pallas_call(
        load_kernel,
        out_shape=(pltpu.VMEM(x.shape, x.dtype), TOKEN),
        in_specs=[ANYWHERE] * (1 + len(tokens)),
        out_specs=(pl.BlockSpec(memory_space=pltpu.VMEM), ANYWHERE),
        scratch_shapes=[pltpu.SemaphoreType.DMA],
        compiler_params=pltpu.CompilerParams(vmem_limit_bytes=MIB),
        cost_estimate=NO_COST,
    )(pltpu.with_memory_space_constraint(x, pltpu.HBM), *tokens)


def gate_kernel(*refs):
    del refs


def gate(x, tokens):
    return pl.pallas_call(
        gate_kernel,
        out_shape=(jax.ShapeDtypeStruct(x.shape, x.dtype), TOKEN),
        in_specs=[ANYWHERE] * (1 + len(tokens)),
        out_specs=(ANYWHERE, ANYWHERE),
        input_output_aliases={0: 0},
        compiler_params=pltpu.CompilerParams(vmem_limit_bytes=MIB),
        cost_estimate=NO_COST,
    )(x, *tokens)


def product_kernel(start, has_back, tile, side_of, mine, other, weight, *refs):
    if has_back:
        back = refs[0]
        out, _, near, far, slots, in_sems, out_sems, held, back_sems = refs[-9:]
    else:
        out, _, near, far, slots, in_sems, out_sems = refs[-7:]
    many, half = near.shape
    tiles = weight.shape[1] // tile

    def back_copy(j, at):
        return pltpu.make_async_copy(back.at[:, pl.ds(at, tile)], held.at[:, pl.ds(at, tile)], back_sems.at[j])

    def out_copy(j, slot):
        at = pl.multiple_of(j * tile, tile)
        return pltpu.make_async_copy(slots.at[slot], out.at[pl.ds(start, many), pl.ds(at, tile)], out_sems.at[slot])

    fetch = [pltpu.make_async_copy(mine, near, in_sems.at[0]), pltpu.make_async_copy(other, far, in_sems.at[1])]
    for c in fetch:
        c.start()
    if has_back:
        for j in range(tiles):
            back_copy(j, j * tile).start()
    for c in fetch:
        c.wait()
    side = side_of(lax.axis_index("col"))
    near_rows = pl.ds(pl.multiple_of(side * half, half), half)
    far_rows = pl.ds(pl.multiple_of((1 - side) * half, half), half)

    def one_tile(j, carry):
        slot = lax.rem(j, 2)
        at = pl.multiple_of(j * tile, tile)
        total = jnp.dot(near[...], weight[near_rows, pl.ds(at, tile)], preferred_element_type=jnp.float32)
        total += jnp.dot(far[...], weight[far_rows, pl.ds(at, tile)], preferred_element_type=jnp.float32)
        if has_back:
            back_copy(j, at).wait()
            total += held[:, pl.ds(at, tile)]
        pl.when(j >= 2)(lambda: out_copy(j - 2, slot).wait())
        slots[slot] = total.astype(out.dtype)
        out_copy(j, slot).start()
        return carry

    lax.fori_loop(0, tiles, one_tile, 0)
    for j in range(max(0, tiles - 2), tiles):
        out_copy(j, j % 2).wait()


def product(side_of, mine, other, weight, tokens, back=None, into=None, start=0):
    depth, width = weight.shape
    many = mine.shape[0]
    tile = max(t for t in range(128, 513, 128) if width % t == 0)
    args = [mine, other, pltpu.with_memory_space_constraint(weight, pltpu.VMEM)]
    in_specs = [ANYWHERE, ANYWHERE, pl.BlockSpec(memory_space=pltpu.VMEM)]
    aliases = {}
    dtype = jnp.float32 if back is None else jnp.bfloat16
    scratch = [
        pltpu.VMEM((many, depth // 2), weight.dtype),
        pltpu.VMEM((many, depth // 2), weight.dtype),
        pltpu.VMEM((2, many, tile), dtype),
        pltpu.SemaphoreType.DMA((2,)),
        pltpu.SemaphoreType.DMA((2,)),
    ]
    total = many
    if back is not None:
        total = into[0]
        in_specs.append(ANYWHERE)
        args.append(back)
        scratch += [pltpu.VMEM((many, width), jnp.float32), pltpu.SemaphoreType.DMA((width // tile,))]
        if into[1] is not None:
            aliases = {len(args): 0}
            in_specs.append(ANYWHERE)
            args.append(into[1])
    in_specs += [ANYWHERE] * len(tokens)
    args += tokens
    return pl.pallas_call(
        functools.partial(product_kernel, start, back is not None, tile, side_of),
        out_shape=(jax.ShapeDtypeStruct((total, width), dtype), TOKEN),
        in_specs=in_specs,
        out_specs=(ANYWHERE, ANYWHERE),
        scratch_shapes=scratch,
        input_output_aliases=aliases,
        compiler_params=pltpu.CompilerParams(vmem_limit_bytes=PRODUCT_VMEM),
        cost_estimate=pl.CostEstimate(flops=4 * many * depth * width, bytes_accessed=0, transcendentals=0),
    )(*args)


def body(n_row, n_col, tokens, weight):
    inner = n_col // n_row
    assert inner == 2
    count = tokens.shape[0]
    size = count // PIECES

    def device(r, b, s):
        return (r % n_row) * n_col + (b % n_row) * inner + s

    sides = range(inner)
    chain = [(device(r, r - d, s), device(r, r - d - 1, s)) for r in range(n_row) for d in range(n_row - 1) for s in sides]
    chain += [(device(r - 1, r, s), device(r, r, s)) for r in range(n_row) for s in sides]
    everyone = [(r, b, s) for r in range(n_row) for b in range(n_row) for s in sides]
    swap_pairs = [(device(r, b, s), device(r, b, 1 - s)) for r, b, s in everyone]
    back_pairs = [(device(r, b, s), device(r - 1, b, s)) for r, b, s in everyone]

    def block_of(col):
        return lax.div(col, inner)

    def side_of(col):
        return lax.rem(col, inner)

    def distance(row, col):
        return lax.rem(row - block_of(col) + n_row, n_row)

    def crosses(row, col):
        return jnp.where(lax.rem(row + 1, n_row) == block_of(col), 0, 1)

    def sends(row, col):
        return jnp.where(row == block_of(col), 0, -1)

    tokens = pltpu.with_memory_space_constraint(tokens, pltpu.HBM)
    counts = [0, 0]
    pieces = []
    for group in STREAM:
        pieces.append((group, counts[group]))
        counts[group] += 1
    total = len(pieces)
    chunk = size // SUB
    chunks = total * SUB
    whole = SUB * (n_row + 1) - 1
    when = {at: at * SUB + whole + SUB for at, (group, _) in enumerate(pieces) if group == 1}
    sent_back = []
    for at in sorted(when):
        sent_back.append(max([when[at] + 1] + [b + BACK_STEPS for b in sent_back[-1:]]))
    for at, (group, piece) in enumerate(pieces):
        if group == 0:
            step = max(at * SUB + whole + SUB, sent_back[piece] + BACK_STEPS + 1)
            while step in when.values() or (step - whole) % SUB and step < chunks - SUB:
                step += 1
            when[at] = step

    def rows_of(k):
        return pieces[k // SUB][1] * size + k % SUB * chunk

    seen = []
    sent, held_last, mine, other, back, arriving = {}, {}, {}, {}, {}, {}
    out, waiting = None, []
    last_chain = chunks - 1 + SUB * (n_row - 1)
    first = 0 if pieces[0][0] == 1 else SUB
    for step in range(first, max(when.values()) + 1):
        if step <= last_chain + SUB:
            value, token = arriving.pop(step - SUB, None), None
            came = value
            if step < chunks and pieces[step // SUB][0] == 1:
                options = [[tokens]] if value is None else [[tokens], [value]]
                value, token = choose(crosses, options, rows_of(step), chunk, seen)
                seen = [token]
            else:
                came = None
            if 0 <= step - SUB < chunks and pieces[step // SUB - 1][0] == 0:
                value, token = choose(sends, [[tokens]], rows_of(step - SUB), chunk, seen, value)
                seen = [token]
            if token is None:
                value, token = gate(value, seen)
                seen = [token]
            sent[step] = value
            held_last[step] = value if came is None else came
            if step <= last_chain:
                with jax.named_scope(f"chain{step}"):
                    arriving[step] = lax.ppermute(value, AXES, chain)
        if step == first + SUB - 1:
            weight, token = load(weight, seen)
            seen = [token]
        if waiting and step >= sent_back[waiting[0][0]]:
            piece, partial = waiting.pop(0)
            if piece > 1:
                back[piece - 2], token = gate(back[piece - 2], seen)
                seen = [token]
            partial, token = gate(partial, seen)
            seen = [token]
            with jax.named_scope(f"back{piece}"):
                back[piece] = lax.ppermute(partial, AXES, back_pairs)
        at, part = divmod(step - whole, SUB)
        if part == 0 and 0 <= at < total:
            held = [sent] * (n_row - 1) + [held_last]
            options = [[held[d][(at + 1 + d) * SUB + k] for k in range(SUB)] for d in range(n_row)]
            mine[at], token = choose(distance, options, 0, size, seen)
            seen = [token]
            with jax.named_scope(f"swap{at}"):
                other[at] = lax.ppermute(mine[at], AXES, swap_pairs)
        for at in range(total):
            if when[at] != step:
                continue
            group, piece = pieces[at]
            if group == 1:
                partial, token = product(side_of, mine[at], other[at], weight, seen)
                seen = [token]
                waiting.append((piece, partial))
            else:
                out, token = product(
                    side_of, mine[at], other[at], weight, seen, back[piece], (count, out), piece * size
                )
                seen = [token]
    return out


def solution(mesh):
    n_row, n_col = mesh.shape["row"], mesh.shape["col"]
    placed = P("row", "col")
    return jax.shard_map(
        functools.partial(body, n_row, n_col), mesh=mesh, in_specs=(placed, placed), out_specs=placed, check_vma=False
    )
```

time: 610 us -> 326 us (0.53)
  waiting for transfers between devices: 515 us -> 111 us
  Pallas kernels: 0 us -> 116 us
  starting transfers between devices: 0.06 us -> 87.7 us
  matrix products: 73.4 us -> 0 us
  between operations: 13.4 us -> 1.06 us
  local copies, waits for them, and re-layouts: 0.01 us -> 9.68 us
  other arithmetic: 7.58 us -> 0 us
    psum x1 -> x0, waiting for transfers between devices: 515 us -> none  [from_root(): return lax.psum(kept, axis)]
    pallas_call x0 -> x91, Pallas kernels: none -> 116 us  [the longest x16 93.4 us: product(): pl.pallas_call(functools.partial(product_kernel, start, back is not None,...]
    ppermute x1 -> x60, waiting for transfers between devices: 0.01 us -> 111 us  [the longest x8 76 us: body(): back[piece] = lax.ppermute(partial, AXES, back_pairs)]
    ppermute x1 -> x60, starting transfers between devices: 0.06 us -> 87.7 us  [the longest x36 66.7 us: body(): arriving[step] = lax.ppermute(value, AXES, chain)]
    dot_general x2 -> x0, matrix products: 73.4 us -> none  [the longest x1 37.6 us: body(): jnp.dot(gathered[:, :split_at], up_weight, preferred_element_type=jnp.flo...]
    unnamed x4, local copies, waits for them, and re-layouts: 0.01 us -> 9.68 us
    select_n x1 -> x0, other arithmetic: 7.58 us -> none  [from_root(): jnp.where(lax.axis_index(axis) == source, value, 0).astype(value.dtype)]
  transfers between devices with their start and end apart: 2 -> 60, of which waited for: 1 -> 21; matrix products, arithmetic and copies ran while one was open for 7% -> 0% of each run, Pallas kernels for 0% -> 33%
where the time goes in v1:
time: 326 us; the launch traced here: 325 us
  Pallas kernels  116 us (36%)
  waiting for transfers between devices  111 us (34%)
  starting transfers between devices  87.7 us (27%)
  local copies, waits for them, and re-layouts  9.68 us (3%)
    pallas_call x16, Pallas kernels, product(): pl.pallas_call(functools.partial(product_kernel, start, back is not None,...  93.4 us
    ppermute x8, waiting for transfers between devices, body(): back[piece] = lax.ppermute(partial, AXES, back_pairs)  76 us
    ppermute x36, starting transfers between devices, body(): arriving[step] = lax.ppermute(value, AXES, chain)  66.7 us
    ppermute x36, waiting for transfers between devices, body(): arriving[step] = lax.ppermute(value, AXES, chain)  24.6 us
    ppermute x16, starting transfers between devices, body(): other[at] = lax.ppermute(mine[at], AXES, swap_pairs)  14.6 us
    pallas_call x48, Pallas kernels, choose(): pl.pallas_call(functools.partial(choose_kernel, len(options), parts, whic...  12.9 us
    ppermute x16, waiting for transfers between devices, body(): other[at] = lax.ppermute(mine[at], AXES, swap_pairs)  10.5 us
    unnamed x4, local copies, waits for them, and re-layouts  9.68 us
  transfers between devices with their start and end apart: 60, of which 21 were waited for; matrix products, arithmetic and copies ran while one was open for 0% of the time, Pallas kernels for 33%

profile of v1, /device:TPU:1, one launch (start us, length us, event | category | flops | bytes accessed | tf_op | source)
XLA Modules:
  0.0 325.2 jit_solution(16988184244706840136)
XLA Ops:
  0.1 4.2 %collective-permute-start = (bf16[64,2048]{1,0:T(8,128)(2,1)S(1)}, bf16[64,2048]{1,0:T(8,128)(2,1)S(1)}, u32[]{:S(2)}, u32[]{:S(2)}) collective-permute-start(bf16[64,2048]{1,0:T(8,128)(2,1)S(1)} %get-tuple-element.187.refs_0_), channel_id=1, source_target_pairs={{0,6},{1,7},{6,4},{7,5},{4,2},{5,3},{10,8},{11,9},{8,14},{9,15},{1... | collective-permute-start | bytes 786440 | tf_op jit(solution)/shard_map/chain2/ppermute | solution.py:275
  5.9 9.4 %shard_map.32 = (bf16[4096,3584]{1,0:T(8,128)(2,1)S(1)}, f32[8,128]{1,0:T(8,128)S(1)}) custom-call(bf16[4096,3584]{1,0:T(8,128)(2,1)} %x.1, f32[8,128]{1,0:T(8,128)S(1)} %get-tuple-element.191.refs_0_), custom_call_target="tpu_custom_call" | custom-call | tf_op jit(solution)/shard_map/pallas_call | solution.py:83
  15.2 9.7 %copy-done = bf16[4096,3584]{1,0:T(8,128)(2,1)} copy-done((bf16[4096,3584]{1,0:T(8,128)(2,1)}, bf16[4096,3584]{1,0:T(8,128)(2,1)S(1)}, u32[]{:S(2)}) %copy-start) | copy-done | bytes 29360152
  25.6 3.0 collective-permute-start.1
  30.0 4.8 %collective-permute-done.1.refs_1_ = bf16[64,2048]{1,0:T(8,128)(2,1)S(1)} collective-permute-done((bf16[64,2048]{1,0:T(8,128)(2,1)S(1)}, bf16[64,2048]{1,0:T(8,128)(2,1)S(1)}, u32[]{:S(2)}, u32[]{:S(2)}) %collective-permute-start.1) | collective-permute-done | bytes 262176 | tf_op jit(solution)/shard_map/chain4/ppermute | solution.py:275
  35.5 4.1 %collective-permute-start.3 = (bf16[64,2048]{1,0:T(8,128)(2,1)S(1)}, bf16[64,2048]{1,0:T(8,128)(2,1)S(1)}, u32[]{:S(2)}, u32[]{:S(2)}) collective-permute-start(bf16[64,2048]{1,0:T(8,128)(2,1)S(1)} %get-tuple-element.197.refs_4_.refs_2_.refs_0_), channel_id=1, source_target_pairs={{0,6},{1,7},{6,4},{7,5},{4,2},{5,3},{10,8},{11,9},{8,14},{9,15},{1... | collective-permute-start | bytes 786440 | tf_op jit(solution)/shard_map/chain6/ppermute | solution.py:275
  40.5 4.1 %collective-permute-start.6 = (bf16[64,2048]{1,0:T(8,128)(2,1)S(1)}, bf16[64,2048]{1,0:T(8,128)(2,1)S(1)}, u32[]{:S(2)}, u32[]{:S(2)}) collective-permute-start(bf16[64,2048]{1,0:T(8,128)(2,1)S(1)} %get-tuple-element.202.refs_5_.refs_3_.refs_1_), channel_id=1, source_target_pairs={{0,6},{1,7},{6,4},{7,5},{4,2},{5,3},{10,8},{11,9},{8,14},{9,15},{1... | collective-permute-start | bytes 786440 | tf_op jit(solution)/shard_map/chain7/ppermute | solution.py:275
  45.5 4.0 %collective-permute-start.5 = (bf16[64,2048]{1,0:T(8,128)(2,1)S(1)}, bf16[64,2048]{1,0:T(8,128)(2,1)S(1)}, u32[]{:S(2)}, u32[]{:S(2)}) collective-permute-start(bf16[64,2048]{1,0:T(8,128)(2,1)S(1)} %get-tuple-element.201.refs_6_.refs_4_.refs_2_.refs_0_), channel_id=1, source_target_pairs={{0,6},{1,7},{6,4},{7,5},{4,2},{5,3},{10,8},{11,9},{8,14},{9,15},{1... | collective-permute-start | bytes 786440 | tf_op jit(solution)/shard_map/chain8/ppermute | solution.py:275
  51.1 4.0 %collective-permute-start.8 = (bf16[64,2048]{1,0:T(8,128)(2,1)S(1)}, bf16[64,2048]{1,0:T(8,128)(2,1)S(1)}, u32[]{:S(2)}, u32[]{:S(2)}) collective-permute-start(bf16[64,2048]{1,0:T(8,128)(2,1)S(1)} %get-tuple-element.204.refs_7_.refs_5_.refs_3_.refs_1_), channel_id=1, source_target_pairs={{0,6},{1,7},{6,4},{7,5},{4,2},{5,3},{10,8},{11,9},{8,14},{9,15},{1... | collective-permute-start | bytes 786440 | tf_op jit(solution)/shard_map/chain9/ppermute | solution.py:275
  57.5 4.3 %collective-permute-done.8.refs_1_.refs_7_ = bf16[64,2048]{1,0:T(8,128)(2,1)S(1)} collective-permute-done((bf16[64,2048]{1,0:T(8,128)(2,1)S(1)}, bf16[64,2048]{1,0:T(8,128)(2,1)S(1)}, u32[]{:S(2)}, u32[]{:S(2)}) %collective-permute-start.8) | collective-permute-done | bytes 262176 | tf_op jit(solution)/shard_map/chain9/ppermute | solution.py:275
  64.0 3.7 %collective-permute-start.7 = (bf16[64,2048]{1,0:T(8,128)(2,1)S(1)}, bf16[64,2048]{1,0:T(8,128)(2,1)S(1)}, u32[]{:S(2)}, u32[]{:S(2)}) collective-permute-start(bf16[64,2048]{1,0:T(8,128)(2,1)S(1)} %get-tuple-element.209.refs_4_.refs_2_.refs_0_), channel_id=1, source_target_pairs={{0,6},{1,7},{6,4},{7,5},{4,2},{5,3},{10,8},{11,9},{8,14},{9,15},{1... | collective-permute-start | bytes 786440 | tf_op jit(solution)/shard_map/chain10/ppermute | solution.py:275
  68.1 4.8 %collective-permute-done.7.refs_1_.refs_6_ = bf16[64,2048]{1,0:T(8,128)(2,1)S(1)} collective-permute-done((bf16[64,2048]{1,0:T(8,128)(2,1)S(1)}, bf16[64,2048]{1,0:T(8,128)(2,1)S(1)}, u32[]{:S(2)}, u32[]{:S(2)}) %collective-permute-start.7) | collective-permute-done | bytes 262176 | tf_op jit(solution)/shard_map/chain10/ppermute | solution.py:275
  73.6 4.1 %collective-permute-start.9 = (bf16[64,2048]{1,0:T(8,128)(2,1)S(1)}, bf16[64,2048]{1,0:T(8,128)(2,1)S(1)}, u32[]{:S(2)}, u32[]{:S(2)}) collective-permute-start(bf16[64,2048]{1,0:T(8,128)(2,1)S(1)} %get-tuple-element.215.refs_4_.refs_2_.refs_0_), channel_id=1, source_target_pairs={{0,6},{1,7},{6,4},{7,5},{4,2},{5,3},{10,8},{11,9},{8,14},{9,15},{1... | collective-permute-start | bytes 786440 | tf_op jit(solution)/shard_map/chain12/ppermute | solution.py:275
  79.7 5.5 %shard_map.48 = (f32[128,3584]{1,0:T(8,128)S(1)}, f32[8,128]{1,0:T(8,128)S(1)}) custom-call(bf16[128,2048]{1,0:T(8,128)(2,1)S(1)} %get-tuple-element.216.mine, bf16[128,2048]{1,0:T(8,128)(2,1)S(1)} %collective-permute-done.10.other, bf16[4096,3584]{1,0:T(8,128)(2,1)S(1)} %copy-done.1, f32[8,128]{1,0:T(8,128)S(1)} %get-tuple-element.221.refs_0_), custom_call_target="tpu_custom_call" | custom-call | flops 7516192768 | tf_op jit(solution)/shard_map/pallas_call | solution.py:183
  85.9 2.5 collective-permute-start.20
  88.4 4.0 %collective-permute-start.14 = (bf16[64,2048]{1,0:T(8,128)(2,1)S(1)}, bf16[64,2048]{1,0:T(8,128)(2,1)S(1)}, u32[]{:S(2)}, u32[]{:S(2)}) collective-permute-start(bf16[64,2048]{1,0:T(8,128)(2,1)S(1)} %get-tuple-element.225.refs_5_.refs_3_.refs_1_), channel_id=1, source_target_pairs={{0,6},{1,7},{6,4},{7,5},{4,2},{5,3},{10,8},{11,9},{8,14},{9,15},{1... | collective-permute-start | bytes 786440 | tf_op jit(solution)/shard_map/chain13/ppermute | solution.py:275
  93.6 4.4 %collective-permute-done.14.refs_1_.refs_7_ = bf16[64,2048]{1,0:T(8,128)(2,1)S(1)} collective-permute-done((bf16[64,2048]{1,0:T(8,128)(2,1)S(1)}, bf16[64,2048]{1,0:T(8,128)(2,1)S(1)}, u32[]{:S(2)}, u32[]{:S(2)}) %collective-permute-start.14) | collective-permute-done | bytes 262176 | tf_op jit(solution)/shard_map/chain13/ppermute | solution.py:275
  98.7 4.1 %collective-permute-start.17 = (bf16[64,2048]{1,0:T(8,128)(2,1)S(1)}, bf16[64,2048]{1,0:T(8,128)(2,1)S(1)}, u32[]{:S(2)}, u32[]{:S(2)}) collective-permute-start(bf16[64,2048]{1,0:T(8,128)(2,1)S(1)} %get-tuple-element.234.refs_5_.refs_3_.refs_1_), channel_id=1, source_target_pairs={{0,6},{1,7},{6,4},{7,5},{4,2},{5,3},{10,8},{11,9},{8,14},{9,15},{1... | collective-permute-start | bytes 786440 | tf_op jit(solution)/shard_map/chain15/ppermute | solution.py:275
  104.3 5.5 %shard_map.53 = (f32[128,3584]{1,0:T(8,128)S(1)}, f32[8,128]{1,0:T(8,128)S(1)}) custom-call(bf16[128,2048]{1,0:T(8,128)(2,1)S(1)} %get-tuple-element.224.mine, bf16[128,2048]{1,0:T(8,128)(2,1)S(1)} %collective-permute-done.13.other, bf16[4096,3584]{1,0:T(8,128)(2,1)S(1)} %copy-done.1, f32[8,128]{1,0:T(8,128)S(1)} %get-tuple-element.230.refs_0_), custom_call_target="tpu_custom_call" | custom-call | flops 7516192768 | tf_op jit(solution)/shard_map/pallas_call | solution.py:183
  109.9 2.9 collective-permute-start.21
  112.9 3.2 collective-permute-done.16.other
  118.0 5.5 %shard_map.58 = (f32[128,3584]{1,0:T(8,128)S(1)}, f32[8,128]{1,0:T(8,128)S(1)}) custom-call(bf16[128,2048]{1,0:T(8,128)(2,1)S(1)} %get-tuple-element.233.mine, bf16[128,2048]{1,0:T(8,128)(2,1)S(1)} %collective-permute-done.16.other, bf16[4096,3584]{1,0:T(8,128)(2,1)S(1)} %copy-done.1, f32[8,128]{1,0:T(8,128)S(1)} %get-tuple-element.240.refs_0_), custom_call_target="tpu_custom_call" | custom-call | flops 7516192768 | tf_op jit(solution)/shard_map/pallas_call | solution.py:183
  124.3 2.4 collective-permute-start.18
  128.4 6.2 %shard_map.64 = (bf16[1024,3584]{1,0:T(8,128)(2,1)}, f32[8,128]{1,0:T(8,128)S(1)}) custom-call(bf16[128,2048]{1,0:T(8,128)(2,1)S(1)} %get-tuple-element.245.mine, bf16[128,2048]{1,0:T(8,128)(2,1)S(1)} %collective-permute-done.19.other, bf16[4096,3584]{1,0:T(8,128)(2,1)S(1)} %copy-done.1, f32[128,3584]{1,0:T(8,128)S(1)} %collective-permute-done.20.refs_0_, ...), custom_call_target="tpu_custom_call" | custom-call | flops 7516192768 | tf_op jit(solution)/shard_map/pallas_call | solution.py:183
  138.7 4.1 %collective-permute-start.25 = (bf16[64,2048]{1,0:T(8,128)(2,1)S(1)}, bf16[64,2048]{1,0:T(8,128)(2,1)S(1)}, u32[]{:S(2)}, u32[]{:S(2)}) collective-permute-start(bf16[64,2048]{1,0:T(8,128)(2,1)S(1)} %get-tuple-element.264.refs_5_.refs_3_.refs_1_), channel_id=1, source_target_pairs={{0,6},{1,7},{6,4},{7,5},{4,2},{5,3},{10,8},{11,9},{8,14},{9,15},{1... | collective-permute-start | bytes 786440 | tf_op jit(solution)/shard_map/chain21/ppermute | solution.py:275
  144.5 5.5 %shard_map.70 = (f32[128,3584]{1,0:T(8,128)S(1)}, f32[8,128]{1,0:T(8,128)S(1)}) custom-call(bf16[128,2048]{1,0:T(8,128)(2,1)S(1)} %get-tuple-element.254.mine, bf16[128,2048]{1,0:T(8,128)(2,1)S(1)} %collective-permute-done.23.other, bf16[4096,3584]{1,0:T(8,128)(2,1)S(1)} %copy-done.1, f32[8,128]{1,0:T(8,128)S(1)} %get-tuple-element.261.refs_0_), custom_call_target="tpu_custom_call" | custom-call | flops 7516192768 | tf_op jit(solution)/shard_map/pallas_call | solution.py:183
  150.1 2.7 collective-permute-start.29
  152.8 6.9 %collective-permute-done.27.refs_0_ = f32[128,3584]{1,0:T(8,128)S(1)} collective-permute-done((f32[128,3584]{1,0:T(8,128)S(1)}, f32[128,3584]{1,0:T(8,128)S(1)}, u32[]{:S(2)}, u32[]{:S(2)}) %collective-permute-start.27) | collective-permute-done | bytes 1835040 | tf_op jit(solution)/shard_map/back1/ppermute | solution.py:287
  160.8 5.5 %shard_map.76 = (f32[128,3584]{1,0:T(8,128)S(1)}, f32[8,128]{1,0:T(8,128)S(1)}) custom-call(bf16[128,2048]{1,0:T(8,128)(2,1)S(1)} %get-tuple-element.267.mine, bf16[128,2048]{1,0:T(8,128)(2,1)S(1)} %collective-permute-done.26.other, bf16[4096,3584]{1,0:T(8,128)(2,1)S(1)} %copy-done.1, f32[8,128]{1,0:T(8,128)S(1)} %get-tuple-element.273.refs_0_), custom_call_target="tpu_custom_call" | custom-call | flops 7516192768 | tf_op jit(solution)/shard_map/pallas_call | solution.py:183
  167.2 4.5 %collective-permute-done.30.other = bf16[128,2048]{1,0:T(8,128)(2,1)S(1)} collective-permute-done((bf16[128,2048]{1,0:T(8,128)(2,1)S(1)}, bf16[128,2048]{1,0:T(8,128)(2,1)S(1)}, u32[]{:S(2)}, u32[]{:S(2)}) %collective-permute-start.30) | collective-permute-done | bytes 524320 | tf_op jit(solution)/shard_map/swap7/ppermute | solution.py:295
  171.7 5.5 %shard_map.80 = (f32[128,3584]{1,0:T(8,128)S(1)}, f32[8,128]{1,0:T(8,128)S(1)}) custom-call(bf16[128,2048]{1,0:T(8,128)(2,1)S(1)} %get-tuple-element.278.mine, bf16[128,2048]{1,0:T(8,128)(2,1)S(1)} %collective-permute-done.30.other, bf16[4096,3584]{1,0:T(8,128)(2,1)S(1)} %copy-done.1, f32[8,128]{1,0:T(8,128)S(1)} %get-tuple-element.280.refs_0_), custom_call_target="tpu_custom_call" | custom-call | flops 7516192768 | tf_op jit(solution)/shard_map/pallas_call | solution.py:183
  178.9 13.7 %collective-permute-done.32.refs_0_ = f32[128,3584]{1,0:T(8,128)S(1)} collective-permute-done((f32[128,3584]{1,0:T(8,128)S(1)}, f32[128,3584]{1,0:T(8,128)S(1)}, u32[]{:S(2)}, u32[]{:S(2)}) %collective-permute-start.32) | collective-permute-done | bytes 1835040 | tf_op jit(solution)/shard_map/back2/ppermute | solution.py:287
  194.0 6.2 %shard_map.86 = (bf16[1024,3584]{1,0:T(8,128)(2,1)}, f32[8,128]{1,0:T(8,128)S(1)}) custom-call(bf16[128,2048]{1,0:T(8,128)(2,1)S(1)} %get-tuple-element.289.mine, bf16[128,2048]{1,0:T(8,128)(2,1)S(1)} %collective-permute-done.34.other, bf16[4096,3584]{1,0:T(8,128)(2,1)S(1)} %copy-done.1, ...), custom_call_target="tpu_custom_call", output_to_operand_aliasing={{0}: (4, {})} | custom-call | flops 7516192768 | tf_op jit(solution)/shard_map/pallas_call | solution.py:183
  201.9 15.7 %collective-permute-done.37.refs_0_ = f32[128,3584]{1,0:T(8,128)S(1)} collective-permute-done((f32[128,3584]{1,0:T(8,128)S(1)}, f32[128,3584]{1,0:T(8,128)S(1)}, u32[]{:S(2)}, u32[]{:S(2)}) %collective-permute-start.37) | collective-permute-done | bytes 1835040 | tf_op jit(solution)/shard_map/back3/ppermute | solution.py:287
  219.1 5.5 %shard_map.92 = (f32[128,3584]{1,0:T(8,128)S(1)}, f32[8,128]{1,0:T(8,128)S(1)}) custom-call(bf16[128,2048]{1,0:T(8,128)(2,1)S(1)} %get-tuple-element.304.mine, bf16[128,2048]{1,0:T(8,128)(2,1)S(1)} %collective-permute-done.39.other, bf16[4096,3584]{1,0:T(8,128)(2,1)S(1)} %copy-done.1, f32[8,128]{1,0:T(8,128)S(1)} %get-tuple-element.305.refs_0_), custom_call_target="tpu_custom_call" | custom-call | flops 7516192768 | tf_op jit(solution)/shard_map/pallas_call | solution.py:183
  225.5 6.2 %shard_map.94 = (bf16[1024,3584]{1,0:T(8,128)(2,1)}, f32[8,128]{1,0:T(8,128)S(1)}) custom-call(bf16[128,2048]{1,0:T(8,128)(2,1)S(1)} %get-tuple-element.308.mine, bf16[128,2048]{1,0:T(8,128)(2,1)S(1)} %collective-permute-done.41.other, bf16[4096,3584]{1,0:T(8,128)(2,1)S(1)} %copy-done.1, ...), custom_call_target="tpu_custom_call", output_to_operand_aliasing={{0}: (4, {})} | custom-call | flops 7516192768 | tf_op jit(solution)/shard_map/pallas_call | solution.py:183
  232.1 5.5 %shard_map.97 = (f32[128,3584]{1,0:T(8,128)S(1)}, f32[8,128]{1,0:T(8,128)S(1)}) custom-call(bf16[128,2048]{1,0:T(8,128)(2,1)S(1)} %get-tuple-element.303.mine, bf16[128,2048]{1,0:T(8,128)(2,1)S(1)} %collective-permute-done.38.other, bf16[4096,3584]{1,0:T(8,128)(2,1)S(1)} %copy-done.1, f32[8,128]{1,0:T(8,128)S(1)} %get-tuple-element.315.refs_0_), custom_call_target="tpu_custom_call" | custom-call | flops 7516192768 | tf_op jit(solution)/shard_map/pallas_call | solution.py:183
  237.7 5.5 %collective-permute-done.44.refs_0_ = f32[128,3584]{1,0:T(8,128)S(1)} collective-permute-done((f32[128,3584]{1,0:T(8,128)S(1)}, f32[128,3584]{1,0:T(8,128)S(1)}, u32[]{:S(2)}, u32[]{:S(2)}) %collective-permute-start.44) | collective-permute-done | bytes 1835040 | tf_op jit(solution)/shard_map/back4/ppermute | solution.py:287
  246.4 6.2 %shard_map.103 = (bf16[1024,3584]{1,0:T(8,128)(2,1)}, f32[8,128]{1,0:T(8,128)S(1)}) custom-call(bf16[128,2048]{1,0:T(8,128)(2,1)S(1)} %get-tuple-element.324.mine, bf16[128,2048]{1,0:T(8,128)(2,1)S(1)} %collective-permute-done.47.other, bf16[4096,3584]{1,0:T(8,128)(2,1)S(1)} %copy-done.1, ...), custom_call_target="tpu_custom_call", output_to_operand_aliasing={{0}: (4, {})} | custom-call | flops 7516192768 | tf_op jit(solution)/shard_map/pallas_call | solution.py:183
  253.6 5.0 %collective-permute-start.52 = (bf16[64,2048]{1,0:T(8,128)(2,1)S(1)}, bf16[64,2048]{1,0:T(8,128)(2,1)S(1)}, u32[]{:S(2)}, u32[]{:S(2)}) collective-permute-start(bf16[64,2048]{1,0:T(8,128)(2,1)S(1)} %get-tuple-element.332.refs_7_.refs_5_.refs_3_), channel_id=1, source_target_pairs={{0,6},{1,7},{6,4},{7,5},{4,2},{5,3},{10,8},{11,9},{8,14},{9,15},{1... | collective-permute-start | bytes 786440 | tf_op jit(solution)/shard_map/chain35/ppermute | solution.py:275
  258.6 15.3 %collective-permute-done.51.refs_0_ = f32[128,3584]{1,0:T(8,128)S(1)} collective-permute-done((f32[128,3584]{1,0:T(8,128)S(1)}, f32[128,3584]{1,0:T(8,128)S(1)}, u32[]{:S(2)}, u32[]{:S(2)}) %collective-permute-start.51) | collective-permute-done | bytes 1835040 | tf_op jit(solution)/shard_map/back5/ppermute | solution.py:287
  275.3 6.2 %shard_map.109 = (bf16[1024,3584]{1,0:T(8,128)(2,1)}, f32[8,128]{1,0:T(8,128)S(1)}) custom-call(bf16[128,2048]{1,0:T(8,128)(2,1)S(1)} %get-tuple-element.333.mine, bf16[128,2048]{1,0:T(8,128)(2,1)S(1)} %collective-permute-done.50.other, bf16[4096,3584]{1,0:T(8,128)(2,1)S(1)} %copy-done.1, ...), custom_call_target="tpu_custom_call", output_to_operand_aliasing={{0}: (4, {})} | custom-call | flops 7516192768 | tf_op jit(solution)/shard_map/pallas_call | solution.py:183
  283.6 6.2 %shard_map.113 = (bf16[1024,3584]{1,0:T(8,128)(2,1)}, f32[8,128]{1,0:T(8,128)S(1)}) custom-call(bf16[128,2048]{1,0:T(8,128)(2,1)S(1)} %get-tuple-element.346.mine, bf16[128,2048]{1,0:T(8,128)(2,1)S(1)} %collective-permute-done.54.other, bf16[4096,3584]{1,0:T(8,128)(2,1)S(1)} %copy-done.1, ...), custom_call_target="tpu_custom_call", output_to_operand_aliasing={{0}: (4, {})} | custom-call | flops 7516192768 | tf_op jit(solution)/shard_map/pallas_call | solution.py:183
  290.9 2.8 collective-permute-done.58.other
  293.7 5.8 %collective-permute-done.59.refs_0_ = f32[128,3584]{1,0:T(8,128)S(1)} collective-permute-done((f32[128,3584]{1,0:T(8,128)S(1)}, f32[128,3584]{1,0:T(8,128)S(1)}, u32[]{:S(2)}, u32[]{:S(2)}) %collective-permute-start.59) | collective-permute-done | bytes 1835040 | tf_op jit(solution)/shard_map/back6/ppermute | solution.py:287
  299.4 6.2 %shard_map.117 = (bf16[1024,3584]{1,0:T(8,128)(2,1)}, f32[8,128]{1,0:T(8,128)S(1)}) custom-call(bf16[128,2048]{1,0:T(8,128)(2,1)S(1)} %get-tuple-element.358.mine, bf16[128,2048]{1,0:T(8,128)(2,1)S(1)} %collective-permute-done.58.other, bf16[4096,3584]{1,0:T(8,128)(2,1)S(1)} %copy-done.1, ...), custom_call_target="tpu_custom_call", output_to_operand_aliasing={{0}: (4, {})} | custom-call | flops 7516192768 | tf_op jit(solution)/shard_map/pallas_call | solution.py:183
  305.7 13.1 %collective-permute-done.57.refs_0_ = f32[128,3584]{1,0:T(8,128)S(1)} collective-permute-done((f32[128,3584]{1,0:T(8,128)S(1)}, f32[128,3584]{1,0:T(8,128)S(1)}, u32[]{:S(2)}, u32[]{:S(2)}) %collective-permute-start.57) | collective-permute-done | bytes 1835040 | tf_op jit(solution)/shard_map/back7/ppermute | solution.py:287
  318.8 6.2 %shard_map.118 = (bf16[1024,3584]{1,0:T(8,128)(2,1)}, f32[8,128]{1,0:T(8,128)}) custom-call(bf16[128,2048]{1,0:T(8,128)(2,1)S(1)} %get-tuple-element.356.mine, bf16[128,2048]{1,0:T(8,128)(2,1)S(1)} %collective-permute-done.56.other, bf16[4096,3584]{1,0:T(8,128)(2,1)S(1)} %copy-done.1, ...), custom_call_target="tpu_custom_call", output_to_operand_aliasing={{0}: (4, {})} | custom-call | flops 7516192768 | tf_op jit(solution)/shard_map/pallas_call | solution.py:183
  (167 shorter events, 48.4 us)
Async XLA Ops:
  0.1 24.8 %collective-permute-start = (bf16[64,2048]{1,0:T(8,128)(2,1)S(1)}, bf16[64,2048]{1,0:T(8,128)(2,1)S(1)}, u32[]{:S(2)}, u32[]{:S(2)}) collective-permute-start(bf16[64,2048]{1,0:T(8,128)(2,1)S(1)} %get-tuple-element.187.refs_0_), channel_id=1, source_target_pairs={{0,6},{1,7},{6,4},{7,5},{4,2},{5,3},{10,8},{11,9},{8,14},{9,15},{1... | collective-permute-start | bytes 786440 | tf_op jit(solution)/shard_map/chain2/ppermute | solution.py:275
  4.4 24.2 %collective-permute-start.2 = (bf16[64,2048]{1,0:T(8,128)(2,1)S(1)}, bf16[64,2048]{1,0:T(8,128)(2,1)S(1)}, u32[]{:S(2)}, u32[]{:S(2)}) collective-permute-start(bf16[64,2048]{1,0:T(8,128)(2,1)S(1)} %get-tuple-element.194.refs_1_), channel_id=1, source_target_pairs={{0,6},{1,7},{6,4},{7,5},{4,2},{5,3},{10,8},{11,9},{8,14},{9,15},{1... | collective-permute-start | bytes 786440 | tf_op jit(solution)/shard_map/chain3/ppermute | solution.py:275
  29.4 10.5 %collective-permute-start.4 = (bf16[64,2048]{1,0:T(8,128)(2,1)S(1)}, bf16[64,2048]{1,0:T(8,128)(2,1)S(1)}, u32[]{:S(2)}, u32[]{:S(2)}) collective-permute-start(bf16[64,2048]{1,0:T(8,128)(2,1)S(1)} %get-tuple-element.198.refs_3_.refs_1_), channel_id=1, source_target_pairs={{0,6},{1,7},{6,4},{7,5},{4,2},{5,3},{10,8},{11,9},{8,14},{9,15},{1... | collective-permute-start | bytes 786440 | tf_op jit(solution)/shard_map/chain5/ppermute | solution.py:275
  40.5 10.5 %collective-permute-start.6 = (bf16[64,2048]{1,0:T(8,128)(2,1)S(1)}, bf16[64,2048]{1,0:T(8,128)(2,1)S(1)}, u32[]{:S(2)}, u32[]{:S(2)}) collective-permute-start(bf16[64,2048]{1,0:T(8,128)(2,1)S(1)} %get-tuple-element.202.refs_5_.refs_3_.refs_1_), channel_id=1, source_target_pairs={{0,6},{1,7},{6,4},{7,5},{4,2},{5,3},{10,8},{11,9},{8,14},{9,15},{1... | collective-permute-start | bytes 786440 | tf_op jit(solution)/shard_map/chain7/ppermute | solution.py:275
  45.5 11.2 %collective-permute-start.5 = (bf16[64,2048]{1,0:T(8,128)(2,1)S(1)}, bf16[64,2048]{1,0:T(8,128)(2,1)S(1)}, u32[]{:S(2)}, u32[]{:S(2)}) collective-permute-start(bf16[64,2048]{1,0:T(8,128)(2,1)S(1)} %get-tuple-element.201.refs_6_.refs_4_.refs_2_.refs_0_), channel_id=1, source_target_pairs={{0,6},{1,7},{6,4},{7,5},{4,2},{5,3},{10,8},{11,9},{8,14},{9,15},{1... | collective-permute-start | bytes 786440 | tf_op jit(solution)/shard_map/chain8/ppermute | solution.py:275
  51.1 10.7 %collective-permute-start.8 = (bf16[64,2048]{1,0:T(8,128)(2,1)S(1)}, bf16[64,2048]{1,0:T(8,128)(2,1)S(1)}, u32[]{:S(2)}, u32[]{:S(2)}) collective-permute-start(bf16[64,2048]{1,0:T(8,128)(2,1)S(1)} %get-tuple-element.204.refs_7_.refs_5_.refs_3_.refs_1_), channel_id=1, source_target_pairs={{0,6},{1,7},{6,4},{7,5},{4,2},{5,3},{10,8},{11,9},{8,14},{9,15},{1... | collective-permute-start | bytes 786440 | tf_op jit(solution)/shard_map/chain9/ppermute | solution.py:275
  62.7 17.0 %collective-permute-start.10 = (bf16[128,2048]{1,0:T(8,128)(2,1)S(1)}, bf16[128,2048]{1,0:T(8,128)(2,1)S(1)}, u32[]{:S(2)}, u32[]{:S(2)}) collective-permute-start(bf16[128,2048]{1,0:T(8,128)(2,1)S(1)} %get-tuple-element.216.mine), channel_id=1, source_target_pairs={{0,1},{1,0},{2,3},{3,2},{4,5},{5,4},{6,7},{7,6},{8,9},{9,8},{10,11... | collective-permute-start | bytes 1572872 | tf_op jit(solution)/shard_map/swap1/ppermute | solution.py:295
  67.7 10.9 %collective-permute-start.11 = (bf16[64,2048]{1,0:T(8,128)(2,1)S(1)}, bf16[64,2048]{1,0:T(8,128)(2,1)S(1)}, u32[]{:S(2)}, u32[]{:S(2)}) collective-permute-start(bf16[64,2048]{1,0:T(8,128)(2,1)S(1)} %get-tuple-element.218.refs_5_.refs_3_.refs_1_), channel_id=1, source_target_pairs={{0,6},{1,7},{6,4},{7,5},{4,2},{5,3},{10,8},{11,9},{8,14},{9,15},{1... | collective-permute-start | bytes 786440 | tf_op jit(solution)/shard_map/chain11/ppermute | solution.py:275
  73.6 11.6 %collective-permute-start.9 = (bf16[64,2048]{1,0:T(8,128)(2,1)S(1)}, bf16[64,2048]{1,0:T(8,128)(2,1)S(1)}, u32[]{:S(2)}, u32[]{:S(2)}) collective-permute-start(bf16[64,2048]{1,0:T(8,128)(2,1)S(1)} %get-tuple-element.215.refs_4_.refs_2_.refs_0_), channel_id=1, source_target_pairs={{0,6},{1,7},{6,4},{7,5},{4,2},{5,3},{10,8},{11,9},{8,14},{9,15},{1... | collective-permute-start | bytes 786440 | tf_op jit(solution)/shard_map/chain12/ppermute | solution.py:275
  79.4 23.5 %collective-permute-start.13 = (bf16[128,2048]{1,0:T(8,128)(2,1)S(1)}, bf16[128,2048]{1,0:T(8,128)(2,1)S(1)}, u32[]{:S(2)}, u32[]{:S(2)}) collective-permute-start(bf16[128,2048]{1,0:T(8,128)(2,1)S(1)} %get-tuple-element.224.mine), channel_id=1, source_target_pairs={{0,1},{1,0},{2,3},{3,2},{4,5},{5,4},{6,7},{7,6},{8,9},{9,8},{10,11... | collective-permute-start | bytes 1572872 | tf_op jit(solution)/shard_map/swap2/ppermute | solution.py:295
  85.9 42.5 %collective-permute-start.20 = (f32[128,3584]{1,0:T(8,128)S(1)}, f32[128,3584]{1,0:T(8,128)S(1)}, u32[]{:S(2)}, u32[]{:S(2)}) collective-permute-start(f32[128,3584]{1,0:T(8,128)S(1)} %get-tuple-element.246), channel_id=1, source_target_pairs={{0,24},{1,25},{2,26},{3,27},{4,28},{5,29},{6,30},{7,31},{8,0},{9,1... | collective-permute-start | bytes 5505032 | tf_op jit(solution)/shard_map/back0/ppermute | solution.py:287
  92.4 35.7 %collective-permute-start.19 = (bf16[128,2048]{1,0:T(8,128)(2,1)S(1)}, bf16[128,2048]{1,0:T(8,128)(2,1)S(1)}, u32[]{:S(2)}, u32[]{:S(2)}) collective-permute-start(bf16[128,2048]{1,0:T(8,128)(2,1)S(1)} %get-tuple-element.245.mine), channel_id=1, source_target_pairs={{0,1},{1,0},{2,3},{3,2},{4,5},{5,4},{6,7},{7,6},{8,9},{9,8},{10,11... | collective-permute-start | bytes 1572872 | tf_op jit(solution)/shard_map/swap0/ppermute | solution.py:295
  93.6 16.1 %collective-permute-start.12 = (bf16[64,2048]{1,0:T(8,128)(2,1)S(1)}, bf16[64,2048]{1,0:T(8,128)(2,1)S(1)}, u32[]{:S(2)}, u32[]{:S(2)}) collective-permute-start(bf16[64,2048]{1,0:T(8,128)(2,1)S(1)} %get-tuple-element.223.refs_4_.refs_2_.refs_0_), channel_id=1, source_target_pairs={{0,6},{1,7},{6,4},{7,5},{4,2},{5,3},{10,8},{11,9},{8,14},{9,15},{1... | collective-permute-start | bytes 786440 | tf_op jit(solution)/shard_map/chain14/ppermute | solution.py:275
  98.7 11.1 %collective-permute-start.17 = (bf16[64,2048]{1,0:T(8,128)(2,1)S(1)}, bf16[64,2048]{1,0:T(8,128)(2,1)S(1)}, u32[]{:S(2)}, u32[]{:S(2)}) collective-permute-start(bf16[64,2048]{1,0:T(8,128)(2,1)S(1)} %get-tuple-element.234.refs_5_.refs_3_.refs_1_), channel_id=1, source_target_pairs={{0,6},{1,7},{6,4},{7,5},{4,2},{5,3},{10,8},{11,9},{8,14},{9,15},{1... | collective-permute-start | bytes 786440 | tf_op jit(solution)/shard_map/chain15/ppermute | solution.py:275
  102.9 13.1 %collective-permute-start.16 = (bf16[128,2048]{1,0:T(8,128)(2,1)S(1)}, bf16[128,2048]{1,0:T(8,128)(2,1)S(1)}, u32[]{:S(2)}, u32[]{:S(2)}) collective-permute-start(bf16[128,2048]{1,0:T(8,128)(2,1)S(1)} %get-tuple-element.233.mine), channel_id=1, source_target_pairs={{0,1},{1,0},{2,3},{3,2},{4,5},{5,4},{6,7},{7,6},{8,9},{9,8},{10,11... | collective-permute-start | bytes 1572872 | tf_op jit(solution)/shard_map/swap3/ppermute | solution.py:295
  109.7 13.7 %collective-permute-start.15 = (bf16[64,2048]{1,0:T(8,128)(2,1)S(1)}, bf16[64,2048]{1,0:T(8,128)(2,1)S(1)}, u32[]{:S(2)}, u32[]{:S(2)}) collective-permute-start(bf16[64,2048]{1,0:T(8,128)(2,1)S(1)} %get-tuple-element.232.refs_6_.refs_4_.refs_2_.refs_0_), channel_id=1, source_target_pairs={{0,6},{1,7},{6,4},{7,5},{4,2},{5,3},{10,8},{11,9},{8,14},{9,15},{1... | collective-permute-start | bytes 786440 | tf_op jit(solution)/shard_map/chain16/ppermute | solution.py:275
  109.9 16.8 %collective-permute-start.21 = (bf16[64,2048]{1,0:T(8,128)(2,1)S(1)}, bf16[64,2048]{1,0:T(8,128)(2,1)S(1)}, u32[]{:S(2)}, u32[]{:S(2)}) collective-permute-start(bf16[64,2048]{1,0:T(8,128)(2,1)S(1)} %get-tuple-element.236.refs_7_.refs_5_.refs_3_.refs_1_), channel_id=1, source_target_pairs={{0,6},{1,7},{6,4},{7,5},{4,2},{5,3},{10,8},{11,9},{8,14},{9,15},{1... | collective-permute-start | bytes 786440 | tf_op jit(solution)/shard_map/chain17/ppermute | solution.py:275
  116.1 43.6 %collective-permute-start.27 = (f32[128,3584]{1,0:T(8,128)S(1)}, f32[128,3584]{1,0:T(8,128)S(1)}, u32[]{:S(2)}, u32[]{:S(2)}) collective-permute-start(f32[128,3584]{1,0:T(8,128)S(1)} %get-tuple-element.269), channel_id=1, source_target_pairs={{0,24},{1,25},{2,26},{3,27},{4,28},{5,29},{6,30},{7,31},{8,0},{9,1... | collective-permute-start | bytes 5505032 | tf_op jit(solution)/shard_map/back1/ppermute | solution.py:287
  127.4 10.6 %collective-permute-start.24 = (bf16[64,2048]{1,0:T(8,128)(2,1)S(1)}, bf16[64,2048]{1,0:T(8,128)(2,1)S(1)}, u32[]{:S(2)}, u32[]{:S(2)}) collective-permute-start(bf16[64,2048]{1,0:T(8,128)(2,1)S(1)} %get-tuple-element.255.refs_5_.refs_3_.refs_1_), channel_id=1, source_target_pairs={{0,6},{1,7},{6,4},{7,5},{4,2},{5,3},{10,8},{11,9},{8,14},{9,15},{1... | collective-permute-start | bytes 786440 | tf_op jit(solution)/shard_map/chain19/ppermute | solution.py:275
  128.1 15.1 %collective-permute-start.23 = (bf16[128,2048]{1,0:T(8,128)(2,1)S(1)}, bf16[128,2048]{1,0:T(8,128)(2,1)S(1)}, u32[]{:S(2)}, u32[]{:S(2)}) collective-permute-start(bf16[128,2048]{1,0:T(8,128)(2,1)S(1)} %get-tuple-element.254.mine), channel_id=1, source_target_pairs={{0,1},{1,0},{2,3},{3,2},{4,5},{5,4},{6,7},{7,6},{8,9},{9,8},{10,11... | collective-permute-start | bytes 1572872 | tf_op jit(solution)/shard_map/swap5/ppermute | solution.py:295
  135.4 14.6 %collective-permute-start.22 = (bf16[64,2048]{1,0:T(8,128)(2,1)S(1)}, bf16[64,2048]{1,0:T(8,128)(2,1)S(1)}, u32[]{:S(2)}, u32[]{:S(2)}) collective-permute-start(bf16[64,2048]{1,0:T(8,128)(2,1)S(1)} %get-tuple-element.253.refs_4_.refs_2_.refs_0_), channel_id=1, source_target_pairs={{0,6},{1,7},{6,4},{7,5},{4,2},{5,3},{10,8},{11,9},{8,14},{9,15},{1... | collective-permute-start | bytes 786440 | tf_op jit(solution)/shard_map/chain20/ppermute | solution.py:275
  138.7 11.4 %collective-permute-start.25 = (bf16[64,2048]{1,0:T(8,128)(2,1)S(1)}, bf16[64,2048]{1,0:T(8,128)(2,1)S(1)}, u32[]{:S(2)}, u32[]{:S(2)}) collective-permute-start(bf16[64,2048]{1,0:T(8,128)(2,1)S(1)} %get-tuple-element.264.refs_5_.refs_3_.refs_1_), channel_id=1, source_target_pairs={{0,6},{1,7},{6,4},{7,5},{4,2},{5,3},{10,8},{11,9},{8,14},{9,15},{1... | collective-permute-start | bytes 786440 | tf_op jit(solution)/shard_map/chain21/ppermute | solution.py:275
  142.9 18.0 %collective-permute-start.26 = (bf16[128,2048]{1,0:T(8,128)(2,1)S(1)}, bf16[128,2048]{1,0:T(8,128)(2,1)S(1)}, u32[]{:S(2)}, u32[]{:S(2)}) collective-permute-start(bf16[128,2048]{1,0:T(8,128)(2,1)S(1)} %get-tuple-element.267.mine), channel_id=1, source_target_pairs={{0,1},{1,0},{2,3},{3,2},{4,5},{5,4},{6,7},{7,6},{8,9},{9,8},{10,11... | collective-permute-start | bytes 1572872 | tf_op jit(solution)/shard_map/swap6/ppermute | solution.py:295
  143.2 49.4 %collective-permute-start.32 = (f32[128,3584]{1,0:T(8,128)S(1)}, f32[128,3584]{1,0:T(8,128)S(1)}, u32[]{:S(2)}, u32[]{:S(2)}) collective-permute-start(f32[128,3584]{1,0:T(8,128)S(1)} %get-tuple-element.284), channel_id=1, source_target_pairs={{0,24},{1,25},{2,26},{3,27},{4,28},{5,29},{6,30},{7,31},{8,0},{9,1... | collective-permute-start | bytes 5505032 | tf_op jit(solution)/shard_map/back2/ppermute | solution.py:287
  150.0 16.3 %collective-permute-start.28 = (bf16[64,2048]{1,0:T(8,128)(2,1)S(1)}, bf16[64,2048]{1,0:T(8,128)(2,1)S(1)}, u32[]{:S(2)}, u32[]{:S(2)}) collective-permute-start(bf16[64,2048]{1,0:T(8,128)(2,1)S(1)} %get-tuple-element.263.refs_6_.refs_4_.refs_2_.refs_0_), channel_id=1, source_target_pairs={{0,6},{1,7},{6,4},{7,5},{4,2},{5,3},{10,8},{11,9},{8,14},{9,15},{1... | collective-permute-start | bytes 786440 | tf_op jit(solution)/shard_map/chain22/ppermute | solution.py:275
  150.1 16.8 %collective-permute-start.29 = (bf16[64,2048]{1,0:T(8,128)(2,1)S(1)}, bf16[64,2048]{1,0:T(8,128)(2,1)S(1)}, u32[]{:S(2)}, u32[]{:S(2)}) collective-permute-start(bf16[64,2048]{1,0:T(8,128)(2,1)S(1)} %get-tuple-element.266.refs_7_.refs_5_.refs_3_.refs_1_), channel_id=1, source_target_pairs={{0,6},{1,7},{6,4},{7,5},{4,2},{5,3},{10,8},{11,9},{8,14},{9,15},{1... | collective-permute-start | bytes 786440 | tf_op jit(solution)/shard_map/chain23/ppermute | solution.py:275
  159.8 11.9 %collective-permute-start.30 = (bf16[128,2048]{1,0:T(8,128)(2,1)S(1)}, bf16[128,2048]{1,0:T(8,128)(2,1)S(1)}, u32[]{:S(2)}, u32[]{:S(2)}) collective-permute-start(bf16[128,2048]{1,0:T(8,128)(2,1)S(1)} %get-tuple-element.278.mine), channel_id=1, source_target_pairs={{0,1},{1,0},{2,3},{3,2},{4,5},{5,4},{6,7},{7,6},{8,9},{9,8},{10,11... | collective-permute-start | bytes 1572872 | tf_op jit(solution)/shard_map/swap7/ppermute | solution.py:295
  160.8 56.9 %collective-permute-start.37 = (f32[128,3584]{1,0:T(8,128)S(1)}, f32[128,3584]{1,0:T(8,128)S(1)}, u32[]{:S(2)}, u32[]{:S(2)}) collective-permute-start(f32[128,3584]{1,0:T(8,128)S(1)} %get-tuple-element.299), channel_id=1, source_target_pairs={{0,24},{1,25},{2,26},{3,27},{4,28},{5,29},{6,30},{7,31},{8,0},{9,1... | collective-permute-start | bytes 5505032 | tf_op jit(solution)/shard_map/back3/ppermute | solution.py:287
  166.3 26.6 %collective-permute-start.34 = (bf16[128,2048]{1,0:T(8,128)(2,1)S(1)}, bf16[128,2048]{1,0:T(8,128)(2,1)S(1)}, u32[]{:S(2)}, u32[]{:S(2)}) collective-permute-start(bf16[128,2048]{1,0:T(8,128)(2,1)S(1)} %get-tuple-element.289.mine), channel_id=1, source_target_pairs={{0,1},{1,0},{2,3},{3,2},{4,5},{5,4},{6,7},{7,6},{8,9},{9,8},{10,11... | collective-permute-start | bytes 1572872 | tf_op jit(solution)/shard_map/swap4/ppermute | solution.py:295
  171.7 20.9 %collective-permute-start.33 = (bf16[64,2048]{1,0:T(8,128)(2,1)S(1)}, bf16[64,2048]{1,0:T(8,128)(2,1)S(1)}, u32[]{:S(2)}, u32[]{:S(2)}) collective-permute-start(bf16[64,2048]{1,0:T(8,128)(2,1)S(1)} %get-tuple-element.277.refs_7_.refs_5_.refs_3_.refs_1_), channel_id=1, source_target_pairs={{0,6},{1,7},{6,4},{7,5},{4,2},{5,3},{10,8},{11,9},{8,14},{9,15},{1... | collective-permute-start | bytes 786440 | tf_op jit(solution)/shard_map/chain25/ppermute | solution.py:275
  177.2 47.6 %collective-permute-start.41 = (bf16[128,2048]{1,0:T(8,128)(2,1)S(1)}, bf16[128,2048]{1,0:T(8,128)(2,1)S(1)}, u32[]{:S(2)}, u32[]{:S(2)}) collective-permute-start(bf16[128,2048]{1,0:T(8,128)(2,1)S(1)} %get-tuple-element.308.mine), channel_id=1, source_target_pairs={{0,1},{1,0},{2,3},{3,2},{4,5},{5,4},{6,7},{7,6},{8,9},{9,8},{10,11... | collective-permute-start | bytes 1572872 | tf_op jit(solution)/shard_map/swap8/ppermute | solution.py:295
  192.9 24.9 %collective-permute-start.39 = (bf16[128,2048]{1,0:T(8,128)(2,1)S(1)}, bf16[128,2048]{1,0:T(8,128)(2,1)S(1)}, u32[]{:S(2)}, u32[]{:S(2)}) collective-permute-start(bf16[128,2048]{1,0:T(8,128)(2,1)S(1)} %get-tuple-element.304.mine), channel_id=1, source_target_pairs={{0,1},{1,0},{2,3},{3,2},{4,5},{5,4},{6,7},{7,6},{8,9},{9,8},{10,11... | collective-permute-start | bytes 1572872 | tf_op jit(solution)/shard_map/swap9/ppermute | solution.py:295
  200.3 24.3 %collective-permute-start.40 = (bf16[64,2048]{1,0:T(8,128)(2,1)S(1)}, bf16[64,2048]{1,0:T(8,128)(2,1)S(1)}, u32[]{:S(2)}, u32[]{:S(2)}) collective-permute-start(bf16[64,2048]{1,0:T(8,128)(2,1)S(1)} %get-tuple-element.295.refs_6_.refs_4_.refs_2_.refs_0_), channel_id=1, source_target_pairs={{0,6},{1,7},{6,4},{7,5},{4,2},{5,3},{10,8},{11,9},{8,14},{9,15},{1... | collective-permute-start | bytes 786440 | tf_op jit(solution)/shard_map/chain28/ppermute | solution.py:275
  201.9 41.4 %collective-permute-start.44 = (f32[128,3584]{1,0:T(8,128)S(1)}, f32[128,3584]{1,0:T(8,128)S(1)}, u32[]{:S(2)}, u32[]{:S(2)}) collective-permute-start(f32[128,3584]{1,0:T(8,128)S(1)} %get-tuple-element.319), channel_id=1, source_target_pairs={{0,24},{1,25},{2,26},{3,27},{4,28},{5,29},{6,30},{7,31},{8,0},{9,1... | collective-permute-start | bytes 5505032 | tf_op jit(solution)/shard_map/back4/ppermute | solution.py:287
  217.7 14.0 %collective-permute-start.42 = (bf16[64,2048]{1,0:T(8,128)(2,1)S(1)}, bf16[64,2048]{1,0:T(8,128)(2,1)S(1)}, u32[]{:S(2)}, u32[]{:S(2)}) collective-permute-start(bf16[64,2048]{1,0:T(8,128)(2,1)S(1)} %get-tuple-element.297.refs_7_.refs_5_.refs_3_.refs_1_), channel_id=1, source_target_pairs={{0,6},{1,7},{6,4},{7,5},{4,2},{5,3},{10,8},{11,9},{8,14},{9,15},{1... | collective-permute-start | bytes 786440 | tf_op jit(solution)/shard_map/chain29/ppermute | solution.py:275
  217.8 14.2 %collective-permute-start.38 = (bf16[128,2048]{1,0:T(8,128)(2,1)S(1)}, bf16[128,2048]{1,0:T(8,128)(2,1)S(1)}, u32[]{:S(2)}, u32[]{:S(2)}) collective-permute-start(bf16[128,2048]{1,0:T(8,128)(2,1)S(1)} %get-tuple-element.303.mine), channel_id=1, source_target_pairs={{0,1},{1,0},{2,3},{3,2},{4,5},{5,4},{6,7},{7,6},{8,9},{9,8},{10,11... | collective-permute-start | bytes 1572872 | tf_op jit(solution)/shard_map/swap10/ppermute | solution.py:295
  224.6 49.2 %collective-permute-start.51 = (f32[128,3584]{1,0:T(8,128)S(1)}, f32[128,3584]{1,0:T(8,128)S(1)}, u32[]{:S(2)}, u32[]{:S(2)}) collective-permute-start(f32[128,3584]{1,0:T(8,128)S(1)} %get-tuple-element.337), channel_id=1, source_target_pairs={{0,24},{1,25},{2,26},{3,27},{4,28},{5,29},{6,30},{7,31},{8,0},{9,1... | collective-permute-start | bytes 5505032 | tf_op jit(solution)/shard_map/back5/ppermute | solution.py:287
  224.8 12.8 %collective-permute-start.43 = (bf16[64,2048]{1,0:T(8,128)(2,1)S(1)}, bf16[64,2048]{1,0:T(8,128)(2,1)S(1)}, u32[]{:S(2)}, u32[]{:S(2)}) collective-permute-start(bf16[64,2048]{1,0:T(8,128)(2,1)S(1)} %get-tuple-element.307.refs_6_.refs_4_.refs_2_.refs_0_), channel_id=1, source_target_pairs={{0,6},{1,7},{6,4},{7,5},{4,2},{5,3},{10,8},{11,9},{8,14},{9,15},{1... | collective-permute-start | bytes 786440 | tf_op jit(solution)/shard_map/chain30/ppermute | solution.py:275
  231.8 11.5 %collective-permute-start.45 = (bf16[64,2048]{1,0:T(8,128)(2,1)S(1)}, bf16[64,2048]{1,0:T(8,128)(2,1)S(1)}, u32[]{:S(2)}, u32[]{:S(2)}) collective-permute-start(bf16[64,2048]{1,0:T(8,128)(2,1)S(1)} %get-tuple-element.313.refs_7_.refs_5_.refs_3_.refs_1_), channel_id=1, source_target_pairs={{0,6},{1,7},{6,4},{7,5},{4,2},{5,3},{10,8},{11,9},{8,14},{9,15},{1... | collective-permute-start | bytes 786440 | tf_op jit(solution)/shard_map/chain31/ppermute | solution.py:275
  232.0 13.8 %collective-permute-start.47 = (bf16[128,2048]{1,0:T(8,128)(2,1)S(1)}, bf16[128,2048]{1,0:T(8,128)(2,1)S(1)}, u32[]{:S(2)}, u32[]{:S(2)}) collective-permute-start(bf16[128,2048]{1,0:T(8,128)(2,1)S(1)} %get-tuple-element.324.mine), channel_id=1, source_target_pairs={{0,1},{1,0},{2,3},{3,2},{4,5},{5,4},{6,7},{7,6},{8,9},{9,8},{10,11... | collective-permute-start | bytes 1572872 | tf_op jit(solution)/shard_map/swap11/ppermute | solution.py:295
  237.7 15.0 %collective-permute-start.46 = (bf16[64,2048]{1,0:T(8,128)(2,1)S(1)}, bf16[64,2048]{1,0:T(8,128)(2,1)S(1)}, u32[]{:S(2)}, u32[]{:S(2)}) collective-permute-start(bf16[64,2048]{1,0:T(8,128)(2,1)S(1)} %get-tuple-element.317.refs_6_.refs_4_.refs_2_.refs_0_), channel_id=1, source_target_pairs={{0,6},{1,7},{6,4},{7,5},{4,2},{5,3},{10,8},{11,9},{8,14},{9,15},{1... | collective-permute-start | bytes 786440 | tf_op jit(solution)/shard_map/chain32/ppermute | solution.py:275
  244.5 30.8 %collective-permute-start.50 = (bf16[128,2048]{1,0:T(8,128)(2,1)S(1)}, bf16[128,2048]{1,0:T(8,128)(2,1)S(1)}, u32[]{:S(2)}, u32[]{:S(2)}) collective-permute-start(bf16[128,2048]{1,0:T(8,128)(2,1)S(1)} %get-tuple-element.333.mine), channel_id=1, source_target_pairs={{0,1},{1,0},{2,3},{3,2},{4,5},{5,4},{6,7},{7,6},{8,9},{9,8},{10,11... | collective-permute-start | bytes 1572872 | tf_op jit(solution)/shard_map/swap12/ppermute | solution.py:295
  245.8 53.6 %collective-permute-start.59 = (f32[128,3584]{1,0:T(8,128)S(1)}, f32[128,3584]{1,0:T(8,128)S(1)}, u32[]{:S(2)}, u32[]{:S(2)}) collective-permute-start(f32[128,3584]{1,0:T(8,128)S(1)} %get-tuple-element.359), channel_id=1, source_target_pairs={{0,24},{1,25},{2,26},{3,27},{4,28},{5,29},{6,30},{7,31},{8,0},{9,1... | collective-permute-start | bytes 5505032 | tf_op jit(solution)/shard_map/back6/ppermute | solution.py:287
  252.7 28.9 %collective-permute-start.49 = (bf16[64,2048]{1,0:T(8,128)(2,1)S(1)}, bf16[64,2048]{1,0:T(8,128)(2,1)S(1)}, u32[]{:S(2)}, u32[]{:S(2)}) collective-permute-start(bf16[64,2048]{1,0:T(8,128)(2,1)S(1)} %get-tuple-element.330.refs_6_.refs_4_.refs_2_), channel_id=1, source_target_pairs={{0,6},{1,7},{6,4},{7,5},{4,2},{5,3},{10,8},{11,9},{8,14},{9,15},{1... | collective-permute-start | bytes 786440 | tf_op jit(solution)/shard_map/chain34/ppermute | solution.py:275
  253.6 28.0 %collective-permute-start.52 = (bf16[64,2048]{1,0:T(8,128)(2,1)S(1)}, bf16[64,2048]{1,0:T(8,128)(2,1)S(1)}, u32[]{:S(2)}, u32[]{:S(2)}) collective-permute-start(bf16[64,2048]{1,0:T(8,128)(2,1)S(1)} %get-tuple-element.332.refs_7_.refs_5_.refs_3_), channel_id=1, source_target_pairs={{0,6},{1,7},{6,4},{7,5},{4,2},{5,3},{10,8},{11,9},{8,14},{9,15},{1... | collective-permute-start | bytes 786440 | tf_op jit(solution)/shard_map/chain35/ppermute | solution.py:275
  275.3 43.5 %collective-permute-start.57 = (f32[128,3584]{1,0:T(8,128)S(1)}, f32[128,3584]{1,0:T(8,128)S(1)}, u32[]{:S(2)}, u32[]{:S(2)}) collective-permute-start(f32[128,3584]{1,0:T(8,128)S(1)} %get-tuple-element.357), channel_id=1, source_target_pairs={{0,24},{1,25},{2,26},{3,27},{4,28},{5,29},{6,30},{7,31},{8,0},{9,1... | collective-permute-start | bytes 5505032 | tf_op jit(solution)/shard_map/back7/ppermute | solution.py:287
  282.4 11.3 %collective-permute-start.58 = (bf16[128,2048]{1,0:T(8,128)(2,1)S(1)}, bf16[128,2048]{1,0:T(8,128)(2,1)S(1)}, u32[]{:S(2)}, u32[]{:S(2)}) collective-permute-start(bf16[128,2048]{1,0:T(8,128)(2,1)S(1)} %get-tuple-element.358.mine), channel_id=1, source_target_pairs={{0,1},{1,0},{2,3},{3,2},{4,5},{5,4},{6,7},{7,6},{8,9},{9,8},{10,11... | collective-permute-start | bytes 1572872 | tf_op jit(solution)/shard_map/swap14/ppermute | solution.py:295
  290.7 15.0 %collective-permute-start.56 = (bf16[128,2048]{1,0:T(8,128)(2,1)S(1)}, bf16[128,2048]{1,0:T(8,128)(2,1)S(1)}, u32[]{:S(2)}, u32[]{:S(2)}) collective-permute-start(bf16[128,2048]{1,0:T(8,128)(2,1)S(1)} %get-tuple-element.356.mine), channel_id=1, source_target_pairs={{0,1},{1,0},{2,3},{3,2},{4,5},{5,4},{6,7},{7,6},{8,9},{9,8},{10,11... | collective-permute-start | bytes 1572872 | tf_op jit(solution)/shard_map/swap15/ppermute | solution.py:295
  (14 other events, 143.8 us)

commit v2 on v1

--- a/solution.py
+++ b/solution.py
@@ -9,7 +9,7 @@
 
 AXES = ("row", "col")
 PIECES = 8
-STREAM = (0, 1, 1, 1, 0, 1, 1, 1, 0, 1, 1, 0, 0, 0, 0, 0)
+STREAM = (0, 1, 1, 1, 1, 1, 1, 1, 1, 0, 0, 0, 0, 0, 0, 0)
 SUB = 2
 BACK_STEPS = 3
 MIB = 1024 * 1024
@@ -203,7 +203,7 @@
 
     sides = range(inner)
     chain = [(device(r, r - d, s), device(r, r - d - 1, s)) for r in range(n_row) for d in range(n_row - 1) for s in sides]
-    chain += [(device(r - 1, r, s), device(r, r, s)) for r in range(n_row) for s in sides]
+    cross = [(device(r - 1, r, s), device(r, r, s)) for r in range(n_row) for s in sides]
     everyone = [(r, b, s) for r in range(n_row) for b in range(n_row) for s in sides]
     swap_pairs = [(device(r, b, s), device(r, b, 1 - s)) for r, b, s in everyone]
     back_pairs = [(device(r, b, s), device(r - 1, b, s)) for r, b, s in everyone]
@@ -256,7 +256,8 @@
         if step <= last_chain + SUB:
             value, token = arriving.pop(step - SUB, None), None
             came = value
-            if step < chunks and pieces[step // SUB][0] == 1:
+            crossing = step < chunks and pieces[step // SUB][0] == 1
+            if crossing:
                 options = [[tokens]] if value is None else [[tokens], [value]]
                 value, token = choose(crosses, options, rows_of(step), chunk, seen)
                 seen = [token]
@@ -272,7 +273,7 @@
             held_last[step] = value if came is None else came
             if step <= last_chain:
                 with jax.named_scope(f"chain{step}"):
-                    arriving[step] = lax.ppermute(value, AXES, chain)
+                    arriving[step] = lax.ppermute(value, AXES, chain + cross if crossing else chain)
         if step == first + SUB - 1:
             weight, token = load(weight, seen)
             seen = [token]

time: 326 us -> 283 us (0.87)
  waiting for transfers between devices: 111 us -> 30.7 us
  starting transfers between devices: 87.7 us -> 123 us
    ppermute x8, waiting for transfers between devices: 76 us -> 0.02 us  [body(): back[piece] = lax.ppermute(partial, AXES, back_pairs)]
    ppermute x36, starting transfers between devices: 66.7 us -> 91.1 us  [body(): lax.ppermute(value, AXES, chain + cross if crossing else chain)]
    ppermute x8, starting transfers between devices: 6.41 us -> 21 us  [body(): back[piece] = lax.ppermute(partial, AXES, back_pairs)]
    ppermute x36, waiting for transfers between devices: 24.6 us -> 19.6 us  [body(): lax.ppermute(value, AXES, chain + cross if crossing else chain)]
    ppermute x16, starting transfers between devices: 14.6 us -> 11.3 us  [body(): other[at] = lax.ppermute(mine[at], AXES, swap_pairs)]
  transfers between devices with their start and end apart: 60 -> 60, of which waited for: 21 -> 13; matrix products, arithmetic and copies ran while one was open for 0% -> 0% of each run, Pallas kernels for 33% -> 39%
where the time goes in v2:
time: 283 us; the launch traced here: 281 us
  starting transfers between devices  123 us (43%)
  Pallas kernels  116 us (41%)
  waiting for transfers between devices  30.7 us (11%)
  local copies, waits for them, and re-layouts  9.68 us (3%)
    pallas_call x16, Pallas kernels, product(): pl.pallas_call(functools.partial(product_kernel, start, back is not None,...  93.4 us
    ppermute x36, starting transfers between devices, body(): lax.ppermute(value, AXES, chain + cross if crossing else chain)  91.1 us
    ppermute x8, starting transfers between devices, body(): back[piece] = lax.ppermute(partial, AXES, back_pairs)  21 us
    ppermute x36, waiting for transfers between devices, body(): lax.ppermute(value, AXES, chain + cross if crossing else chain)  19.6 us
    pallas_call x48, Pallas kernels, choose(): pl.pallas_call(functools.partial(choose_kernel, len(options), parts, whic...  12.9 us
    ppermute x16, starting transfers between devices, body(): other[at] = lax.ppermute(mine[at], AXES, swap_pairs)  11.3 us
    ppermute x16, waiting for transfers between devices, body(): other[at] = lax.ppermute(mine[at], AXES, swap_pairs)  11.1 us
    unnamed x4, local copies, waits for them, and re-layouts  9.68 us
  transfers between devices with their start and end apart: 60, of which 13 were waited for; matrix products, arithmetic and copies ran while one was open for 0% of the time, Pallas kernels for 39%

profile of v2, /device:TPU:1, one launch (start us, length us, event | category | flops | bytes accessed | tf_op | source)
XLA Modules:
  0.0 280.8 jit_solution(15221916984020525964)
XLA Ops:
  0.1 4.2 %collective-permute-start = (bf16[64,2048]{1,0:T(8,128)(2,1)S(1)}, bf16[64,2048]{1,0:T(8,128)(2,1)S(1)}, u32[]{:S(2)}, u32[]{:S(2)}) collective-permute-start(bf16[64,2048]{1,0:T(8,128)(2,1)S(1)} %get-tuple-element.180.refs_0_), channel_id=1, source_target_pairs={{0,6},{1,7},{6,4},{7,5},{4,2},{5,3},{10,8},{11,9},{8,14},{9,15},{1... | collective-permute-start | bytes 786440 | tf_op jit(solution)/shard_map/chain2/ppermute | solution.py:276
  5.9 9.4 %shard_map.32 = (bf16[4096,3584]{1,0:T(8,128)(2,1)S(1)}, f32[8,128]{1,0:T(8,128)S(1)}) custom-call(bf16[4096,3584]{1,0:T(8,128)(2,1)} %x.1, f32[8,128]{1,0:T(8,128)S(1)} %get-tuple-element.184.refs_0_), custom_call_target="tpu_custom_call" | custom-call | tf_op jit(solution)/shard_map/pallas_call | solution.py:83
  15.2 9.7 %copy-done = bf16[4096,3584]{1,0:T(8,128)(2,1)} copy-done((bf16[4096,3584]{1,0:T(8,128)(2,1)}, bf16[4096,3584]{1,0:T(8,128)(2,1)S(1)}, u32[]{:S(2)}) %copy-start) | copy-done | bytes 29360152
  25.6 3.0 %collective-permute-start.1 = (bf16[64,2048]{1,0:T(8,128)(2,1)S(1)}, bf16[64,2048]{1,0:T(8,128)(2,1)S(1)}, u32[]{:S(2)}, u32[]{:S(2)}) collective-permute-start(bf16[64,2048]{1,0:T(8,128)(2,1)S(1)} %get-tuple-element.186.refs_2_.refs_0_), channel_id=1, source_target_pairs={{0,6},{1,7},{6,4},{7,5},{4,2},{5,3},{10,8},{11,9},{8,14},{9,15},{1... | collective-permute-start | bytes 786440 | tf_op jit(solution)/shard_map/chain4/ppermute | solution.py:276
  30.0 4.8 %collective-permute-done.1.refs_1_ = bf16[64,2048]{1,0:T(8,128)(2,1)S(1)} collective-permute-done((bf16[64,2048]{1,0:T(8,128)(2,1)S(1)}, bf16[64,2048]{1,0:T(8,128)(2,1)S(1)}, u32[]{:S(2)}, u32[]{:S(2)}) %collective-permute-start.1) | collective-permute-done | bytes 262176 | tf_op jit(solution)/shard_map/chain4/ppermute | solution.py:276
  35.5 4.1 %collective-permute-start.3 = (bf16[64,2048]{1,0:T(8,128)(2,1)S(1)}, bf16[64,2048]{1,0:T(8,128)(2,1)S(1)}, u32[]{:S(2)}, u32[]{:S(2)}) collective-permute-start(bf16[64,2048]{1,0:T(8,128)(2,1)S(1)} %get-tuple-element.190.refs_4_.refs_2_.refs_0_), channel_id=1, source_target_pairs={{0,6},{1,7},{6,4},{7,5},{4,2},{5,3},{10,8},{11,9},{8,14},{9,15},{1... | collective-permute-start | bytes 786440 | tf_op jit(solution)/shard_map/chain6/ppermute | solution.py:276
  40.5 4.1 %collective-permute-start.6 = (bf16[64,2048]{1,0:T(8,128)(2,1)S(1)}, bf16[64,2048]{1,0:T(8,128)(2,1)S(1)}, u32[]{:S(2)}, u32[]{:S(2)}) collective-permute-start(bf16[64,2048]{1,0:T(8,128)(2,1)S(1)} %get-tuple-element.195.refs_5_.refs_3_.refs_1_), channel_id=1, source_target_pairs={{0,6},{1,7},{6,4},{7,5},{4,2},{5,3},{10,8},{11,9},{8,14},{9,15},{1... | collective-permute-start | bytes 786440 | tf_op jit(solution)/shard_map/chain7/ppermute | solution.py:276
  46.2 4.1 %collective-permute-start.5 = (bf16[64,2048]{1,0:T(8,128)(2,1)S(1)}, bf16[64,2048]{1,0:T(8,128)(2,1)S(1)}, u32[]{:S(2)}, u32[]{:S(2)}) collective-permute-start(bf16[64,2048]{1,0:T(8,128)(2,1)S(1)} %get-tuple-element.194.refs_4_.refs_2_.refs_0_), channel_id=1, source_target_pairs={{0,6},{1,7},{6,4},{7,5},{4,2},{5,3},{10,8},{11,9},{8,14},{9,15},{1... | collective-permute-start | bytes 786440 | tf_op jit(solution)/shard_map/chain8/ppermute | solution.py:276
  51.4 4.1 %collective-permute-start.8 = (bf16[64,2048]{1,0:T(8,128)(2,1)S(1)}, bf16[64,2048]{1,0:T(8,128)(2,1)S(1)}, u32[]{:S(2)}, u32[]{:S(2)}) collective-permute-start(bf16[64,2048]{1,0:T(8,128)(2,1)S(1)} %get-tuple-element.200.refs_5_.refs_3_.refs_1_), channel_id=1, source_target_pairs={{0,6},{1,7},{6,4},{7,5},{4,2},{5,3},{10,8},{11,9},{8,14},{9,15},{1... | collective-permute-start | bytes 786440 | tf_op jit(solution)/shard_map/chain9/ppermute | solution.py:276
  56.8 4.9 %collective-permute-done.8.refs_1_.refs_7_ = bf16[64,2048]{1,0:T(8,128)(2,1)S(1)} collective-permute-done((bf16[64,2048]{1,0:T(8,128)(2,1)S(1)}, bf16[64,2048]{1,0:T(8,128)(2,1)S(1)}, u32[]{:S(2)}, u32[]{:S(2)}) %collective-permute-start.8) | collective-permute-done | bytes 262176 | tf_op jit(solution)/shard_map/chain9/ppermute | solution.py:276
  63.9 4.0 %collective-permute-start.7 = (bf16[64,2048]{1,0:T(8,128)(2,1)S(1)}, bf16[64,2048]{1,0:T(8,128)(2,1)S(1)}, u32[]{:S(2)}, u32[]{:S(2)}) collective-permute-start(bf16[64,2048]{1,0:T(8,128)(2,1)S(1)} %get-tuple-element.199.refs_4_.refs_2_.refs_0_), channel_id=1, source_target_pairs={{0,6},{1,7},{6,4},{7,5},{4,2},{5,3},{10,8},{11,9},{8,14},{9,15},{1... | collective-permute-start | bytes 786440 | tf_op jit(solution)/shard_map/chain10/ppermute | solution.py:276
  67.9 4.9 %collective-permute-done.7.refs_1_.refs_6_ = bf16[64,2048]{1,0:T(8,128)(2,1)S(1)} collective-permute-done((bf16[64,2048]{1,0:T(8,128)(2,1)S(1)}, bf16[64,2048]{1,0:T(8,128)(2,1)S(1)}, u32[]{:S(2)}, u32[]{:S(2)}) %collective-permute-start.7) | collective-permute-done | bytes 262176 | tf_op jit(solution)/shard_map/chain10/ppermute | solution.py:276
  73.6 4.1 %collective-permute-start.10 = (bf16[64,2048]{1,0:T(8,128)(2,1)S(1)}, bf16[64,2048]{1,0:T(8,128)(2,1)S(1)}, u32[]{:S(2)}, u32[]{:S(2)}) collective-permute-start(bf16[64,2048]{1,0:T(8,128)(2,1)S(1)} %get-tuple-element.204.refs_4_.refs_2_.refs_0_), channel_id=1, source_target_pairs={{0,6},{1,7},{6,4},{7,5},{4,2},{5,3},{10,8},{11,9},{8,14},{9,15},{1... | collective-permute-start | bytes 786440 | tf_op jit(solution)/shard_map/chain12/ppermute | solution.py:276
  79.2 4.1 %collective-permute-start.12 = (bf16[64,2048]{1,0:T(8,128)(2,1)S(1)}, bf16[64,2048]{1,0:T(8,128)(2,1)S(1)}, u32[]{:S(2)}, u32[]{:S(2)}) collective-permute-start(bf16[64,2048]{1,0:T(8,128)(2,1)S(1)} %get-tuple-element.207.refs_5_.refs_3_.refs_1_), channel_id=1, source_target_pairs={{0,6},{1,7},{6,4},{7,5},{4,2},{5,3},{10,8},{11,9},{8,14},{9,15},{1... | collective-permute-start | bytes 786440 | tf_op jit(solution)/shard_map/chain13/ppermute | solution.py:276
  83.7 5.5 %shard_map.46 = (f32[128,3584]{1,0:T(8,128)S(1)}, f32[8,128]{1,0:T(8,128)S(1)}) custom-call(bf16[128,2048]{1,0:T(8,128)(2,1)S(1)} %get-tuple-element.208.mine, bf16[128,2048]{1,0:T(8,128)(2,1)S(1)} %collective-permute-done.11.other, bf16[4096,3584]{1,0:T(8,128)(2,1)S(1)} %copy-done.1, f32[8,128]{1,0:T(8,128)S(1)} %get-tuple-element.211.refs_0_), custom_call_target="tpu_custom_call" | custom-call | flops 7516192768 | tf_op jit(solution)/shard_map/pallas_call | solution.py:183
  90.7 3.2 %collective-permute-start.15 = (bf16[64,2048]{1,0:T(8,128)(2,1)S(1)}, bf16[64,2048]{1,0:T(8,128)(2,1)S(1)}, u32[]{:S(2)}, u32[]{:S(2)}) collective-permute-start(bf16[64,2048]{1,0:T(8,128)(2,1)S(1)} %get-tuple-element.217.refs_5_.refs_3_.refs_1_), channel_id=1, source_target_pairs={{0,6},{1,7},{6,4},{7,5},{4,2},{5,3},{10,8},{11,9},{8,14},{9,15},{1... | collective-permute-start | bytes 786440 | tf_op jit(solution)/shard_map/chain15/ppermute | solution.py:276
  94.4 2.7 collective-permute-start.22
  97.0 5.5 %shard_map.51 = (f32[128,3584]{1,0:T(8,128)S(1)}, f32[8,128]{1,0:T(8,128)S(1)}) custom-call(bf16[128,2048]{1,0:T(8,128)(2,1)S(1)} %get-tuple-element.218.mine, bf16[128,2048]{1,0:T(8,128)(2,1)S(1)} %collective-permute-done.14.other, bf16[4096,3584]{1,0:T(8,128)(2,1)S(1)} %copy-done.1, f32[8,128]{1,0:T(8,128)S(1)} %get-tuple-element.220.refs_0_), custom_call_target="tpu_custom_call" | custom-call | flops 7516192768 | tf_op jit(solution)/shard_map/pallas_call | solution.py:183
  106.0 4.0 %collective-permute-start.27 = (f32[128,3584]{1,0:T(8,128)S(1)}, f32[128,3584]{1,0:T(8,128)S(1)}, u32[]{:S(2)}, u32[]{:S(2)}) collective-permute-start(f32[128,3584]{1,0:T(8,128)S(1)} %get-tuple-element.254), channel_id=1, source_target_pairs={{0,24},{1,25},{2,26},{3,27},{4,28},{5,29},{6,30},{7,31},{8,0},{9,1... | collective-permute-start | bytes 5505032 | tf_op jit(solution)/shard_map/back1/ppermute | solution.py:288
  109.9 5.5 %shard_map.56 = (f32[128,3584]{1,0:T(8,128)S(1)}, f32[8,128]{1,0:T(8,128)S(1)}) custom-call(bf16[128,2048]{1,0:T(8,128)(2,1)S(1)} %get-tuple-element.225.mine, bf16[128,2048]{1,0:T(8,128)(2,1)S(1)} %collective-permute-done.17.other, bf16[4096,3584]{1,0:T(8,128)(2,1)S(1)} %copy-done.1, f32[8,128]{1,0:T(8,128)S(1)} %get-tuple-element.229.refs_0_), custom_call_target="tpu_custom_call" | custom-call | flops 7516192768 | tf_op jit(solution)/shard_map/pallas_call | solution.py:183
  115.4 2.4 collective-permute-start.21
  117.8 2.2 collective-permute-start.23
  121.7 5.5 %shard_map.60 = (f32[128,3584]{1,0:T(8,128)S(1)}, f32[8,128]{1,0:T(8,128)S(1)}) custom-call(bf16[128,2048]{1,0:T(8,128)(2,1)S(1)} %get-tuple-element.236.mine, bf16[128,2048]{1,0:T(8,128)(2,1)S(1)} %collective-permute-done.20.other, bf16[4096,3584]{1,0:T(8,128)(2,1)S(1)} %copy-done.1, f32[8,128]{1,0:T(8,128)S(1)} %get-tuple-element.237.refs_0_), custom_call_target="tpu_custom_call" | custom-call | flops 7516192768 | tf_op jit(solution)/shard_map/pallas_call | solution.py:183
  127.2 2.3 collective-permute-start.24
  129.6 5.5 %collective-permute-start.25 = (bf16[64,2048]{1,0:T(8,128)(2,1)S(1)}, bf16[64,2048]{1,0:T(8,128)(2,1)S(1)}, u32[]{:S(2)}, u32[]{:S(2)}) collective-permute-start(bf16[64,2048]{1,0:T(8,128)(2,1)S(1)} %get-tuple-element.245.refs_7_.refs_5_.refs_3_.refs_1_), channel_id=1, source_target_pairs={{0,6},{1,7},{6,4},{7,5},{4,2},{5,3},{10,8},{11,9},{8,14},{9,15},{1... | collective-permute-start | bytes 786440 | tf_op jit(solution)/shard_map/chain21/ppermute | solution.py:276
  137.9 5.5 %shard_map.66 = (f32[128,3584]{1,0:T(8,128)S(1)}, f32[8,128]{1,0:T(8,128)S(1)}) custom-call(bf16[128,2048]{1,0:T(8,128)(2,1)S(1)} %get-tuple-element.235.mine, bf16[128,2048]{1,0:T(8,128)(2,1)S(1)} %collective-permute-done.19.other, bf16[4096,3584]{1,0:T(8,128)(2,1)S(1)} %copy-done.1, f32[8,128]{1,0:T(8,128)S(1)} %get-tuple-element.247.refs_0_), custom_call_target="tpu_custom_call" | custom-call | flops 7516192768 | tf_op jit(solution)/shard_map/pallas_call | solution.py:183
  149.7 5.5 %shard_map.72 = (f32[128,3584]{1,0:T(8,128)S(1)}, f32[8,128]{1,0:T(8,128)S(1)}) custom-call(bf16[128,2048]{1,0:T(8,128)(2,1)S(1)} %get-tuple-element.252.mine, bf16[128,2048]{1,0:T(8,128)(2,1)S(1)} %collective-permute-done.26.other, bf16[4096,3584]{1,0:T(8,128)(2,1)S(1)} %copy-done.1, f32[8,128]{1,0:T(8,128)S(1)} %get-tuple-element.258.refs_0_), custom_call_target="tpu_custom_call" | custom-call | flops 7516192768 | tf_op jit(solution)/shard_map/pallas_call | solution.py:183
  155.2 1.9 collective-permute-start.31
  157.2 5.3 %collective-permute-start.33 = (bf16[64,2048]{1,0:T(8,128)(2,1)S(1)}, bf16[64,2048]{1,0:T(8,128)(2,1)S(1)}, u32[]{:S(2)}, u32[]{:S(2)}) collective-permute-start(bf16[64,2048]{1,0:T(8,128)(2,1)S(1)} %get-tuple-element.262.refs_7_.refs_5_.refs_3_.refs_1_), channel_id=1, source_target_pairs={{0,6},{1,7},{6,4},{7,5},{4,2},{5,3},{10,8},{11,9},{8,14},{9,15},{1... | collective-permute-start | bytes 786440 | tf_op jit(solution)/shard_map/chain25/ppermute | solution.py:276
  163.0 5.5 %shard_map.76 = (f32[128,3584]{1,0:T(8,128)S(1)}, f32[8,128]{1,0:T(8,128)S(1)}) custom-call(bf16[128,2048]{1,0:T(8,128)(2,1)S(1)} %get-tuple-element.263.mine, bf16[128,2048]{1,0:T(8,128)(2,1)S(1)} %collective-permute-done.30.other, bf16[4096,3584]{1,0:T(8,128)(2,1)S(1)} %copy-done.1, f32[8,128]{1,0:T(8,128)S(1)} %get-tuple-element.265.refs_0_), custom_call_target="tpu_custom_call" | custom-call | flops 7516192768 | tf_op jit(solution)/shard_map/pallas_call | solution.py:183
  174.8 5.5 %shard_map.82 = (f32[128,3584]{1,0:T(8,128)S(1)}, f32[8,128]{1,0:T(8,128)S(1)}) custom-call(bf16[128,2048]{1,0:T(8,128)(2,1)S(1)} %get-tuple-element.274.mine, bf16[128,2048]{1,0:T(8,128)(2,1)S(1)} %collective-permute-done.34.other, bf16[4096,3584]{1,0:T(8,128)(2,1)S(1)} %copy-done.1, f32[8,128]{1,0:T(8,128)S(1)} %get-tuple-element.276.refs_0_), custom_call_target="tpu_custom_call" | custom-call | flops 7516192768 | tf_op jit(solution)/shard_map/pallas_call | solution.py:183
  180.3 2.2 collective-permute-start.41
  183.2 4.5 %collective-permute-start.44 = (f32[128,3584]{1,0:T(8,128)S(1)}, f32[128,3584]{1,0:T(8,128)S(1)}, u32[]{:S(2)}, u32[]{:S(2)}) collective-permute-start(f32[128,3584]{1,0:T(8,128)S(1)} %get-tuple-element.305), channel_id=1, source_target_pairs={{0,24},{1,25},{2,26},{3,27},{4,28},{5,29},{6,30},{7,31},{8,0},{9,1... | collective-permute-start | bytes 5505032 | tf_op jit(solution)/shard_map/back4/ppermute | solution.py:288
  187.7 2.5 collective-permute-start.42
  191.4 6.2 %shard_map.88 = (bf16[1024,3584]{1,0:T(8,128)(2,1)}, f32[8,128]{1,0:T(8,128)S(1)}) custom-call(bf16[128,2048]{1,0:T(8,128)(2,1)S(1)} %get-tuple-element.290.mine, bf16[128,2048]{1,0:T(8,128)(2,1)S(1)} %collective-permute-done.40.other, bf16[4096,3584]{1,0:T(8,128)(2,1)S(1)} %copy-done.1, f32[128,3584]{1,0:T(8,128)S(1)} %get-tuple-element.291.refs_0_, ...), custom_call_target="tpu_custom_call" | custom-call | flops 7516192768 | tf_op jit(solution)/shard_map/pallas_call | solution.py:183
  199.6 2.6 collective-permute-start.51
  202.2 6.2 %shard_map.90 = (bf16[1024,3584]{1,0:T(8,128)(2,1)}, f32[8,128]{1,0:T(8,128)S(1)}) custom-call(bf16[128,2048]{1,0:T(8,128)(2,1)S(1)} %get-tuple-element.288.mine, bf16[128,2048]{1,0:T(8,128)(2,1)S(1)} %collective-permute-done.39.other, bf16[4096,3584]{1,0:T(8,128)(2,1)S(1)} %copy-done.1, ...), custom_call_target="tpu_custom_call", output_to_operand_aliasing={{0}: (4, {})} | custom-call | flops 7516192768 | tf_op jit(solution)/shard_map/pallas_call | solution.py:183
  210.7 6.2 %shard_map.93 = (bf16[1024,3584]{1,0:T(8,128)(2,1)}, f32[8,128]{1,0:T(8,128)S(1)}) custom-call(bf16[128,2048]{1,0:T(8,128)(2,1)S(1)} %get-tuple-element.286.mine, bf16[128,2048]{1,0:T(8,128)(2,1)S(1)} %collective-permute-done.38.other, bf16[4096,3584]{1,0:T(8,128)(2,1)S(1)} %copy-done.1, ...), custom_call_target="tpu_custom_call", output_to_operand_aliasing={{0}: (4, {})} | custom-call | flops 7516192768 | tf_op jit(solution)/shard_map/pallas_call | solution.py:183
  219.0 2.7 collective-permute-start.48
  225.0 6.2 %shard_map.99 = (bf16[1024,3584]{1,0:T(8,128)(2,1)}, f32[8,128]{1,0:T(8,128)S(1)}) custom-call(bf16[128,2048]{1,0:T(8,128)(2,1)S(1)} %get-tuple-element.310.mine, bf16[128,2048]{1,0:T(8,128)(2,1)S(1)} %collective-permute-done.47.other, bf16[4096,3584]{1,0:T(8,128)(2,1)S(1)} %copy-done.1, ...), custom_call_target="tpu_custom_call", output_to_operand_aliasing={{0}: (4, {})} | custom-call | flops 7516192768 | tf_op jit(solution)/shard_map/pallas_call | solution.py:183
  236.5 2.7 collective-permute-start.57
  239.2 6.2 %shard_map.105 = (bf16[1024,3584]{1,0:T(8,128)(2,1)}, f32[8,128]{1,0:T(8,128)S(1)}) custom-call(bf16[128,2048]{1,0:T(8,128)(2,1)S(1)} %get-tuple-element.319.mine, bf16[128,2048]{1,0:T(8,128)(2,1)S(1)} %collective-permute-done.50.other, bf16[4096,3584]{1,0:T(8,128)(2,1)S(1)} %copy-done.1, ...), custom_call_target="tpu_custom_call", output_to_operand_aliasing={{0}: (4, {})} | custom-call | flops 7516192768 | tf_op jit(solution)/shard_map/pallas_call | solution.py:183
  247.4 3.1 %collective-permute-start.55 = (bf16[64,2048]{1,0:T(8,128)(2,1)S(1)}, bf16[64,2048]{1,0:T(8,128)(2,1)S(1)}, u32[]{:S(2)}, u32[]{:S(2)}) collective-permute-start(bf16[64,2048]{1,0:T(8,128)(2,1)S(1)} %get-tuple-element.331.refs_7_.refs_5_), channel_id=1, source_target_pairs={{0,6},{1,7},{6,4},{7,5},{4,2},{5,3},{10,8},{11,9},{8,14},{9,15},{1... | collective-permute-start | bytes 786440 | tf_op jit(solution)/shard_map/chain37/ppermute | solution.py:276
  250.8 6.2 %shard_map.109 = (bf16[1024,3584]{1,0:T(8,128)(2,1)}, f32[8,128]{1,0:T(8,128)S(1)}) custom-call(bf16[128,2048]{1,0:T(8,128)(2,1)S(1)} %get-tuple-element.332.mine, bf16[128,2048]{1,0:T(8,128)(2,1)S(1)} %collective-permute-done.54.other, bf16[4096,3584]{1,0:T(8,128)(2,1)S(1)} %copy-done.1, ...), custom_call_target="tpu_custom_call", output_to_operand_aliasing={{0}: (4, {})} | custom-call | flops 7516192768 | tf_op jit(solution)/shard_map/pallas_call | solution.py:183
  259.0 4.2 %collective-permute-done.58.other = bf16[128,2048]{1,0:T(8,128)(2,1)S(1)} collective-permute-done((bf16[128,2048]{1,0:T(8,128)(2,1)S(1)}, bf16[128,2048]{1,0:T(8,128)(2,1)S(1)}, u32[]{:S(2)}, u32[]{:S(2)}) %collective-permute-start.58) | collective-permute-done | bytes 524320 | tf_op jit(solution)/shard_map/swap14/ppermute | solution.py:296
  263.2 6.2 %shard_map.113 = (bf16[1024,3584]{1,0:T(8,128)(2,1)}, f32[8,128]{1,0:T(8,128)S(1)}) custom-call(bf16[128,2048]{1,0:T(8,128)(2,1)S(1)} %get-tuple-element.344.mine, bf16[128,2048]{1,0:T(8,128)(2,1)S(1)} %collective-permute-done.58.other, bf16[4096,3584]{1,0:T(8,128)(2,1)S(1)} %copy-done.1, ...), custom_call_target="tpu_custom_call", output_to_operand_aliasing={{0}: (4, {})} | custom-call | flops 7516192768 | tf_op jit(solution)/shard_map/pallas_call | solution.py:183
  269.4 5.0 %collective-permute-done.56.other = bf16[128,2048]{1,0:T(8,128)(2,1)S(1)} collective-permute-done((bf16[128,2048]{1,0:T(8,128)(2,1)S(1)}, bf16[128,2048]{1,0:T(8,128)(2,1)S(1)}, u32[]{:S(2)}, u32[]{:S(2)}) %collective-permute-start.56) | collective-permute-done | bytes 524320 | tf_op jit(solution)/shard_map/swap15/ppermute | solution.py:296
  274.5 6.2 %shard_map.114 = (bf16[1024,3584]{1,0:T(8,128)(2,1)}, f32[8,128]{1,0:T(8,128)}) custom-call(bf16[128,2048]{1,0:T(8,128)(2,1)S(1)} %get-tuple-element.342.mine, bf16[128,2048]{1,0:T(8,128)(2,1)S(1)} %collective-permute-done.56.other, bf16[4096,3584]{1,0:T(8,128)(2,1)S(1)} %copy-done.1, ...), custom_call_target="tpu_custom_call", output_to_operand_aliasing={{0}: (4, {})} | custom-call | flops 7516192768 | tf_op jit(solution)/shard_map/pallas_call | solution.py:183
  (163 shorter events, 57.8 us)
Async XLA Ops:
  0.1 24.8 %collective-permute-start = (bf16[64,2048]{1,0:T(8,128)(2,1)S(1)}, bf16[64,2048]{1,0:T(8,128)(2,1)S(1)}, u32[]{:S(2)}, u32[]{:S(2)}) collective-permute-start(bf16[64,2048]{1,0:T(8,128)(2,1)S(1)} %get-tuple-element.180.refs_0_), channel_id=1, source_target_pairs={{0,6},{1,7},{6,4},{7,5},{4,2},{5,3},{10,8},{11,9},{8,14},{9,15},{1... | collective-permute-start | bytes 786440 | tf_op jit(solution)/shard_map/chain2/ppermute | solution.py:276
  4.4 24.2 %collective-permute-start.2 = (bf16[64,2048]{1,0:T(8,128)(2,1)S(1)}, bf16[64,2048]{1,0:T(8,128)(2,1)S(1)}, u32[]{:S(2)}, u32[]{:S(2)}) collective-permute-start(bf16[64,2048]{1,0:T(8,128)(2,1)S(1)} %get-tuple-element.187.refs_1_), channel_id=1, source_target_pairs={{0,6},{1,7},{6,4},{7,5},{4,2},{5,3},{10,8},{11,9},{8,14},{9,15},{1... | collective-permute-start | bytes 786440 | tf_op jit(solution)/shard_map/chain3/ppermute | solution.py:276
  62.6 21.1 %collective-permute-start.11 = (bf16[128,2048]{1,0:T(8,128)(2,1)S(1)}, bf16[128,2048]{1,0:T(8,128)(2,1)S(1)}, u32[]{:S(2)}, u32[]{:S(2)}) collective-permute-start(bf16[128,2048]{1,0:T(8,128)(2,1)S(1)} %get-tuple-element.208.mine), channel_id=1, source_target_pairs={{0,1},{1,0},{2,3},{3,2},{4,5},{5,4},{6,7},{7,6},{8,9},{9,8},{10,11... | collective-permute-start | bytes 1572872 | tf_op jit(solution)/shard_map/swap1/ppermute | solution.py:296
  73.6 15.6 %collective-permute-start.10 = (bf16[64,2048]{1,0:T(8,128)(2,1)S(1)}, bf16[64,2048]{1,0:T(8,128)(2,1)S(1)}, u32[]{:S(2)}, u32[]{:S(2)}) collective-permute-start(bf16[64,2048]{1,0:T(8,128)(2,1)S(1)} %get-tuple-element.204.refs_4_.refs_2_.refs_0_), channel_id=1, source_target_pairs={{0,6},{1,7},{6,4},{7,5},{4,2},{5,3},{10,8},{11,9},{8,14},{9,15},{1... | collective-permute-start | bytes 786440 | tf_op jit(solution)/shard_map/chain12/ppermute | solution.py:276
  83.4 13.6 %collective-permute-start.14 = (bf16[128,2048]{1,0:T(8,128)(2,1)S(1)}, bf16[128,2048]{1,0:T(8,128)(2,1)S(1)}, u32[]{:S(2)}, u32[]{:S(2)}) collective-permute-start(bf16[128,2048]{1,0:T(8,128)(2,1)S(1)} %get-tuple-element.218.mine), channel_id=1, source_target_pairs={{0,1},{1,0},{2,3},{3,2},{4,5},{5,4},{6,7},{7,6},{8,9},{9,8},{10,11... | collective-permute-start | bytes 1572872 | tf_op jit(solution)/shard_map/swap2/ppermute | solution.py:296
  89.9 12.6 %collective-permute-start.13 = (bf16[64,2048]{1,0:T(8,128)(2,1)S(1)}, bf16[64,2048]{1,0:T(8,128)(2,1)S(1)}, u32[]{:S(2)}, u32[]{:S(2)}) collective-permute-start(bf16[64,2048]{1,0:T(8,128)(2,1)S(1)} %get-tuple-element.213.refs_4_.refs_2_.refs_0_), channel_id=1, source_target_pairs={{0,6},{1,7},{6,4},{7,5},{4,2},{5,3},{10,8},{11,9},{8,14},{9,15},{1... | collective-permute-start | bytes 786440 | tf_op jit(solution)/shard_map/chain14/ppermute | solution.py:276
  90.7 12.6 %collective-permute-start.15 = (bf16[64,2048]{1,0:T(8,128)(2,1)S(1)}, bf16[64,2048]{1,0:T(8,128)(2,1)S(1)}, u32[]{:S(2)}, u32[]{:S(2)}) collective-permute-start(bf16[64,2048]{1,0:T(8,128)(2,1)S(1)} %get-tuple-element.217.refs_5_.refs_3_.refs_1_), channel_id=1, source_target_pairs={{0,6},{1,7},{6,4},{7,5},{4,2},{5,3},{10,8},{11,9},{8,14},{9,15},{1... | collective-permute-start | bytes 786440 | tf_op jit(solution)/shard_map/chain15/ppermute | solution.py:276
  94.0 11.9 %collective-permute-start.17 = (bf16[128,2048]{1,0:T(8,128)(2,1)S(1)}, bf16[128,2048]{1,0:T(8,128)(2,1)S(1)}, u32[]{:S(2)}, u32[]{:S(2)}) collective-permute-start(bf16[128,2048]{1,0:T(8,128)(2,1)S(1)} %get-tuple-element.225.mine), channel_id=1, source_target_pairs={{0,1},{1,0},{2,3},{3,2},{4,5},{5,4},{6,7},{7,6},{8,9},{9,8},{10,11... | collective-permute-start | bytes 1572872 | tf_op jit(solution)/shard_map/swap3/ppermute | solution.py:296
  94.4 35.1 %collective-permute-start.22 = (f32[128,3584]{1,0:T(8,128)S(1)}, f32[128,3584]{1,0:T(8,128)S(1)}, u32[]{:S(2)}, u32[]{:S(2)}) collective-permute-start(f32[128,3584]{1,0:T(8,128)S(1)} %get-tuple-element.241), channel_id=1, source_target_pairs={{0,24},{1,25},{2,26},{3,27},{4,28},{5,29},{6,30},{7,31},{8,0},{9,1... | collective-permute-start | bytes 5505032 | tf_op jit(solution)/shard_map/back0/ppermute | solution.py:288
  103.2 12.2 %collective-permute-start.16 = (bf16[64,2048]{1,0:T(8,128)(2,1)S(1)}, bf16[64,2048]{1,0:T(8,128)(2,1)S(1)}, u32[]{:S(2)}, u32[]{:S(2)}) collective-permute-start(bf16[64,2048]{1,0:T(8,128)(2,1)S(1)} %get-tuple-element.222.refs_4_.refs_2_.refs_0_), channel_id=1, source_target_pairs={{0,6},{1,7},{6,4},{7,5},{4,2},{5,3},{10,8},{11,9},{8,14},{9,15},{1... | collective-permute-start | bytes 786440 | tf_op jit(solution)/shard_map/chain16/ppermute | solution.py:276
  104.1 13.7 %collective-permute-start.18 = (bf16[64,2048]{1,0:T(8,128)(2,1)S(1)}, bf16[64,2048]{1,0:T(8,128)(2,1)S(1)}, u32[]{:S(2)}, u32[]{:S(2)}) collective-permute-start(bf16[64,2048]{1,0:T(8,128)(2,1)S(1)} %get-tuple-element.224.refs_5_.refs_3_.refs_1_), channel_id=1, source_target_pairs={{0,6},{1,7},{6,4},{7,5},{4,2},{5,3},{10,8},{11,9},{8,14},{9,15},{1... | collective-permute-start | bytes 786440 | tf_op jit(solution)/shard_map/chain17/ppermute | solution.py:276
  104.8 15.4 %collective-permute-start.20 = (bf16[128,2048]{1,0:T(8,128)(2,1)S(1)}, bf16[128,2048]{1,0:T(8,128)(2,1)S(1)}, u32[]{:S(2)}, u32[]{:S(2)}) collective-permute-start(bf16[128,2048]{1,0:T(8,128)(2,1)S(1)} %get-tuple-element.236.mine), channel_id=1, source_target_pairs={{0,1},{1,0},{2,3},{3,2},{4,5},{5,4},{6,7},{7,6},{8,9},{9,8},{10,11... | collective-permute-start | bytes 1572872 | tf_op jit(solution)/shard_map/swap4/ppermute | solution.py:296
  106.0 41.4 %collective-permute-start.27 = (f32[128,3584]{1,0:T(8,128)S(1)}, f32[128,3584]{1,0:T(8,128)S(1)}, u32[]{:S(2)}, u32[]{:S(2)}) collective-permute-start(f32[128,3584]{1,0:T(8,128)S(1)} %get-tuple-element.254), channel_id=1, source_target_pairs={{0,24},{1,25},{2,26},{3,27},{4,28},{5,29},{6,30},{7,31},{8,0},{9,1... | collective-permute-start | bytes 5505032 | tf_op jit(solution)/shard_map/back1/ppermute | solution.py:288
  115.4 11.7 %collective-permute-start.21 = (bf16[64,2048]{1,0:T(8,128)(2,1)S(1)}, bf16[64,2048]{1,0:T(8,128)(2,1)S(1)}, u32[]{:S(2)}, u32[]{:S(2)}) collective-permute-start(bf16[64,2048]{1,0:T(8,128)(2,1)S(1)} %get-tuple-element.231.refs_6_.refs_4_.refs_2_.refs_0_), channel_id=1, source_target_pairs={{0,6},{1,7},{6,4},{7,5},{4,2},{5,3},{10,8},{11,9},{8,14},{9,15},{1... | collective-permute-start | bytes 786440 | tf_op jit(solution)/shard_map/chain18/ppermute | solution.py:276
  117.8 11.7 %collective-permute-start.23 = (bf16[64,2048]{1,0:T(8,128)(2,1)S(1)}, bf16[64,2048]{1,0:T(8,128)(2,1)S(1)}, u32[]{:S(2)}, u32[]{:S(2)}) collective-permute-start(bf16[64,2048]{1,0:T(8,128)(2,1)S(1)} %get-tuple-element.233.refs_7_.refs_5_.refs_3_.refs_1_), channel_id=1, source_target_pairs={{0,6},{1,7},{6,4},{7,5},{4,2},{5,3},{10,8},{11,9},{8,14},{9,15},{1... | collective-permute-start | bytes 786440 | tf_op jit(solution)/shard_map/chain19/ppermute | solution.py:276
  120.2 16.3 %collective-permute-start.19 = (bf16[128,2048]{1,0:T(8,128)(2,1)S(1)}, bf16[128,2048]{1,0:T(8,128)(2,1)S(1)}, u32[]{:S(2)}, u32[]{:S(2)}) collective-permute-start(bf16[128,2048]{1,0:T(8,128)(2,1)S(1)} %get-tuple-element.235.mine), channel_id=1, source_target_pairs={{0,1},{1,0},{2,3},{3,2},{4,5},{5,4},{6,7},{7,6},{8,9},{9,8},{10,11... | collective-permute-start | bytes 1572872 | tf_op jit(solution)/shard_map/swap5/ppermute | solution.py:296
  127.2 16.2 %collective-permute-start.24 = (bf16[64,2048]{1,0:T(8,128)(2,1)S(1)}, bf16[64,2048]{1,0:T(8,128)(2,1)S(1)}, u32[]{:S(2)}, u32[]{:S(2)}) collective-permute-start(bf16[64,2048]{1,0:T(8,128)(2,1)S(1)} %get-tuple-element.239.refs_6_.refs_4_.refs_2_.refs_0_), channel_id=1, source_target_pairs={{0,6},{1,7},{6,4},{7,5},{4,2},{5,3},{10,8},{11,9},{8,14},{9,15},{1... | collective-permute-start | bytes 786440 | tf_op jit(solution)/shard_map/chain20/ppermute | solution.py:276
  129.6 15.8 %collective-permute-start.25 = (bf16[64,2048]{1,0:T(8,128)(2,1)S(1)}, bf16[64,2048]{1,0:T(8,128)(2,1)S(1)}, u32[]{:S(2)}, u32[]{:S(2)}) collective-permute-start(bf16[64,2048]{1,0:T(8,128)(2,1)S(1)} %get-tuple-element.245.refs_7_.refs_5_.refs_3_.refs_1_), channel_id=1, source_target_pairs={{0,6},{1,7},{6,4},{7,5},{4,2},{5,3},{10,8},{11,9},{8,14},{9,15},{1... | collective-permute-start | bytes 786440 | tf_op jit(solution)/shard_map/chain21/ppermute | solution.py:276
  135.3 12.6 %collective-permute-start.26 = (bf16[128,2048]{1,0:T(8,128)(2,1)S(1)}, bf16[128,2048]{1,0:T(8,128)(2,1)S(1)}, u32[]{:S(2)}, u32[]{:S(2)}) collective-permute-start(bf16[128,2048]{1,0:T(8,128)(2,1)S(1)} %get-tuple-element.252.mine), channel_id=1, source_target_pairs={{0,1},{1,0},{2,3},{3,2},{4,5},{5,4},{6,7},{7,6},{8,9},{9,8},{10,11... | collective-permute-start | bytes 1572872 | tf_op jit(solution)/shard_map/swap6/ppermute | solution.py:296
  136.6 33.3 %collective-permute-start.32 = (f32[128,3584]{1,0:T(8,128)S(1)}, f32[128,3584]{1,0:T(8,128)S(1)}, u32[]{:S(2)}, u32[]{:S(2)}) collective-permute-start(f32[128,3584]{1,0:T(8,128)S(1)} %get-tuple-element.269), channel_id=1, source_target_pairs={{0,24},{1,25},{2,26},{3,27},{4,28},{5,29},{6,30},{7,31},{8,0},{9,1... | collective-permute-start | bytes 5505032 | tf_op jit(solution)/shard_map/back2/ppermute | solution.py:288
  143.5 11.7 %collective-permute-start.28 = (bf16[64,2048]{1,0:T(8,128)(2,1)S(1)}, bf16[64,2048]{1,0:T(8,128)(2,1)S(1)}, u32[]{:S(2)}, u32[]{:S(2)}) collective-permute-start(bf16[64,2048]{1,0:T(8,128)(2,1)S(1)} %get-tuple-element.249.refs_6_.refs_4_.refs_2_.refs_0_), channel_id=1, source_target_pairs={{0,6},{1,7},{6,4},{7,5},{4,2},{5,3},{10,8},{11,9},{8,14},{9,15},{1... | collective-permute-start | bytes 786440 | tf_op jit(solution)/shard_map/chain22/ppermute | solution.py:276
  145.5 11.7 %collective-permute-start.29 = (bf16[64,2048]{1,0:T(8,128)(2,1)S(1)}, bf16[64,2048]{1,0:T(8,128)(2,1)S(1)}, u32[]{:S(2)}, u32[]{:S(2)}) collective-permute-start(bf16[64,2048]{1,0:T(8,128)(2,1)S(1)} %get-tuple-element.251.refs_7_.refs_5_.refs_3_.refs_1_), channel_id=1, source_target_pairs={{0,6},{1,7},{6,4},{7,5},{4,2},{5,3},{10,8},{11,9},{8,14},{9,15},{1... | collective-permute-start | bytes 786440 | tf_op jit(solution)/shard_map/chain23/ppermute | solution.py:276
  147.6 15.1 %collective-permute-start.30 = (bf16[128,2048]{1,0:T(8,128)(2,1)S(1)}, bf16[128,2048]{1,0:T(8,128)(2,1)S(1)}, u32[]{:S(2)}, u32[]{:S(2)}) collective-permute-start(bf16[128,2048]{1,0:T(8,128)(2,1)S(1)} %get-tuple-element.263.mine), channel_id=1, source_target_pairs={{0,1},{1,0},{2,3},{3,2},{4,5},{5,4},{6,7},{7,6},{8,9},{9,8},{10,11... | collective-permute-start | bytes 1572872 | tf_op jit(solution)/shard_map/swap7/ppermute | solution.py:296
  147.9 39.8 %collective-permute-start.37 = (f32[128,3584]{1,0:T(8,128)S(1)}, f32[128,3584]{1,0:T(8,128)S(1)}, u32[]{:S(2)}, u32[]{:S(2)}) collective-permute-start(f32[128,3584]{1,0:T(8,128)S(1)} %get-tuple-element.282), channel_id=1, source_target_pairs={{0,24},{1,25},{2,26},{3,27},{4,28},{5,29},{6,30},{7,31},{8,0},{9,1... | collective-permute-start | bytes 5505032 | tf_op jit(solution)/shard_map/back3/ppermute | solution.py:288
  155.2 13.2 %collective-permute-start.31 = (bf16[64,2048]{1,0:T(8,128)(2,1)S(1)}, bf16[64,2048]{1,0:T(8,128)(2,1)S(1)}, u32[]{:S(2)}, u32[]{:S(2)}) collective-permute-start(bf16[64,2048]{1,0:T(8,128)(2,1)S(1)} %get-tuple-element.260.refs_6_.refs_4_.refs_2_.refs_0_), channel_id=1, source_target_pairs={{0,6},{1,7},{6,4},{7,5},{4,2},{5,3},{10,8},{11,9},{8,14},{9,15},{1... | collective-permute-start | bytes 786440 | tf_op jit(solution)/shard_map/chain24/ppermute | solution.py:276
  157.2 14.6 %collective-permute-start.33 = (bf16[64,2048]{1,0:T(8,128)(2,1)S(1)}, bf16[64,2048]{1,0:T(8,128)(2,1)S(1)}, u32[]{:S(2)}, u32[]{:S(2)}) collective-permute-start(bf16[64,2048]{1,0:T(8,128)(2,1)S(1)} %get-tuple-element.262.refs_7_.refs_5_.refs_3_.refs_1_), channel_id=1, source_target_pairs={{0,6},{1,7},{6,4},{7,5},{4,2},{5,3},{10,8},{11,9},{8,14},{9,15},{1... | collective-permute-start | bytes 786440 | tf_op jit(solution)/shard_map/chain25/ppermute | solution.py:276
  162.7 12.1 %collective-permute-start.34 = (bf16[128,2048]{1,0:T(8,128)(2,1)S(1)}, bf16[128,2048]{1,0:T(8,128)(2,1)S(1)}, u32[]{:S(2)}, u32[]{:S(2)}) collective-permute-start(bf16[128,2048]{1,0:T(8,128)(2,1)S(1)} %get-tuple-element.274.mine), channel_id=1, source_target_pairs={{0,1},{1,0},{2,3},{3,2},{4,5},{5,4},{6,7},{7,6},{8,9},{9,8},{10,11... | collective-permute-start | bytes 1572872 | tf_op jit(solution)/shard_map/swap8/ppermute | solution.py:296
  168.5 22.0 %collective-permute-start.40 = (bf16[128,2048]{1,0:T(8,128)(2,1)S(1)}, bf16[128,2048]{1,0:T(8,128)(2,1)S(1)}, u32[]{:S(2)}, u32[]{:S(2)}) collective-permute-start(bf16[128,2048]{1,0:T(8,128)(2,1)S(1)} %get-tuple-element.290.mine), channel_id=1, source_target_pairs={{0,1},{1,0},{2,3},{3,2},{4,5},{5,4},{6,7},{7,6},{8,9},{9,8},{10,11... | collective-permute-start | bytes 1572872 | tf_op jit(solution)/shard_map/swap0/ppermute | solution.py:296
  180.3 17.2 %collective-permute-start.41 = (bf16[64,2048]{1,0:T(8,128)(2,1)S(1)}, bf16[64,2048]{1,0:T(8,128)(2,1)S(1)}, u32[]{:S(2)}, u32[]{:S(2)}) collective-permute-start(bf16[64,2048]{1,0:T(8,128)(2,1)S(1)} %get-tuple-element.278.refs_6_.refs_4_.refs_2_.refs_0_), channel_id=1, source_target_pairs={{0,6},{1,7},{6,4},{7,5},{4,2},{5,3},{10,8},{11,9},{8,14},{9,15},{1... | collective-permute-start | bytes 786440 | tf_op jit(solution)/shard_map/chain28/ppermute | solution.py:276
  182.5 17.0 %collective-permute-start.39 = (bf16[128,2048]{1,0:T(8,128)(2,1)S(1)}, bf16[128,2048]{1,0:T(8,128)(2,1)S(1)}, u32[]{:S(2)}, u32[]{:S(2)}) collective-permute-start(bf16[128,2048]{1,0:T(8,128)(2,1)S(1)} %get-tuple-element.288.mine), channel_id=1, source_target_pairs={{0,1},{1,0},{2,3},{3,2},{4,5},{5,4},{6,7},{7,6},{8,9},{9,8},{10,11... | collective-permute-start | bytes 1572872 | tf_op jit(solution)/shard_map/swap9/ppermute | solution.py:296
  183.2 35.7 %collective-permute-start.44 = (f32[128,3584]{1,0:T(8,128)S(1)}, f32[128,3584]{1,0:T(8,128)S(1)}, u32[]{:S(2)}, u32[]{:S(2)}) collective-permute-start(f32[128,3584]{1,0:T(8,128)S(1)} %get-tuple-element.305), channel_id=1, source_target_pairs={{0,24},{1,25},{2,26},{3,27},{4,28},{5,29},{6,30},{7,31},{8,0},{9,1... | collective-permute-start | bytes 5505032 | tf_op jit(solution)/shard_map/back4/ppermute | solution.py:288
  187.7 20.7 %collective-permute-start.42 = (bf16[64,2048]{1,0:T(8,128)(2,1)S(1)}, bf16[64,2048]{1,0:T(8,128)(2,1)S(1)}, u32[]{:S(2)}, u32[]{:S(2)}) collective-permute-start(bf16[64,2048]{1,0:T(8,128)(2,1)S(1)} %get-tuple-element.280.refs_7_.refs_5_.refs_3_.refs_1_), channel_id=1, source_target_pairs={{0,6},{1,7},{6,4},{7,5},{4,2},{5,3},{10,8},{11,9},{8,14},{9,15},{1... | collective-permute-start | bytes 786440 | tf_op jit(solution)/shard_map/chain29/ppermute | solution.py:276
  190.4 20.2 %collective-permute-start.38 = (bf16[128,2048]{1,0:T(8,128)(2,1)S(1)}, bf16[128,2048]{1,0:T(8,128)(2,1)S(1)}, u32[]{:S(2)}, u32[]{:S(2)}) collective-permute-start(bf16[128,2048]{1,0:T(8,128)(2,1)S(1)} %get-tuple-element.286.mine), channel_id=1, source_target_pairs={{0,1},{1,0},{2,3},{3,2},{4,5},{5,4},{6,7},{7,6},{8,9},{9,8},{10,11... | collective-permute-start | bytes 1572872 | tf_op jit(solution)/shard_map/swap10/ppermute | solution.py:296
  197.7 19.3 %collective-permute-start.43 = (bf16[64,2048]{1,0:T(8,128)(2,1)S(1)}, bf16[64,2048]{1,0:T(8,128)(2,1)S(1)}, u32[]{:S(2)}, u32[]{:S(2)}) collective-permute-start(bf16[64,2048]{1,0:T(8,128)(2,1)S(1)} %get-tuple-element.297.refs_6_.refs_4_.refs_2_.refs_0_), channel_id=1, source_target_pairs={{0,6},{1,7},{6,4},{7,5},{4,2},{5,3},{10,8},{11,9},{8,14},{9,15},{1... | collective-permute-start | bytes 786440 | tf_op jit(solution)/shard_map/chain30/ppermute | solution.py:276
  199.6 35.5 %collective-permute-start.51 = (f32[128,3584]{1,0:T(8,128)S(1)}, f32[128,3584]{1,0:T(8,128)S(1)}, u32[]{:S(2)}, u32[]{:S(2)}) collective-permute-start(f32[128,3584]{1,0:T(8,128)S(1)} %get-tuple-element.323), channel_id=1, source_target_pairs={{0,24},{1,25},{2,26},{3,27},{4,28},{5,29},{6,30},{7,31},{8,0},{9,1... | collective-permute-start | bytes 5505032 | tf_op jit(solution)/shard_map/back5/ppermute | solution.py:288
  210.6 12.9 %collective-permute-start.47 = (bf16[128,2048]{1,0:T(8,128)(2,1)S(1)}, bf16[128,2048]{1,0:T(8,128)(2,1)S(1)}, u32[]{:S(2)}, u32[]{:S(2)}) collective-permute-start(bf16[128,2048]{1,0:T(8,128)(2,1)S(1)} %get-tuple-element.310.mine), channel_id=1, source_target_pairs={{0,1},{1,0},{2,3},{3,2},{4,5},{5,4},{6,7},{7,6},{8,9},{9,8},{10,11... | collective-permute-start | bytes 1572872 | tf_op jit(solution)/shard_map/swap11/ppermute | solution.py:296
  217.0 14.2 %collective-permute-start.46 = (bf16[64,2048]{1,0:T(8,128)(2,1)S(1)}, bf16[64,2048]{1,0:T(8,128)(2,1)S(1)}, u32[]{:S(2)}, u32[]{:S(2)}) collective-permute-start(bf16[64,2048]{1,0:T(8,128)(2,1)S(1)} %get-tuple-element.303.refs_6_.refs_4_.refs_2_.refs_0_), channel_id=1, source_target_pairs={{0,6},{1,7},{6,4},{7,5},{4,2},{5,3},{10,8},{11,9},{8,14},{9,15},{1... | collective-permute-start | bytes 786440 | tf_op jit(solution)/shard_map/chain32/ppermute | solution.py:276
  219.0 14.2 %collective-permute-start.48 = (bf16[64,2048]{1,0:T(8,128)(2,1)S(1)}, bf16[64,2048]{1,0:T(8,128)(2,1)S(1)}, u32[]{:S(2)}, u32[]{:S(2)}) collective-permute-start(bf16[64,2048]{1,0:T(8,128)(2,1)S(1)} %get-tuple-element.309.refs_7_.refs_5_.refs_3_.refs_1_), channel_id=1, source_target_pairs={{0,6},{1,7},{6,4},{7,5},{4,2},{5,3},{10,8},{11,9},{8,14},{9,15},{1... | collective-permute-start | bytes 786440 | tf_op jit(solution)/shard_map/chain33/ppermute | solution.py:276
  221.9 14.6 %collective-permute-start.50 = (bf16[128,2048]{1,0:T(8,128)(2,1)S(1)}, bf16[128,2048]{1,0:T(8,128)(2,1)S(1)}, u32[]{:S(2)}, u32[]{:S(2)}) collective-permute-start(bf16[128,2048]{1,0:T(8,128)(2,1)S(1)} %get-tuple-element.319.mine), channel_id=1, source_target_pairs={{0,1},{1,0},{2,3},{3,2},{4,5},{5,4},{6,7},{7,6},{8,9},{9,8},{10,11... | collective-permute-start | bytes 1572872 | tf_op jit(solution)/shard_map/swap12/ppermute | solution.py:296
  223.6 39.7 %collective-permute-start.59 = (f32[128,3584]{1,0:T(8,128)S(1)}, f32[128,3584]{1,0:T(8,128)S(1)}, u32[]{:S(2)}, u32[]{:S(2)}) collective-permute-start(f32[128,3584]{1,0:T(8,128)S(1)} %get-tuple-element.345), channel_id=1, source_target_pairs={{0,24},{1,25},{2,26},{3,27},{4,28},{5,29},{6,30},{7,31},{8,0},{9,1... | collective-permute-start | bytes 5505032 | tf_op jit(solution)/shard_map/back6/ppermute | solution.py:288
  231.3 14.2 %collective-permute-start.49 = (bf16[64,2048]{1,0:T(8,128)(2,1)S(1)}, bf16[64,2048]{1,0:T(8,128)(2,1)S(1)}, u32[]{:S(2)}, u32[]{:S(2)}) collective-permute-start(bf16[64,2048]{1,0:T(8,128)(2,1)S(1)} %get-tuple-element.316.refs_6_.refs_4_.refs_2_), channel_id=1, source_target_pairs={{0,6},{1,7},{6,4},{7,5},{4,2},{5,3},{10,8},{11,9},{8,14},{9,15},{1... | collective-permute-start | bytes 786440 | tf_op jit(solution)/shard_map/chain34/ppermute | solution.py:276
  233.2 14.2 %collective-permute-start.52 = (bf16[64,2048]{1,0:T(8,128)(2,1)S(1)}, bf16[64,2048]{1,0:T(8,128)(2,1)S(1)}, u32[]{:S(2)}, u32[]{:S(2)}) collective-permute-start(bf16[64,2048]{1,0:T(8,128)(2,1)S(1)} %get-tuple-element.318.refs_7_.refs_5_.refs_3_), channel_id=1, source_target_pairs={{0,6},{1,7},{6,4},{7,5},{4,2},{5,3},{10,8},{11,9},{8,14},{9,15},{1... | collective-permute-start | bytes 786440 | tf_op jit(solution)/shard_map/chain35/ppermute | solution.py:276
  235.3 15.4 %collective-permute-start.54 = (bf16[128,2048]{1,0:T(8,128)(2,1)S(1)}, bf16[128,2048]{1,0:T(8,128)(2,1)S(1)}, u32[]{:S(2)}, u32[]{:S(2)}) collective-permute-start(bf16[128,2048]{1,0:T(8,128)(2,1)S(1)} %get-tuple-element.332.mine), channel_id=1, source_target_pairs={{0,1},{1,0},{2,3},{3,2},{4,5},{5,4},{6,7},{7,6},{8,9},{9,8},{10,11... | collective-permute-start | bytes 1572872 | tf_op jit(solution)/shard_map/swap13/ppermute | solution.py:296
  236.5 37.9 %collective-permute-start.57 = (f32[128,3584]{1,0:T(8,128)S(1)}, f32[128,3584]{1,0:T(8,128)S(1)}, u32[]{:S(2)}, u32[]{:S(2)}) collective-permute-start(f32[128,3584]{1,0:T(8,128)S(1)} %get-tuple-element.343), channel_id=1, source_target_pairs={{0,24},{1,25},{2,26},{3,27},{4,28},{5,29},{6,30},{7,31},{8,0},{9,1... | collective-permute-start | bytes 5505032 | tf_op jit(solution)/shard_map/back7/ppermute | solution.py:288
  245.4 11.6 %collective-permute-start.53 = (bf16[64,2048]{1,0:T(8,128)(2,1)S(1)}, bf16[64,2048]{1,0:T(8,128)(2,1)S(1)}, u32[]{:S(2)}, u32[]{:S(2)}) collective-permute-start(bf16[64,2048]{1,0:T(8,128)(2,1)S(1)} %get-tuple-element.329.refs_6_.refs_4_), channel_id=1, source_target_pairs={{0,6},{1,7},{6,4},{7,5},{4,2},{5,3},{10,8},{11,9},{8,14},{9,15},{1... | collective-permute-start | bytes 786440 | tf_op jit(solution)/shard_map/chain36/ppermute | solution.py:276
  247.4 11.4 %collective-permute-start.55 = (bf16[64,2048]{1,0:T(8,128)(2,1)S(1)}, bf16[64,2048]{1,0:T(8,128)(2,1)S(1)}, u32[]{:S(2)}, u32[]{:S(2)}) collective-permute-start(bf16[64,2048]{1,0:T(8,128)(2,1)S(1)} %get-tuple-element.331.refs_7_.refs_5_), channel_id=1, source_target_pairs={{0,6},{1,7},{6,4},{7,5},{4,2},{5,3},{10,8},{11,9},{8,14},{9,15},{1... | collective-permute-start | bytes 786440 | tf_op jit(solution)/shard_map/chain37/ppermute | solution.py:276
  250.7 12.5 %collective-permute-start.58 = (bf16[128,2048]{1,0:T(8,128)(2,1)S(1)}, bf16[128,2048]{1,0:T(8,128)(2,1)S(1)}, u32[]{:S(2)}, u32[]{:S(2)}) collective-permute-start(bf16[128,2048]{1,0:T(8,128)(2,1)S(1)} %get-tuple-element.344.mine), channel_id=1, source_target_pairs={{0,1},{1,0},{2,3},{3,2},{4,5},{5,4},{6,7},{7,6},{8,9},{9,8},{10,11... | collective-permute-start | bytes 1572872 | tf_op jit(solution)/shard_map/swap14/ppermute | solution.py:296
  258.9 15.6 %collective-permute-start.56 = (bf16[128,2048]{1,0:T(8,128)(2,1)S(1)}, bf16[128,2048]{1,0:T(8,128)(2,1)S(1)}, u32[]{:S(2)}, u32[]{:S(2)}) collective-permute-start(bf16[128,2048]{1,0:T(8,128)(2,1)S(1)} %get-tuple-element.342.mine), channel_id=1, source_target_pairs={{0,1},{1,0},{2,3},{3,2},{4,5},{5,4},{6,7},{7,6},{8,9},{9,8},{10,11... | collective-permute-start | bytes 1572872 | tf_op jit(solution)/shard_map/swap15/ppermute | solution.py:296
  (14 other events, 170.6 us)

commit v3 on v2

--- a/solution.py
+++ b/solution.py
@@ -12,6 +12,7 @@
 STREAM = (0, 1, 1, 1, 1, 1, 1, 1, 1, 0, 0, 0, 0, 0, 0, 0)
 SUB = 2
 BACK_STEPS = 3
+LOADS = 4
 MIB = 1024 * 1024
 CHOOSE_VMEM = 4 * MIB
 PRODUCT_VMEM = 12 * MIB
@@ -72,17 +73,17 @@
     )(*args)
 
 
-def load_kernel(x, *refs):
+def load_kernel(start, x, *refs):
     out, _, sem = refs[-3:]
-    copy = pltpu.make_async_copy(x, out, sem)
+    copy = pltpu.make_async_copy(x.at[pl.ds(start, out.shape[0])], out, sem)
     copy.start()
     copy.wait()
 
 
-def load(x, tokens):
+def load(x, start, size, tokens):
     return pl.pallas_call(
-        load_kernel,
-        out_shape=(pltpu.VMEM(x.shape, x.dtype), TOKEN),
+        functools.partial(load_kernel, start),
+        out_shape=(pltpu.VMEM((size, x.shape[1]), x.dtype), TOKEN),
         in_specs=[ANYWHERE] * (1 + len(tokens)),
         out_specs=(pl.BlockSpec(memory_space=pltpu.VMEM), ANYWHERE),
         scratch_shapes=[pltpu.SemaphoreType.DMA],
@@ -107,14 +108,16 @@
     )(x, *tokens)
 
 
-def product_kernel(start, has_back, tile, side_of, mine, other, weight, *refs):
+def product_kernel(start, has_back, tile, side_of, mine, other, *refs):
+    weights, refs = refs[:LOADS], refs[LOADS:]
     if has_back:
         back = refs[0]
-        out, _, near, far, slots, in_sems, out_sems, held, back_sems = refs[-9:]
+        out, _, features, slots, in_sems, out_sems, held, back_sems = refs[-8:]
     else:
-        out, _, near, far, slots, in_sems, out_sems = refs[-7:]
-    many, half = near.shape
-    tiles = weight.shape[1] // tile
+        out, _, features, slots, in_sems, out_sems = refs[-6:]
+    many, half = mine.shape
+    part = weights[0].shape[0]
+    tiles = weights[0].shape[1] // tile
 
     def back_copy(j, at):
         return pltpu.make_async_copy(back.at[:, pl.ds(at, tile)], held.at[:, pl.ds(at, tile)], back_sems.at[j])
@@ -123,23 +126,32 @@
         at = pl.multiple_of(j * tile, tile)
         return pltpu.make_async_copy(slots.at[slot], out.at[pl.ds(start, many), pl.ds(at, tile)], out_sems.at[slot])
 
-    fetch = [pltpu.make_async_copy(mine, near, in_sems.at[0]), pltpu.make_async_copy(other, far, in_sems.at[1])]
-    for c in fetch:
-        c.start()
-    if has_back:
-        for j in range(tiles):
-            back_copy(j, j * tile).start()
-    for c in fetch:
-        c.wait()
+    def fetch(first, second):
+        copies = [
+            pltpu.make_async_copy(first, features.at[:, pl.ds(0, half)], in_sems.at[0]),
+            pltpu.make_async_copy(second, features.at[:, pl.ds(half, half)], in_sems.at[1]),
+        ]
+        for c in copies:
+            c.start()
+        if has_back:
+            for j in range(tiles):
+                back_copy(j, j * tile).start()
+        for c in copies:
+            c.wait()
+
     side = side_of(lax.axis_index("col"))
-    near_rows = pl.ds(pl.multiple_of(side * half, half), half)
-    far_rows = pl.ds(pl.multiple_of((1 - side) * half, half), half)
+    pl.when(side == 0)(lambda: fetch(mine, other))
+    pl.when(side != 0)(lambda: fetch(other, mine))
 
     def one_tile(j, carry):
         slot = lax.rem(j, 2)
         at = pl.multiple_of(j * tile, tile)
-        total = jnp.dot(near[...], weight[near_rows, pl.ds(at, tile)], preferred_element_type=jnp.float32)
-        total += jnp.dot(far[...], weight[far_rows, pl.ds(at, tile)], preferred_element_type=jnp.float32)
+        total = None
+        for i, weight in enumerate(weights):
+            term = jnp.dot(
+                features[:, i * part:(i + 1) * part], weight[:, pl.ds(at, tile)], preferred_element_type=jnp.float32
+            )
+            total = term if total is None else total + term
         if has_back:
             back_copy(j, at).wait()
             total += held[:, pl.ds(at, tile)]
@@ -153,17 +165,17 @@
         out_copy(j, j % 2).wait()
 
 
-def product(side_of, mine, other, weight, tokens, back=None, into=None, start=0):
-    depth, width = weight.shape
+def product(side_of, mine, other, weights, tokens, back=None, into=None, start=0):
+    part, width = weights[0].shape
+    depth = part * len(weights)
     many = mine.shape[0]
     tile = max(t for t in range(128, 513, 128) if width % t == 0)
-    args = [mine, other, pltpu.with_memory_space_constraint(weight, pltpu.VMEM)]
-    in_specs = [ANYWHERE, ANYWHERE, pl.BlockSpec(memory_space=pltpu.VMEM)]
+    args = [mine, other] + [pltpu.with_memory_space_constraint(w, pltpu.VMEM) for w in weights]
+    in_specs = [ANYWHERE, ANYWHERE] + [pl.BlockSpec(memory_space=pltpu.VMEM)] * len(weights)
     aliases = {}
     dtype = jnp.float32 if back is None else jnp.bfloat16
     scratch = [
-        pltpu.VMEM((many, depth // 2), weight.dtype),
-        pltpu.VMEM((many, depth // 2), weight.dtype),
+        pltpu.VMEM((many, depth), mine.dtype),
         pltpu.VMEM((2, many, tile), dtype),
         pltpu.SemaphoreType.DMA((2,)),
         pltpu.SemaphoreType.DMA((2,)),
@@ -249,7 +261,7 @@
 
     seen = []
     sent, held_last, mine, other, back, arriving = {}, {}, {}, {}, {}, {}
-    out, waiting = None, []
+    out, waiting, weights = None, [], []
     last_chain = chunks - 1 + SUB * (n_row - 1)
     first = 0 if pieces[0][0] == 1 else SUB
     for step in range(first, max(when.values()) + 1):
@@ -274,8 +286,10 @@
             if step <= last_chain:
                 with jax.named_scope(f"chain{step}"):
                     arriving[step] = lax.ppermute(value, AXES, chain + cross if crossing else chain)
-        if step == first + SUB - 1:
-            weight, token = load(weight, seen)
+        if len(weights) < LOADS and (step - first) % SUB == SUB - 1:
+            part = weight.shape[0] // LOADS
+            loaded, token = load(weight, len(weights) * part, part, seen)
+            weights.append(loaded)
             seen = [token]
         if waiting and step >= sent_back[waiting[0][0]]:
             piece, partial = waiting.pop(0)
@@ -299,12 +313,12 @@
                 continue
             group, piece = pieces[at]
             if group == 1:
-                partial, token = product(side_of, mine[at], other[at], weight, seen)
+                partial, token = product(side_of, mine[at], other[at], weights, seen)
                 seen = [token]
                 waiting.append((piece, partial))
             else:
                 out, token = product(
-                    side_of, mine[at], other[at], weight, seen, back[piece], (count, out), piece * size
+                    side_of, mine[at], other[at], weights, seen, back[piece], (count, out), piece * size
                 )
                 seen = [token]
     return out

time: 283 us -> 271 us (0.958)
  waiting for transfers between devices: 30.7 us -> 18.4 us
  local copies, waits for them, and re-layouts: 9.68 us -> 0 us
  starting transfers between devices: 123 us -> 129 us
  Pallas kernels: 116 us -> 119 us
    ppermute x36, waiting for transfers between devices: 19.6 us -> 7.8 us  [body(): lax.ppermute(value, AXES, chain + cross if crossing else chain)]
    unnamed x4 -> x0, local copies, waits for them, and re-layouts: 9.68 us -> none
    ppermute x16, starting transfers between devices: 11.3 us -> 14.5 us  [body(): other[at] = lax.ppermute(mine[at], AXES, swap_pairs)]
    pallas_call x1 -> x4, Pallas kernels: 9.36 us -> 12.4 us  [load(): pl.pallas_call(functools.partial(load_kernel, start), out_shape=(pltpu.VM...]
  transfers between devices with their start and end apart: 60 -> 60, of which waited for: 13 -> 12; matrix products, arithmetic and copies ran while one was open for 0% -> 0% of each run, Pallas kernels for 39% -> 42%
where the time goes in v3:
time: 271 us; the launch traced here: 268 us
  starting transfers between devices  129 us (48%)
  Pallas kernels  119 us (44%)
  waiting for transfers between devices  18.4 us (7%)
    pallas_call x16, Pallas kernels, product(): pl.pallas_call(functools.partial(product_kernel, start, back is not None,...  93.3 us
    ppermute x36, starting transfers between devices, body(): lax.ppermute(value, AXES, chain + cross if crossing else chain)  91.6 us
    ppermute x8, starting transfers between devices, body(): back[piece] = lax.ppermute(partial, AXES, back_pairs)  23.3 us
    ppermute x16, starting transfers between devices, body(): other[at] = lax.ppermute(mine[at], AXES, swap_pairs)  14.5 us
    pallas_call x48, Pallas kernels, choose(): pl.pallas_call(functools.partial(choose_kernel, len(options), parts, whic...  13.3 us
    pallas_call x4, Pallas kernels, load(): pl.pallas_call(functools.partial(load_kernel, start), out_shape=(pltpu.VM...  12.4 us
    ppermute x16, waiting for transfers between devices, body(): other[at] = lax.ppermute(mine[at], AXES, swap_pairs)  10.6 us
    ppermute x36, waiting for transfers between devices, body(): lax.ppermute(value, AXES, chain + cross if crossing else chain)  7.8 us
  transfers between devices with their start and end apart: 60, of which 12 were waited for; matrix products, arithmetic and copies ran while one was open for 0% of the time, Pallas kernels for 42%

profile of v3, /device:TPU:1, one launch (start us, length us, event | category | flops | bytes accessed | tf_op | source)
XLA Modules:
  0.0 268.2 jit_solution(16751421268805860370)
XLA Ops:
  0.1 4.2 %collective-permute-start = (bf16[64,2048]{1,0:T(8,128)(2,1)S(1)}, bf16[64,2048]{1,0:T(8,128)(2,1)S(1)}, u32[]{:S(2)}, u32[]{:S(2)}) collective-permute-start(bf16[64,2048]{1,0:T(8,128)(2,1)S(1)} %get-tuple-element.186.refs_0_), channel_id=1, source_target_pairs={{0,6},{1,7},{6,4},{7,5},{4,2},{5,3},{10,8},{11,9},{8,14},{9,15},{1... | collective-permute-start | bytes 786440 | tf_op jit(solution)/shard_map/chain2/ppermute | solution.py:288
  5.9 3.1 %shard_map.32 = (bf16[1024,3584]{1,0:T(8,128)(2,1)S(1)}, f32[8,128]{1,0:T(8,128)S(1)}) custom-call(bf16[4096,3584]{1,0:T(8,128)(2,1)} %x.7, f32[8,128]{1,0:T(8,128)S(1)} %get-tuple-element.190.refs_0_), custom_call_target="tpu_custom_call" | custom-call | tf_op jit(solution)/shard_map/pallas_call | solution.py:84
  10.0 4.1 %collective-permute-start.1 = (bf16[64,2048]{1,0:T(8,128)(2,1)S(1)}, bf16[64,2048]{1,0:T(8,128)(2,1)S(1)}, u32[]{:S(2)}, u32[]{:S(2)}) collective-permute-start(bf16[64,2048]{1,0:T(8,128)(2,1)S(1)} %get-tuple-element.192.refs_2_.refs_0_), channel_id=1, source_target_pairs={{0,6},{1,7},{6,4},{7,5},{4,2},{5,3},{10,8},{11,9},{8,14},{9,15},{1... | collective-permute-start | bytes 786440 | tf_op jit(solution)/shard_map/chain4/ppermute | solution.py:288
  15.6 4.1 %collective-permute-start.4 = (bf16[64,2048]{1,0:T(8,128)(2,1)S(1)}, bf16[64,2048]{1,0:T(8,128)(2,1)S(1)}, u32[]{:S(2)}, u32[]{:S(2)}) collective-permute-start(bf16[64,2048]{1,0:T(8,128)(2,1)S(1)} %get-tuple-element.198.refs_3_.refs_1_), channel_id=1, source_target_pairs={{0,6},{1,7},{6,4},{7,5},{4,2},{5,3},{10,8},{11,9},{8,14},{9,15},{1... | collective-permute-start | bytes 786440 | tf_op jit(solution)/shard_map/chain5/ppermute | solution.py:288
  19.7 3.1 %shard_map.35 = (bf16[1024,3584]{1,0:T(8,128)(2,1)S(1)}, f32[8,128]{1,0:T(8,128)S(1)}) custom-call(bf16[4096,3584]{1,0:T(8,128)(2,1)} %x.7, f32[8,128]{1,0:T(8,128)S(1)} %get-tuple-element.195.refs_0_), custom_call_target="tpu_custom_call" | custom-call | tf_op jit(solution)/shard_map/pallas_call | solution.py:84
  26.3 4.1 %collective-permute-start.6 = (bf16[64,2048]{1,0:T(8,128)(2,1)S(1)}, bf16[64,2048]{1,0:T(8,128)(2,1)S(1)}, u32[]{:S(2)}, u32[]{:S(2)}) collective-permute-start(bf16[64,2048]{1,0:T(8,128)(2,1)S(1)} %get-tuple-element.203.refs_5_.refs_3_.refs_1_), channel_id=1, source_target_pairs={{0,6},{1,7},{6,4},{7,5},{4,2},{5,3},{10,8},{11,9},{8,14},{9,15},{1... | collective-permute-start | bytes 786440 | tf_op jit(solution)/shard_map/chain7/ppermute | solution.py:288
  30.3 3.1 %shard_map.38 = (bf16[1024,3584]{1,0:T(8,128)(2,1)S(1)}, f32[8,128]{1,0:T(8,128)S(1)}) custom-call(bf16[4096,3584]{1,0:T(8,128)(2,1)} %x.7, f32[8,128]{1,0:T(8,128)S(1)} %get-tuple-element.200.refs_0_), custom_call_target="tpu_custom_call" | custom-call | tf_op jit(solution)/shard_map/pallas_call | solution.py:84
  36.9 4.1 %collective-permute-start.8 = (bf16[64,2048]{1,0:T(8,128)(2,1)S(1)}, bf16[64,2048]{1,0:T(8,128)(2,1)S(1)}, u32[]{:S(2)}, u32[]{:S(2)}) collective-permute-start(bf16[64,2048]{1,0:T(8,128)(2,1)S(1)} %get-tuple-element.209.refs_5_.refs_3_.refs_1_), channel_id=1, source_target_pairs={{0,6},{1,7},{6,4},{7,5},{4,2},{5,3},{10,8},{11,9},{8,14},{9,15},{1... | collective-permute-start | bytes 786440 | tf_op jit(solution)/shard_map/chain9/ppermute | solution.py:288
  41.0 3.1 %shard_map.41 = (bf16[1024,3584]{1,0:T(8,128)(2,1)S(1)}, f32[8,128]{1,0:T(8,128)S(1)}) custom-call(bf16[4096,3584]{1,0:T(8,128)(2,1)} %x.7, f32[8,128]{1,0:T(8,128)S(1)} %get-tuple-element.205.refs_0_), custom_call_target="tpu_custom_call" | custom-call | tf_op jit(solution)/shard_map/pallas_call | solution.py:84
  49.1 4.2 %collective-permute-start.7 = (bf16[64,2048]{1,0:T(8,128)(2,1)S(1)}, bf16[64,2048]{1,0:T(8,128)(2,1)S(1)}, u32[]{:S(2)}, u32[]{:S(2)}) collective-permute-start(bf16[64,2048]{1,0:T(8,128)(2,1)S(1)} %get-tuple-element.208.refs_4_.refs_2_.refs_0_), channel_id=1, source_target_pairs={{0,6},{1,7},{6,4},{7,5},{4,2},{5,3},{10,8},{11,9},{8,14},{9,15},{1... | collective-permute-start | bytes 786440 | tf_op jit(solution)/shard_map/chain10/ppermute | solution.py:288
  57.3 3.8 %collective-permute-start.10 = (bf16[64,2048]{1,0:T(8,128)(2,1)S(1)}, bf16[64,2048]{1,0:T(8,128)(2,1)S(1)}, u32[]{:S(2)}, u32[]{:S(2)}) collective-permute-start(bf16[64,2048]{1,0:T(8,128)(2,1)S(1)} %get-tuple-element.213.refs_4_.refs_2_.refs_0_), channel_id=1, source_target_pairs={{0,6},{1,7},{6,4},{7,5},{4,2},{5,3},{10,8},{11,9},{8,14},{9,15},{1... | collective-permute-start | bytes 786440 | tf_op jit(solution)/shard_map/chain12/ppermute | solution.py:288
  61.9 4.1 %collective-permute-start.12 = (bf16[64,2048]{1,0:T(8,128)(2,1)S(1)}, bf16[64,2048]{1,0:T(8,128)(2,1)S(1)}, u32[]{:S(2)}, u32[]{:S(2)}) collective-permute-start(bf16[64,2048]{1,0:T(8,128)(2,1)S(1)} %get-tuple-element.216.refs_5_.refs_3_.refs_1_), channel_id=1, source_target_pairs={{0,6},{1,7},{6,4},{7,5},{4,2},{5,3},{10,8},{11,9},{8,14},{9,15},{1... | collective-permute-start | bytes 786440 | tf_op jit(solution)/shard_map/chain13/ppermute | solution.py:288
  66.4 5.4 %shard_map.49 = (f32[128,3584]{1,0:T(8,128)S(1)}, f32[8,128]{1,0:T(8,128)S(1)}) custom-call(bf16[128,2048]{1,0:T(8,128)(2,1)S(1)} %get-tuple-element.217.mine, bf16[128,2048]{1,0:T(8,128)(2,1)S(1)} %collective-permute-done.11.other, bf16[1024,3584]{1,0:T(8,128)(2,1)S(1)} %get-tuple-element.218.refs_0_, bf16[1024,3584]{1,0:T(8,128)(2,1)S(1)} %get-tuple-element.219.refs_1_, ...), custom_call_target="tpu_custom_call" | custom-call | flops 7516192768 | tf_op jit(solution)/shard_map/pallas_call | solution.py:195
  72.6 2.4 collective-permute-start.13
  75.7 1.9 collective-permute-start.15
  79.0 5.9 %collective-permute-start.22 = (f32[128,3584]{1,0:T(8,128)S(1)}, f32[128,3584]{1,0:T(8,128)S(1)}, u32[]{:S(2)}, u32[]{:S(2)}) collective-permute-start(f32[128,3584]{1,0:T(8,128)S(1)} %get-tuple-element.253), channel_id=1, source_target_pairs={{0,24},{1,25},{2,26},{3,27},{4,28},{5,29},{6,30},{7,31},{8,0},{9,1... | collective-permute-start | bytes 5505032 | tf_op jit(solution)/shard_map/back0/ppermute | solution.py:302
  84.9 5.4 %shard_map.54 = (f32[128,3584]{1,0:T(8,128)S(1)}, f32[8,128]{1,0:T(8,128)S(1)}) custom-call(bf16[128,2048]{1,0:T(8,128)(2,1)S(1)} %get-tuple-element.230.mine, bf16[128,2048]{1,0:T(8,128)(2,1)S(1)} %collective-permute-done.14.other, bf16[1024,3584]{1,0:T(8,128)(2,1)S(1)} %get-tuple-element.218.refs_0_, bf16[1024,3584]{1,0:T(8,128)(2,1)S(1)} %get-tuple-element.219.refs_1_, ...), custom_call_target="tpu_custom_call" | custom-call | flops 7516192768 | tf_op jit(solution)/shard_map/pallas_call | solution.py:195
  94.0 3.6 %collective-permute-start.27 = (f32[128,3584]{1,0:T(8,128)S(1)}, f32[128,3584]{1,0:T(8,128)S(1)}, u32[]{:S(2)}, u32[]{:S(2)}) collective-permute-start(f32[128,3584]{1,0:T(8,128)S(1)} %get-tuple-element.266), channel_id=1, source_target_pairs={{0,24},{1,25},{2,26},{3,27},{4,28},{5,29},{6,30},{7,31},{8,0},{9,1... | collective-permute-start | bytes 5505032 | tf_op jit(solution)/shard_map/back1/ppermute | solution.py:302
  97.6 5.4 %shard_map.59 = (f32[128,3584]{1,0:T(8,128)S(1)}, f32[8,128]{1,0:T(8,128)S(1)}) custom-call(bf16[128,2048]{1,0:T(8,128)(2,1)S(1)} %get-tuple-element.237.mine, bf16[128,2048]{1,0:T(8,128)(2,1)S(1)} %collective-permute-done.17.other, bf16[1024,3584]{1,0:T(8,128)(2,1)S(1)} %get-tuple-element.218.refs_0_, bf16[1024,3584]{1,0:T(8,128)(2,1)S(1)} %get-tuple-element.219.refs_1_, ...), custom_call_target="tpu_custom_call" | custom-call | flops 7516192768 | tf_op jit(solution)/shard_map/pallas_call | solution.py:195
  103.1 2.3 collective-permute-start.21
  105.3 2.8 %collective-permute-start.23 = (bf16[64,2048]{1,0:T(8,128)(2,1)S(1)}, bf16[64,2048]{1,0:T(8,128)(2,1)S(1)}, u32[]{:S(2)}, u32[]{:S(2)}) collective-permute-start(bf16[64,2048]{1,0:T(8,128)(2,1)S(1)} %get-tuple-element.245.refs_7_.refs_5_.refs_3_.refs_1_), channel_id=1, source_target_pairs={{0,6},{1,7},{6,4},{7,5},{4,2},{5,3},{10,8},{11,9},{8,14},{9,15},{1... | collective-permute-start | bytes 786440 | tf_op jit(solution)/shard_map/chain19/ppermute | solution.py:288
  108.3 2.2 collective-permute-start.19
  110.5 5.4 %shard_map.63 = (f32[128,3584]{1,0:T(8,128)S(1)}, f32[8,128]{1,0:T(8,128)S(1)}) custom-call(bf16[128,2048]{1,0:T(8,128)(2,1)S(1)} %get-tuple-element.248.mine, bf16[128,2048]{1,0:T(8,128)(2,1)S(1)} %collective-permute-done.20.other, bf16[1024,3584]{1,0:T(8,128)(2,1)S(1)} %get-tuple-element.218.refs_0_, bf16[1024,3584]{1,0:T(8,128)(2,1)S(1)} %get-tuple-element.219.refs_1_, ...), custom_call_target="tpu_custom_call" | custom-call | flops 7516192768 | tf_op jit(solution)/shard_map/pallas_call | solution.py:195
  118.1 4.4 %collective-permute-start.25 = (bf16[64,2048]{1,0:T(8,128)(2,1)S(1)}, bf16[64,2048]{1,0:T(8,128)(2,1)S(1)}, u32[]{:S(2)}, u32[]{:S(2)}) collective-permute-start(bf16[64,2048]{1,0:T(8,128)(2,1)S(1)} %get-tuple-element.257.refs_7_.refs_5_.refs_3_.refs_1_), channel_id=1, source_target_pairs={{0,6},{1,7},{6,4},{7,5},{4,2},{5,3},{10,8},{11,9},{8,14},{9,15},{1... | collective-permute-start | bytes 786440 | tf_op jit(solution)/shard_map/chain21/ppermute | solution.py:288
  125.4 5.4 %shard_map.69 = (f32[128,3584]{1,0:T(8,128)S(1)}, f32[8,128]{1,0:T(8,128)S(1)}) custom-call(bf16[128,2048]{1,0:T(8,128)(2,1)S(1)} %get-tuple-element.247.mine, bf16[128,2048]{1,0:T(8,128)(2,1)S(1)} %collective-permute-done.19.other, bf16[1024,3584]{1,0:T(8,128)(2,1)S(1)} %get-tuple-element.218.refs_0_, bf16[1024,3584]{1,0:T(8,128)(2,1)S(1)} %get-tuple-element.219.refs_1_, ...), custom_call_target="tpu_custom_call" | custom-call | flops 7516192768 | tf_op jit(solution)/shard_map/pallas_call | solution.py:195
  137.1 5.6 %shard_map.75 = (f32[128,3584]{1,0:T(8,128)S(1)}, f32[8,128]{1,0:T(8,128)S(1)}) custom-call(bf16[128,2048]{1,0:T(8,128)(2,1)S(1)} %get-tuple-element.264.mine, bf16[128,2048]{1,0:T(8,128)(2,1)S(1)} %collective-permute-done.26.other, bf16[1024,3584]{1,0:T(8,128)(2,1)S(1)} %get-tuple-element.218.refs_0_, bf16[1024,3584]{1,0:T(8,128)(2,1)S(1)} %get-tuple-element.219.refs_1_, ...), custom_call_target="tpu_custom_call" | custom-call | flops 7516192768 | tf_op jit(solution)/shard_map/pallas_call | solution.py:195
  142.8 2.1 collective-permute-start.31
  145.0 4.8 %collective-permute-start.33 = (bf16[64,2048]{1,0:T(8,128)(2,1)S(1)}, bf16[64,2048]{1,0:T(8,128)(2,1)S(1)}, u32[]{:S(2)}, u32[]{:S(2)}) collective-permute-start(bf16[64,2048]{1,0:T(8,128)(2,1)S(1)} %get-tuple-element.274.refs_7_.refs_5_.refs_3_.refs_1_), channel_id=1, source_target_pairs={{0,6},{1,7},{6,4},{7,5},{4,2},{5,3},{10,8},{11,9},{8,14},{9,15},{1... | collective-permute-start | bytes 786440 | tf_op jit(solution)/shard_map/chain25/ppermute | solution.py:288
  150.3 5.4 %shard_map.79 = (f32[128,3584]{1,0:T(8,128)S(1)}, f32[8,128]{1,0:T(8,128)S(1)}) custom-call(bf16[128,2048]{1,0:T(8,128)(2,1)S(1)} %get-tuple-element.275.mine, bf16[128,2048]{1,0:T(8,128)(2,1)S(1)} %collective-permute-done.30.other, bf16[1024,3584]{1,0:T(8,128)(2,1)S(1)} %get-tuple-element.218.refs_0_, bf16[1024,3584]{1,0:T(8,128)(2,1)S(1)} %get-tuple-element.219.refs_1_, ...), custom_call_target="tpu_custom_call" | custom-call | flops 7516192768 | tf_op jit(solution)/shard_map/pallas_call | solution.py:195
  159.1 2.6 collective-permute-start.36
  162.1 5.4 %shard_map.85 = (f32[128,3584]{1,0:T(8,128)S(1)}, f32[8,128]{1,0:T(8,128)S(1)}) custom-call(bf16[128,2048]{1,0:T(8,128)(2,1)S(1)} %get-tuple-element.286.mine, bf16[128,2048]{1,0:T(8,128)(2,1)S(1)} %collective-permute-done.34.other, bf16[1024,3584]{1,0:T(8,128)(2,1)S(1)} %get-tuple-element.218.refs_0_, bf16[1024,3584]{1,0:T(8,128)(2,1)S(1)} %get-tuple-element.219.refs_1_, ...), custom_call_target="tpu_custom_call" | custom-call | flops 7516192768 | tf_op jit(solution)/shard_map/pallas_call | solution.py:195
  167.6 2.2 collective-permute-start.41
  171.1 3.9 %collective-permute-start.44 = (f32[128,3584]{1,0:T(8,128)S(1)}, f32[128,3584]{1,0:T(8,128)S(1)}, u32[]{:S(2)}, u32[]{:S(2)}) collective-permute-start(f32[128,3584]{1,0:T(8,128)S(1)} %get-tuple-element.317), channel_id=1, source_target_pairs={{0,24},{1,25},{2,26},{3,27},{4,28},{5,29},{6,30},{7,31},{8,0},{9,1... | collective-permute-start | bytes 5505032 | tf_op jit(solution)/shard_map/back4/ppermute | solution.py:302
  175.0 2.5 collective-permute-start.42
  178.6 6.2 %shard_map.91 = (bf16[1024,3584]{1,0:T(8,128)(2,1)}, f32[8,128]{1,0:T(8,128)S(1)}) custom-call(bf16[128,2048]{1,0:T(8,128)(2,1)S(1)} %get-tuple-element.302.mine, bf16[128,2048]{1,0:T(8,128)(2,1)S(1)} %collective-permute-done.40.other, bf16[1024,3584]{1,0:T(8,128)(2,1)S(1)} %get-tuple-element.218.refs_0_, bf16[1024,3584]{1,0:T(8,128)(2,1)S(1)} %get-tuple-element.219.refs_1_, ...), custom_call_target="tpu_custom_call" | custom-call | flops 7516192768 | tf_op jit(solution)/shard_map/pallas_call | solution.py:195
  186.8 2.7 collective-permute-start.51
  189.5 6.2 %shard_map.93 = (bf16[1024,3584]{1,0:T(8,128)(2,1)}, f32[8,128]{1,0:T(8,128)S(1)}) custom-call(bf16[128,2048]{1,0:T(8,128)(2,1)S(1)} %get-tuple-element.300.mine, bf16[128,2048]{1,0:T(8,128)(2,1)S(1)} %collective-permute-done.39.other, bf16[1024,3584]{1,0:T(8,128)(2,1)S(1)} %get-tuple-element.218.refs_0_, ...), custom_call_target="tpu_custom_call", output_to_operand_aliasing={{0}: (7, {})} | custom-call | flops 7516192768 | tf_op jit(solution)/shard_map/pallas_call | solution.py:195
  198.0 6.2 %shard_map.96 = (bf16[1024,3584]{1,0:T(8,128)(2,1)}, f32[8,128]{1,0:T(8,128)S(1)}) custom-call(bf16[128,2048]{1,0:T(8,128)(2,1)S(1)} %get-tuple-element.298.mine, bf16[128,2048]{1,0:T(8,128)(2,1)S(1)} %collective-permute-done.38.other, bf16[1024,3584]{1,0:T(8,128)(2,1)S(1)} %get-tuple-element.218.refs_0_, ...), custom_call_target="tpu_custom_call", output_to_operand_aliasing={{0}: (7, {})} | custom-call | flops 7516192768 | tf_op jit(solution)/shard_map/pallas_call | solution.py:195
  206.3 2.8 %collective-permute-start.48 = (bf16[64,2048]{1,0:T(8,128)(2,1)S(1)}, bf16[64,2048]{1,0:T(8,128)(2,1)S(1)}, u32[]{:S(2)}, u32[]{:S(2)}) collective-permute-start(bf16[64,2048]{1,0:T(8,128)(2,1)S(1)} %get-tuple-element.321.refs_7_.refs_5_.refs_3_.refs_1_), channel_id=1, source_target_pairs={{0,6},{1,7},{6,4},{7,5},{4,2},{5,3},{10,8},{11,9},{8,14},{9,15},{1... | collective-permute-start | bytes 786440 | tf_op jit(solution)/shard_map/chain33/ppermute | solution.py:288
  212.3 6.2 %shard_map.102 = (bf16[1024,3584]{1,0:T(8,128)(2,1)}, f32[8,128]{1,0:T(8,128)S(1)}) custom-call(bf16[128,2048]{1,0:T(8,128)(2,1)S(1)} %get-tuple-element.322.mine, bf16[128,2048]{1,0:T(8,128)(2,1)S(1)} %collective-permute-done.47.other, bf16[1024,3584]{1,0:T(8,128)(2,1)S(1)} %get-tuple-element.218.refs_0_, ...), custom_call_target="tpu_custom_call", output_to_operand_aliasing={{0}: (7, {})} | custom-call | flops 7516192768 | tf_op jit(solution)/shard_map/pallas_call | solution.py:195
  223.8 2.7 collective-permute-start.57
  226.5 6.2 %shard_map.108 = (bf16[1024,3584]{1,0:T(8,128)(2,1)}, f32[8,128]{1,0:T(8,128)S(1)}) custom-call(bf16[128,2048]{1,0:T(8,128)(2,1)S(1)} %get-tuple-element.331.mine, bf16[128,2048]{1,0:T(8,128)(2,1)S(1)} %collective-permute-done.50.other, bf16[1024,3584]{1,0:T(8,128)(2,1)S(1)} %get-tuple-element.218.refs_0_, ...), custom_call_target="tpu_custom_call", output_to_operand_aliasing={{0}: (7, {})} | custom-call | flops 7516192768 | tf_op jit(solution)/shard_map/pallas_call | solution.py:195
  234.6 3.1 %collective-permute-start.55 = (bf16[64,2048]{1,0:T(8,128)(2,1)S(1)}, bf16[64,2048]{1,0:T(8,128)(2,1)S(1)}, u32[]{:S(2)}, u32[]{:S(2)}) collective-permute-start(bf16[64,2048]{1,0:T(8,128)(2,1)S(1)} %get-tuple-element.343.refs_7_.refs_5_), channel_id=1, source_target_pairs={{0,6},{1,7},{6,4},{7,5},{4,2},{5,3},{10,8},{11,9},{8,14},{9,15},{1... | collective-permute-start | bytes 786440 | tf_op jit(solution)/shard_map/chain37/ppermute | solution.py:288
  238.2 6.2 %shard_map.112 = (bf16[1024,3584]{1,0:T(8,128)(2,1)}, f32[8,128]{1,0:T(8,128)S(1)}) custom-call(bf16[128,2048]{1,0:T(8,128)(2,1)S(1)} %get-tuple-element.344.mine, bf16[128,2048]{1,0:T(8,128)(2,1)S(1)} %collective-permute-done.54.other, bf16[1024,3584]{1,0:T(8,128)(2,1)S(1)} %get-tuple-element.218.refs_0_, ...), custom_call_target="tpu_custom_call", output_to_operand_aliasing={{0}: (7, {})} | custom-call | flops 7516192768 | tf_op jit(solution)/shard_map/pallas_call | solution.py:195
  246.3 4.4 %collective-permute-done.58.other = bf16[128,2048]{1,0:T(8,128)(2,1)S(1)} collective-permute-done((bf16[128,2048]{1,0:T(8,128)(2,1)S(1)}, bf16[128,2048]{1,0:T(8,128)(2,1)S(1)}, u32[]{:S(2)}, u32[]{:S(2)}) %collective-permute-start.58) | collective-permute-done | bytes 524320 | tf_op jit(solution)/shard_map/swap14/ppermute | solution.py:310
  250.6 6.2 %shard_map.116 = (bf16[1024,3584]{1,0:T(8,128)(2,1)}, f32[8,128]{1,0:T(8,128)S(1)}) custom-call(bf16[128,2048]{1,0:T(8,128)(2,1)S(1)} %get-tuple-element.356.mine, bf16[128,2048]{1,0:T(8,128)(2,1)S(1)} %collective-permute-done.58.other, bf16[1024,3584]{1,0:T(8,128)(2,1)S(1)} %get-tuple-element.218.refs_0_, ...), custom_call_target="tpu_custom_call", output_to_operand_aliasing={{0}: (7, {})} | custom-call | flops 7516192768 | tf_op jit(solution)/shard_map/pallas_call | solution.py:195
  256.8 5.0 %collective-permute-done.56.other = bf16[128,2048]{1,0:T(8,128)(2,1)S(1)} collective-permute-done((bf16[128,2048]{1,0:T(8,128)(2,1)S(1)}, bf16[128,2048]{1,0:T(8,128)(2,1)S(1)}, u32[]{:S(2)}, u32[]{:S(2)}) %collective-permute-start.56) | collective-permute-done | bytes 524320 | tf_op jit(solution)/shard_map/swap15/ppermute | solution.py:310
  261.9 6.2 %shard_map.117 = (bf16[1024,3584]{1,0:T(8,128)(2,1)}, f32[8,128]{1,0:T(8,128)}) custom-call(bf16[128,2048]{1,0:T(8,128)(2,1)S(1)} %get-tuple-element.354.mine, bf16[128,2048]{1,0:T(8,128)(2,1)S(1)} %collective-permute-done.56.other, bf16[1024,3584]{1,0:T(8,128)(2,1)S(1)} %get-tuple-element.218.refs_0_, ...), custom_call_target="tpu_custom_call", output_to_operand_aliasing={{0}: (7, {})} | custom-call | flops 7516192768 | tf_op jit(solution)/shard_map/pallas_call | solution.py:195
  (162 shorter events, 64.6 us)
Async XLA Ops:
  10.0 12.8 %collective-permute-start.1 = (bf16[64,2048]{1,0:T(8,128)(2,1)S(1)}, bf16[64,2048]{1,0:T(8,128)(2,1)S(1)}, u32[]{:S(2)}, u32[]{:S(2)}) collective-permute-start(bf16[64,2048]{1,0:T(8,128)(2,1)S(1)} %get-tuple-element.192.refs_2_.refs_0_), channel_id=1, source_target_pairs={{0,6},{1,7},{6,4},{7,5},{4,2},{5,3},{10,8},{11,9},{8,14},{9,15},{1... | collective-permute-start | bytes 786440 | tf_op jit(solution)/shard_map/chain4/ppermute | solution.py:288
  47.8 18.6 %collective-permute-start.11 = (bf16[128,2048]{1,0:T(8,128)(2,1)S(1)}, bf16[128,2048]{1,0:T(8,128)(2,1)S(1)}, u32[]{:S(2)}, u32[]{:S(2)}) collective-permute-start(bf16[128,2048]{1,0:T(8,128)(2,1)S(1)} %get-tuple-element.217.mine), channel_id=1, source_target_pairs={{0,1},{1,0},{2,3},{3,2},{4,5},{5,4},{6,7},{7,6},{8,9},{9,8},{10,11... | collective-permute-start | bytes 1572872 | tf_op jit(solution)/shard_map/swap1/ppermute | solution.py:310
  57.3 14.5 %collective-permute-start.10 = (bf16[64,2048]{1,0:T(8,128)(2,1)S(1)}, bf16[64,2048]{1,0:T(8,128)(2,1)S(1)}, u32[]{:S(2)}, u32[]{:S(2)}) collective-permute-start(bf16[64,2048]{1,0:T(8,128)(2,1)S(1)} %get-tuple-element.213.refs_4_.refs_2_.refs_0_), channel_id=1, source_target_pairs={{0,6},{1,7},{6,4},{7,5},{4,2},{5,3},{10,8},{11,9},{8,14},{9,15},{1... | collective-permute-start | bytes 786440 | tf_op jit(solution)/shard_map/chain12/ppermute | solution.py:288
  61.9 13.1 %collective-permute-start.12 = (bf16[64,2048]{1,0:T(8,128)(2,1)S(1)}, bf16[64,2048]{1,0:T(8,128)(2,1)S(1)}, u32[]{:S(2)}, u32[]{:S(2)}) collective-permute-start(bf16[64,2048]{1,0:T(8,128)(2,1)S(1)} %get-tuple-element.216.refs_5_.refs_3_.refs_1_), channel_id=1, source_target_pairs={{0,6},{1,7},{6,4},{7,5},{4,2},{5,3},{10,8},{11,9},{8,14},{9,15},{1... | collective-permute-start | bytes 786440 | tf_op jit(solution)/shard_map/chain13/ppermute | solution.py:288
  66.1 18.9 %collective-permute-start.14 = (bf16[128,2048]{1,0:T(8,128)(2,1)S(1)}, bf16[128,2048]{1,0:T(8,128)(2,1)S(1)}, u32[]{:S(2)}, u32[]{:S(2)}) collective-permute-start(bf16[128,2048]{1,0:T(8,128)(2,1)S(1)} %get-tuple-element.230.mine), channel_id=1, source_target_pairs={{0,1},{1,0},{2,3},{3,2},{4,5},{5,4},{6,7},{7,6},{8,9},{9,8},{10,11... | collective-permute-start | bytes 1572872 | tf_op jit(solution)/shard_map/swap2/ppermute | solution.py:310
  72.6 17.8 %collective-permute-start.13 = (bf16[64,2048]{1,0:T(8,128)(2,1)S(1)}, bf16[64,2048]{1,0:T(8,128)(2,1)S(1)}, u32[]{:S(2)}, u32[]{:S(2)}) collective-permute-start(bf16[64,2048]{1,0:T(8,128)(2,1)S(1)} %get-tuple-element.225.refs_4_.refs_2_.refs_0_), channel_id=1, source_target_pairs={{0,6},{1,7},{6,4},{7,5},{4,2},{5,3},{10,8},{11,9},{8,14},{9,15},{1... | collective-permute-start | bytes 786440 | tf_op jit(solution)/shard_map/chain14/ppermute | solution.py:288
  75.7 15.5 %collective-permute-start.15 = (bf16[64,2048]{1,0:T(8,128)(2,1)S(1)}, bf16[64,2048]{1,0:T(8,128)(2,1)S(1)}, u32[]{:S(2)}, u32[]{:S(2)}) collective-permute-start(bf16[64,2048]{1,0:T(8,128)(2,1)S(1)} %get-tuple-element.229.refs_5_.refs_3_.refs_1_), channel_id=1, source_target_pairs={{0,6},{1,7},{6,4},{7,5},{4,2},{5,3},{10,8},{11,9},{8,14},{9,15},{1... | collective-permute-start | bytes 786440 | tf_op jit(solution)/shard_map/chain15/ppermute | solution.py:288
  77.7 16.2 %collective-permute-start.17 = (bf16[128,2048]{1,0:T(8,128)(2,1)S(1)}, bf16[128,2048]{1,0:T(8,128)(2,1)S(1)}, u32[]{:S(2)}, u32[]{:S(2)}) collective-permute-start(bf16[128,2048]{1,0:T(8,128)(2,1)S(1)} %get-tuple-element.237.mine), channel_id=1, source_target_pairs={{0,1},{1,0},{2,3},{3,2},{4,5},{5,4},{6,7},{7,6},{8,9},{9,8},{10,11... | collective-permute-start | bytes 1572872 | tf_op jit(solution)/shard_map/swap3/ppermute | solution.py:310
  79.0 38.9 %collective-permute-start.22 = (f32[128,3584]{1,0:T(8,128)S(1)}, f32[128,3584]{1,0:T(8,128)S(1)}, u32[]{:S(2)}, u32[]{:S(2)}) collective-permute-start(f32[128,3584]{1,0:T(8,128)S(1)} %get-tuple-element.253), channel_id=1, source_target_pairs={{0,24},{1,25},{2,26},{3,27},{4,28},{5,29},{6,30},{7,31},{8,0},{9,1... | collective-permute-start | bytes 5505032 | tf_op jit(solution)/shard_map/back0/ppermute | solution.py:302
  91.1 11.9 %collective-permute-start.16 = (bf16[64,2048]{1,0:T(8,128)(2,1)S(1)}, bf16[64,2048]{1,0:T(8,128)(2,1)S(1)}, u32[]{:S(2)}, u32[]{:S(2)}) collective-permute-start(bf16[64,2048]{1,0:T(8,128)(2,1)S(1)} %get-tuple-element.234.refs_4_.refs_2_.refs_0_), channel_id=1, source_target_pairs={{0,6},{1,7},{6,4},{7,5},{4,2},{5,3},{10,8},{11,9},{8,14},{9,15},{1... | collective-permute-start | bytes 786440 | tf_op jit(solution)/shard_map/chain16/ppermute | solution.py:288
  92.0 13.4 %collective-permute-start.18 = (bf16[64,2048]{1,0:T(8,128)(2,1)S(1)}, bf16[64,2048]{1,0:T(8,128)(2,1)S(1)}, u32[]{:S(2)}, u32[]{:S(2)}) collective-permute-start(bf16[64,2048]{1,0:T(8,128)(2,1)S(1)} %get-tuple-element.236.refs_5_.refs_3_.refs_1_), channel_id=1, source_target_pairs={{0,6},{1,7},{6,4},{7,5},{4,2},{5,3},{10,8},{11,9},{8,14},{9,15},{1... | collective-permute-start | bytes 786440 | tf_op jit(solution)/shard_map/chain17/ppermute | solution.py:288
  92.2 16.1 %collective-permute-start.20 = (bf16[128,2048]{1,0:T(8,128)(2,1)S(1)}, bf16[128,2048]{1,0:T(8,128)(2,1)S(1)}, u32[]{:S(2)}, u32[]{:S(2)}) collective-permute-start(bf16[128,2048]{1,0:T(8,128)(2,1)S(1)} %get-tuple-element.248.mine), channel_id=1, source_target_pairs={{0,1},{1,0},{2,3},{3,2},{4,5},{5,4},{6,7},{7,6},{8,9},{9,8},{10,11... | collective-permute-start | bytes 1572872 | tf_op jit(solution)/shard_map/swap4/ppermute | solution.py:310
  94.0 40.9 %collective-permute-start.27 = (f32[128,3584]{1,0:T(8,128)S(1)}, f32[128,3584]{1,0:T(8,128)S(1)}, u32[]{:S(2)}, u32[]{:S(2)}) collective-permute-start(f32[128,3584]{1,0:T(8,128)S(1)} %get-tuple-element.266), channel_id=1, source_target_pairs={{0,24},{1,25},{2,26},{3,27},{4,28},{5,29},{6,30},{7,31},{8,0},{9,1... | collective-permute-start | bytes 5505032 | tf_op jit(solution)/shard_map/back1/ppermute | solution.py:302
  103.1 12.9 %collective-permute-start.21 = (bf16[64,2048]{1,0:T(8,128)(2,1)S(1)}, bf16[64,2048]{1,0:T(8,128)(2,1)S(1)}, u32[]{:S(2)}, u32[]{:S(2)}) collective-permute-start(bf16[64,2048]{1,0:T(8,128)(2,1)S(1)} %get-tuple-element.243.refs_6_.refs_4_.refs_2_.refs_0_), channel_id=1, source_target_pairs={{0,6},{1,7},{6,4},{7,5},{4,2},{5,3},{10,8},{11,9},{8,14},{9,15},{1... | collective-permute-start | bytes 786440 | tf_op jit(solution)/shard_map/chain18/ppermute | solution.py:288
  105.3 12.7 %collective-permute-start.23 = (bf16[64,2048]{1,0:T(8,128)(2,1)S(1)}, bf16[64,2048]{1,0:T(8,128)(2,1)S(1)}, u32[]{:S(2)}, u32[]{:S(2)}) collective-permute-start(bf16[64,2048]{1,0:T(8,128)(2,1)S(1)} %get-tuple-element.245.refs_7_.refs_5_.refs_3_.refs_1_), channel_id=1, source_target_pairs={{0,6},{1,7},{6,4},{7,5},{4,2},{5,3},{10,8},{11,9},{8,14},{9,15},{1... | collective-permute-start | bytes 786440 | tf_op jit(solution)/shard_map/chain19/ppermute | solution.py:288
  108.3 15.8 %collective-permute-start.19 = (bf16[128,2048]{1,0:T(8,128)(2,1)S(1)}, bf16[128,2048]{1,0:T(8,128)(2,1)S(1)}, u32[]{:S(2)}, u32[]{:S(2)}) collective-permute-start(bf16[128,2048]{1,0:T(8,128)(2,1)S(1)} %get-tuple-element.247.mine), channel_id=1, source_target_pairs={{0,1},{1,0},{2,3},{3,2},{4,5},{5,4},{6,7},{7,6},{8,9},{9,8},{10,11... | collective-permute-start | bytes 1572872 | tf_op jit(solution)/shard_map/swap5/ppermute | solution.py:310
  116.0 14.8 %collective-permute-start.24 = (bf16[64,2048]{1,0:T(8,128)(2,1)S(1)}, bf16[64,2048]{1,0:T(8,128)(2,1)S(1)}, u32[]{:S(2)}, u32[]{:S(2)}) collective-permute-start(bf16[64,2048]{1,0:T(8,128)(2,1)S(1)} %get-tuple-element.251.refs_6_.refs_4_.refs_2_.refs_0_), channel_id=1, source_target_pairs={{0,6},{1,7},{6,4},{7,5},{4,2},{5,3},{10,8},{11,9},{8,14},{9,15},{1... | collective-permute-start | bytes 786440 | tf_op jit(solution)/shard_map/chain20/ppermute | solution.py:288
  118.1 14.8 %collective-permute-start.25 = (bf16[64,2048]{1,0:T(8,128)(2,1)S(1)}, bf16[64,2048]{1,0:T(8,128)(2,1)S(1)}, u32[]{:S(2)}, u32[]{:S(2)}) collective-permute-start(bf16[64,2048]{1,0:T(8,128)(2,1)S(1)} %get-tuple-element.257.refs_7_.refs_5_.refs_3_.refs_1_), channel_id=1, source_target_pairs={{0,6},{1,7},{6,4},{7,5},{4,2},{5,3},{10,8},{11,9},{8,14},{9,15},{1... | collective-permute-start | bytes 786440 | tf_op jit(solution)/shard_map/chain21/ppermute | solution.py:288
  122.6 12.8 %collective-permute-start.26 = (bf16[128,2048]{1,0:T(8,128)(2,1)S(1)}, bf16[128,2048]{1,0:T(8,128)(2,1)S(1)}, u32[]{:S(2)}, u32[]{:S(2)}) collective-permute-start(bf16[128,2048]{1,0:T(8,128)(2,1)S(1)} %get-tuple-element.264.mine), channel_id=1, source_target_pairs={{0,1},{1,0},{2,3},{3,2},{4,5},{5,4},{6,7},{7,6},{8,9},{9,8},{10,11... | collective-permute-start | bytes 1572872 | tf_op jit(solution)/shard_map/swap6/ppermute | solution.py:310
  124.1 33.0 %collective-permute-start.32 = (f32[128,3584]{1,0:T(8,128)S(1)}, f32[128,3584]{1,0:T(8,128)S(1)}, u32[]{:S(2)}, u32[]{:S(2)}) collective-permute-start(f32[128,3584]{1,0:T(8,128)S(1)} %get-tuple-element.281), channel_id=1, source_target_pairs={{0,24},{1,25},{2,26},{3,27},{4,28},{5,29},{6,30},{7,31},{8,0},{9,1... | collective-permute-start | bytes 5505032 | tf_op jit(solution)/shard_map/back2/ppermute | solution.py:302
  131.0 11.8 %collective-permute-start.28 = (bf16[64,2048]{1,0:T(8,128)(2,1)S(1)}, bf16[64,2048]{1,0:T(8,128)(2,1)S(1)}, u32[]{:S(2)}, u32[]{:S(2)}) collective-permute-start(bf16[64,2048]{1,0:T(8,128)(2,1)S(1)} %get-tuple-element.261.refs_6_.refs_4_.refs_2_.refs_0_), channel_id=1, source_target_pairs={{0,6},{1,7},{6,4},{7,5},{4,2},{5,3},{10,8},{11,9},{8,14},{9,15},{1... | collective-permute-start | bytes 786440 | tf_op jit(solution)/shard_map/chain22/ppermute | solution.py:288
  133.0 12.0 %collective-permute-start.29 = (bf16[64,2048]{1,0:T(8,128)(2,1)S(1)}, bf16[64,2048]{1,0:T(8,128)(2,1)S(1)}, u32[]{:S(2)}, u32[]{:S(2)}) collective-permute-start(bf16[64,2048]{1,0:T(8,128)(2,1)S(1)} %get-tuple-element.263.refs_7_.refs_5_.refs_3_.refs_1_), channel_id=1, source_target_pairs={{0,6},{1,7},{6,4},{7,5},{4,2},{5,3},{10,8},{11,9},{8,14},{9,15},{1... | collective-permute-start | bytes 786440 | tf_op jit(solution)/shard_map/chain23/ppermute | solution.py:288
  135.1 14.9 %collective-permute-start.30 = (bf16[128,2048]{1,0:T(8,128)(2,1)S(1)}, bf16[128,2048]{1,0:T(8,128)(2,1)S(1)}, u32[]{:S(2)}, u32[]{:S(2)}) collective-permute-start(bf16[128,2048]{1,0:T(8,128)(2,1)S(1)} %get-tuple-element.275.mine), channel_id=1, source_target_pairs={{0,1},{1,0},{2,3},{3,2},{4,5},{5,4},{6,7},{7,6},{8,9},{9,8},{10,11... | collective-permute-start | bytes 1572872 | tf_op jit(solution)/shard_map/swap7/ppermute | solution.py:310
  135.4 39.6 %collective-permute-start.37 = (f32[128,3584]{1,0:T(8,128)S(1)}, f32[128,3584]{1,0:T(8,128)S(1)}, u32[]{:S(2)}, u32[]{:S(2)}) collective-permute-start(f32[128,3584]{1,0:T(8,128)S(1)} %get-tuple-element.294), channel_id=1, source_target_pairs={{0,24},{1,25},{2,26},{3,27},{4,28},{5,29},{6,30},{7,31},{8,0},{9,1... | collective-permute-start | bytes 5505032 | tf_op jit(solution)/shard_map/back3/ppermute | solution.py:302
  142.8 12.9 %collective-permute-start.31 = (bf16[64,2048]{1,0:T(8,128)(2,1)S(1)}, bf16[64,2048]{1,0:T(8,128)(2,1)S(1)}, u32[]{:S(2)}, u32[]{:S(2)}) collective-permute-start(bf16[64,2048]{1,0:T(8,128)(2,1)S(1)} %get-tuple-element.272.refs_6_.refs_4_.refs_2_.refs_0_), channel_id=1, source_target_pairs={{0,6},{1,7},{6,4},{7,5},{4,2},{5,3},{10,8},{11,9},{8,14},{9,15},{1... | collective-permute-start | bytes 786440 | tf_op jit(solution)/shard_map/chain24/ppermute | solution.py:288
  145.0 14.0 %collective-permute-start.33 = (bf16[64,2048]{1,0:T(8,128)(2,1)S(1)}, bf16[64,2048]{1,0:T(8,128)(2,1)S(1)}, u32[]{:S(2)}, u32[]{:S(2)}) collective-permute-start(bf16[64,2048]{1,0:T(8,128)(2,1)S(1)} %get-tuple-element.274.refs_7_.refs_5_.refs_3_.refs_1_), channel_id=1, source_target_pairs={{0,6},{1,7},{6,4},{7,5},{4,2},{5,3},{10,8},{11,9},{8,14},{9,15},{1... | collective-permute-start | bytes 786440 | tf_op jit(solution)/shard_map/chain25/ppermute | solution.py:288
  150.0 12.1 %collective-permute-start.34 = (bf16[128,2048]{1,0:T(8,128)(2,1)S(1)}, bf16[128,2048]{1,0:T(8,128)(2,1)S(1)}, u32[]{:S(2)}, u32[]{:S(2)}) collective-permute-start(bf16[128,2048]{1,0:T(8,128)(2,1)S(1)} %get-tuple-element.286.mine), channel_id=1, source_target_pairs={{0,1},{1,0},{2,3},{3,2},{4,5},{5,4},{6,7},{7,6},{8,9},{9,8},{10,11... | collective-permute-start | bytes 1572872 | tf_op jit(solution)/shard_map/swap8/ppermute | solution.py:310
  155.7 22.0 %collective-permute-start.40 = (bf16[128,2048]{1,0:T(8,128)(2,1)S(1)}, bf16[128,2048]{1,0:T(8,128)(2,1)S(1)}, u32[]{:S(2)}, u32[]{:S(2)}) collective-permute-start(bf16[128,2048]{1,0:T(8,128)(2,1)S(1)} %get-tuple-element.302.mine), channel_id=1, source_target_pairs={{0,1},{1,0},{2,3},{3,2},{4,5},{5,4},{6,7},{7,6},{8,9},{9,8},{10,11... | collective-permute-start | bytes 1572872 | tf_op jit(solution)/shard_map/swap0/ppermute | solution.py:310
  159.1 11.9 %collective-permute-start.36 = (bf16[64,2048]{1,0:T(8,128)(2,1)S(1)}, bf16[64,2048]{1,0:T(8,128)(2,1)S(1)}, u32[]{:S(2)}, u32[]{:S(2)}) collective-permute-start(bf16[64,2048]{1,0:T(8,128)(2,1)S(1)} %get-tuple-element.285.refs_7_.refs_5_.refs_3_.refs_1_), channel_id=1, source_target_pairs={{0,6},{1,7},{6,4},{7,5},{4,2},{5,3},{10,8},{11,9},{8,14},{9,15},{1... | collective-permute-start | bytes 786440 | tf_op jit(solution)/shard_map/chain27/ppermute | solution.py:288
  167.6 17.2 %collective-permute-start.41 = (bf16[64,2048]{1,0:T(8,128)(2,1)S(1)}, bf16[64,2048]{1,0:T(8,128)(2,1)S(1)}, u32[]{:S(2)}, u32[]{:S(2)}) collective-permute-start(bf16[64,2048]{1,0:T(8,128)(2,1)S(1)} %get-tuple-element.290.refs_6_.refs_4_.refs_2_.refs_0_), channel_id=1, source_target_pairs={{0,6},{1,7},{6,4},{7,5},{4,2},{5,3},{10,8},{11,9},{8,14},{9,15},{1... | collective-permute-start | bytes 786440 | tf_op jit(solution)/shard_map/chain28/ppermute | solution.py:288
  169.8 17.0 %collective-permute-start.39 = (bf16[128,2048]{1,0:T(8,128)(2,1)S(1)}, bf16[128,2048]{1,0:T(8,128)(2,1)S(1)}, u32[]{:S(2)}, u32[]{:S(2)}) collective-permute-start(bf16[128,2048]{1,0:T(8,128)(2,1)S(1)} %get-tuple-element.300.mine), channel_id=1, source_target_pairs={{0,1},{1,0},{2,3},{3,2},{4,5},{5,4},{6,7},{7,6},{8,9},{9,8},{10,11... | collective-permute-start | bytes 1572872 | tf_op jit(solution)/shard_map/swap9/ppermute | solution.py:310
  171.1 35.1 %collective-permute-start.44 = (f32[128,3584]{1,0:T(8,128)S(1)}, f32[128,3584]{1,0:T(8,128)S(1)}, u32[]{:S(2)}, u32[]{:S(2)}) collective-permute-start(f32[128,3584]{1,0:T(8,128)S(1)} %get-tuple-element.317), channel_id=1, source_target_pairs={{0,24},{1,25},{2,26},{3,27},{4,28},{5,29},{6,30},{7,31},{8,0},{9,1... | collective-permute-start | bytes 5505032 | tf_op jit(solution)/shard_map/back4/ppermute | solution.py:302
  175.0 20.7 %collective-permute-start.42 = (bf16[64,2048]{1,0:T(8,128)(2,1)S(1)}, bf16[64,2048]{1,0:T(8,128)(2,1)S(1)}, u32[]{:S(2)}, u32[]{:S(2)}) collective-permute-start(bf16[64,2048]{1,0:T(8,128)(2,1)S(1)} %get-tuple-element.292.refs_7_.refs_5_.refs_3_.refs_1_), channel_id=1, source_target_pairs={{0,6},{1,7},{6,4},{7,5},{4,2},{5,3},{10,8},{11,9},{8,14},{9,15},{1... | collective-permute-start | bytes 786440 | tf_op jit(solution)/shard_map/chain29/ppermute | solution.py:288
  177.7 20.2 %collective-permute-start.38 = (bf16[128,2048]{1,0:T(8,128)(2,1)S(1)}, bf16[128,2048]{1,0:T(8,128)(2,1)S(1)}, u32[]{:S(2)}, u32[]{:S(2)}) collective-permute-start(bf16[128,2048]{1,0:T(8,128)(2,1)S(1)} %get-tuple-element.298.mine), channel_id=1, source_target_pairs={{0,1},{1,0},{2,3},{3,2},{4,5},{5,4},{6,7},{7,6},{8,9},{9,8},{10,11... | collective-permute-start | bytes 1572872 | tf_op jit(solution)/shard_map/swap10/ppermute | solution.py:310
  184.9 19.3 %collective-permute-start.43 = (bf16[64,2048]{1,0:T(8,128)(2,1)S(1)}, bf16[64,2048]{1,0:T(8,128)(2,1)S(1)}, u32[]{:S(2)}, u32[]{:S(2)}) collective-permute-start(bf16[64,2048]{1,0:T(8,128)(2,1)S(1)} %get-tuple-element.309.refs_6_.refs_4_.refs_2_.refs_0_), channel_id=1, source_target_pairs={{0,6},{1,7},{6,4},{7,5},{4,2},{5,3},{10,8},{11,9},{8,14},{9,15},{1... | collective-permute-start | bytes 786440 | tf_op jit(solution)/shard_map/chain30/ppermute | solution.py:288
  186.8 35.5 %collective-permute-start.51 = (f32[128,3584]{1,0:T(8,128)S(1)}, f32[128,3584]{1,0:T(8,128)S(1)}, u32[]{:S(2)}, u32[]{:S(2)}) collective-permute-start(f32[128,3584]{1,0:T(8,128)S(1)} %get-tuple-element.335), channel_id=1, source_target_pairs={{0,24},{1,25},{2,26},{3,27},{4,28},{5,29},{6,30},{7,31},{8,0},{9,1... | collective-permute-start | bytes 5505032 | tf_op jit(solution)/shard_map/back5/ppermute | solution.py:302
  197.9 13.0 %collective-permute-start.47 = (bf16[128,2048]{1,0:T(8,128)(2,1)S(1)}, bf16[128,2048]{1,0:T(8,128)(2,1)S(1)}, u32[]{:S(2)}, u32[]{:S(2)}) collective-permute-start(bf16[128,2048]{1,0:T(8,128)(2,1)S(1)} %get-tuple-element.322.mine), channel_id=1, source_target_pairs={{0,1},{1,0},{2,3},{3,2},{4,5},{5,4},{6,7},{7,6},{8,9},{9,8},{10,11... | collective-permute-start | bytes 1572872 | tf_op jit(solution)/shard_map/swap11/ppermute | solution.py:310
  204.3 14.2 %collective-permute-start.46 = (bf16[64,2048]{1,0:T(8,128)(2,1)S(1)}, bf16[64,2048]{1,0:T(8,128)(2,1)S(1)}, u32[]{:S(2)}, u32[]{:S(2)}) collective-permute-start(bf16[64,2048]{1,0:T(8,128)(2,1)S(1)} %get-tuple-element.315.refs_6_.refs_4_.refs_2_.refs_0_), channel_id=1, source_target_pairs={{0,6},{1,7},{6,4},{7,5},{4,2},{5,3},{10,8},{11,9},{8,14},{9,15},{1... | collective-permute-start | bytes 786440 | tf_op jit(solution)/shard_map/chain32/ppermute | solution.py:288
  206.3 14.1 %collective-permute-start.48 = (bf16[64,2048]{1,0:T(8,128)(2,1)S(1)}, bf16[64,2048]{1,0:T(8,128)(2,1)S(1)}, u32[]{:S(2)}, u32[]{:S(2)}) collective-permute-start(bf16[64,2048]{1,0:T(8,128)(2,1)S(1)} %get-tuple-element.321.refs_7_.refs_5_.refs_3_.refs_1_), channel_id=1, source_target_pairs={{0,6},{1,7},{6,4},{7,5},{4,2},{5,3},{10,8},{11,9},{8,14},{9,15},{1... | collective-permute-start | bytes 786440 | tf_op jit(solution)/shard_map/chain33/ppermute | solution.py:288
  209.2 14.6 %collective-permute-start.50 = (bf16[128,2048]{1,0:T(8,128)(2,1)S(1)}, bf16[128,2048]{1,0:T(8,128)(2,1)S(1)}, u32[]{:S(2)}, u32[]{:S(2)}) collective-permute-start(bf16[128,2048]{1,0:T(8,128)(2,1)S(1)} %get-tuple-element.331.mine), channel_id=1, source_target_pairs={{0,1},{1,0},{2,3},{3,2},{4,5},{5,4},{6,7},{7,6},{8,9},{9,8},{10,11... | collective-permute-start | bytes 1572872 | tf_op jit(solution)/shard_map/swap12/ppermute | solution.py:310
  210.8 39.8 %collective-permute-start.59 = (f32[128,3584]{1,0:T(8,128)S(1)}, f32[128,3584]{1,0:T(8,128)S(1)}, u32[]{:S(2)}, u32[]{:S(2)}) collective-permute-start(f32[128,3584]{1,0:T(8,128)S(1)} %get-tuple-element.357), channel_id=1, source_target_pairs={{0,24},{1,25},{2,26},{3,27},{4,28},{5,29},{6,30},{7,31},{8,0},{9,1... | collective-permute-start | bytes 5505032 | tf_op jit(solution)/shard_map/back6/ppermute | solution.py:302
  218.5 14.2 %collective-permute-start.49 = (bf16[64,2048]{1,0:T(8,128)(2,1)S(1)}, bf16[64,2048]{1,0:T(8,128)(2,1)S(1)}, u32[]{:S(2)}, u32[]{:S(2)}) collective-permute-start(bf16[64,2048]{1,0:T(8,128)(2,1)S(1)} %get-tuple-element.328.refs_6_.refs_4_.refs_2_), channel_id=1, source_target_pairs={{0,6},{1,7},{6,4},{7,5},{4,2},{5,3},{10,8},{11,9},{8,14},{9,15},{1... | collective-permute-start | bytes 786440 | tf_op jit(solution)/shard_map/chain34/ppermute | solution.py:288
  220.5 14.2 %collective-permute-start.52 = (bf16[64,2048]{1,0:T(8,128)(2,1)S(1)}, bf16[64,2048]{1,0:T(8,128)(2,1)S(1)}, u32[]{:S(2)}, u32[]{:S(2)}) collective-permute-start(bf16[64,2048]{1,0:T(8,128)(2,1)S(1)} %get-tuple-element.330.refs_7_.refs_5_.refs_3_), channel_id=1, source_target_pairs={{0,6},{1,7},{6,4},{7,5},{4,2},{5,3},{10,8},{11,9},{8,14},{9,15},{1... | collective-permute-start | bytes 786440 | tf_op jit(solution)/shard_map/chain35/ppermute | solution.py:288
  222.6 15.6 %collective-permute-start.54 = (bf16[128,2048]{1,0:T(8,128)(2,1)S(1)}, bf16[128,2048]{1,0:T(8,128)(2,1)S(1)}, u32[]{:S(2)}, u32[]{:S(2)}) collective-permute-start(bf16[128,2048]{1,0:T(8,128)(2,1)S(1)} %get-tuple-element.344.mine), channel_id=1, source_target_pairs={{0,1},{1,0},{2,3},{3,2},{4,5},{5,4},{6,7},{7,6},{8,9},{9,8},{10,11... | collective-permute-start | bytes 1572872 | tf_op jit(solution)/shard_map/swap13/ppermute | solution.py:310
  223.8 38.0 %collective-permute-start.57 = (f32[128,3584]{1,0:T(8,128)S(1)}, f32[128,3584]{1,0:T(8,128)S(1)}, u32[]{:S(2)}, u32[]{:S(2)}) collective-permute-start(f32[128,3584]{1,0:T(8,128)S(1)} %get-tuple-element.355), channel_id=1, source_target_pairs={{0,24},{1,25},{2,26},{3,27},{4,28},{5,29},{6,30},{7,31},{8,0},{9,1... | collective-permute-start | bytes 5505032 | tf_op jit(solution)/shard_map/back7/ppermute | solution.py:302
  232.7 11.8 %collective-permute-start.53 = (bf16[64,2048]{1,0:T(8,128)(2,1)S(1)}, bf16[64,2048]{1,0:T(8,128)(2,1)S(1)}, u32[]{:S(2)}, u32[]{:S(2)}) collective-permute-start(bf16[64,2048]{1,0:T(8,128)(2,1)S(1)} %get-tuple-element.341.refs_6_.refs_4_), channel_id=1, source_target_pairs={{0,6},{1,7},{6,4},{7,5},{4,2},{5,3},{10,8},{11,9},{8,14},{9,15},{1... | collective-permute-start | bytes 786440 | tf_op jit(solution)/shard_map/chain36/ppermute | solution.py:288
  238.1 12.5 %collective-permute-start.58 = (bf16[128,2048]{1,0:T(8,128)(2,1)S(1)}, bf16[128,2048]{1,0:T(8,128)(2,1)S(1)}, u32[]{:S(2)}, u32[]{:S(2)}) collective-permute-start(bf16[128,2048]{1,0:T(8,128)(2,1)S(1)} %get-tuple-element.356.mine), channel_id=1, source_target_pairs={{0,1},{1,0},{2,3},{3,2},{4,5},{5,4},{6,7},{7,6},{8,9},{9,8},{10,11... | collective-permute-start | bytes 1572872 | tf_op jit(solution)/shard_map/swap14/ppermute | solution.py:310
  246.2 15.7 %collective-permute-start.56 = (bf16[128,2048]{1,0:T(8,128)(2,1)S(1)}, bf16[128,2048]{1,0:T(8,128)(2,1)S(1)}, u32[]{:S(2)}, u32[]{:S(2)}) collective-permute-start(bf16[128,2048]{1,0:T(8,128)(2,1)S(1)} %get-tuple-element.354.mine), channel_id=1, source_target_pairs={{0,1},{1,0},{2,3},{3,2},{4,5},{5,4},{6,7},{7,6},{8,9},{9,8},{10,11... | collective-permute-start | bytes 1572872 | tf_op jit(solution)/shard_map/swap15/ppermute | solution.py:310
  (12 other events, 117.3 us)

commit v4 on v3

--- a/solution.py
+++ b/solution.py
@@ -200,7 +200,7 @@
         scratch_shapes=scratch,
         input_output_aliases=aliases,
         compiler_params=pltpu.CompilerParams(vmem_limit_bytes=PRODUCT_VMEM),
-        cost_estimate=pl.CostEstimate(flops=4 * many * depth * width, bytes_accessed=0, transcendentals=0),
+        cost_estimate=pl.CostEstimate(flops=8 * many * depth * width, bytes_accessed=0, transcendentals=0),
     )(*args)
 
 

time: 271 us -> 268 us (0.989)
    ppermute x36, starting transfers between devices: 91.6 us -> 88.2 us  [body(): lax.ppermute(value, AXES, chain + cross if crossing else chain)]
    ppermute x16, starting transfers between devices: 14.5 us -> 17.8 us  [body(): other[at] = lax.ppermute(mine[at], AXES, swap_pairs)]
  transfers between devices with their start and end apart: 60 -> 60, of which waited for: 12 -> 15; matrix products, arithmetic and copies ran while one was open for 0% -> 0% of each run, Pallas kernels for 42% -> 42%
where the time goes in v4:
time: 268 us; the launch traced here: 266 us
  starting transfers between devices  129 us (48%)
  Pallas kernels  119 us (44%)
  waiting for transfers between devices  16.2 us (6%)
    pallas_call x16, Pallas kernels, product(): pl.pallas_call(functools.partial(product_kernel, start, back is not None,...  93.3 us
    ppermute x36, starting transfers between devices, body(): lax.ppermute(value, AXES, chain + cross if crossing else chain)  88.2 us
    ppermute x8, starting transfers between devices, body(): back[piece] = lax.ppermute(partial, AXES, back_pairs)  23.5 us
    ppermute x16, starting transfers between devices, body(): other[at] = lax.ppermute(mine[at], AXES, swap_pairs)  17.8 us
    pallas_call x48, Pallas kernels, choose(): pl.pallas_call(functools.partial(choose_kernel, len(options), parts, whic...  13.3 us
    pallas_call x4, Pallas kernels, load(): pl.pallas_call(functools.partial(load_kernel, start), out_shape=(pltpu.VM...  12.4 us
    ppermute x16, waiting for transfers between devices, body(): other[at] = lax.ppermute(mine[at], AXES, swap_pairs)  8.51 us
    ppermute x36, waiting for transfers between devices, body(): lax.ppermute(value, AXES, chain + cross if crossing else chain)  6.64 us
  transfers between devices with their start and end apart: 60, of which 15 were waited for; matrix products, arithmetic and copies ran while one was open for 0% of the time, Pallas kernels for 42%

profile of v4, /device:TPU:1, one launch (start us, length us, event | category | flops | bytes accessed | tf_op | source)
XLA Modules:
  0.0 265.9 jit_solution(9576276954490141476)
XLA Ops:
  0.1 4.2 %collective-permute-start = (bf16[64,2048]{1,0:T(8,128)(2,1)S(1)}, bf16[64,2048]{1,0:T(8,128)(2,1)S(1)}, u32[]{:S(2)}, u32[]{:S(2)}) collective-permute-start(bf16[64,2048]{1,0:T(8,128)(2,1)S(1)} %get-tuple-element.186.refs_0_), channel_id=1, source_target_pairs={{0,6},{1,7},{6,4},{7,5},{4,2},{5,3},{10,8},{11,9},{8,14},{9,15},{1... | collective-permute-start | bytes 786440 | tf_op jit(solution)/shard_map/chain2/ppermute | solution.py:288
  5.9 3.1 %shard_map.32 = (bf16[1024,3584]{1,0:T(8,128)(2,1)S(1)}, f32[8,128]{1,0:T(8,128)S(1)}) custom-call(bf16[4096,3584]{1,0:T(8,128)(2,1)} %x.7, f32[8,128]{1,0:T(8,128)S(1)} %get-tuple-element.190.refs_0_), custom_call_target="tpu_custom_call" | custom-call | tf_op jit(solution)/shard_map/pallas_call | solution.py:84
  10.0 4.1 %collective-permute-start.1 = (bf16[64,2048]{1,0:T(8,128)(2,1)S(1)}, bf16[64,2048]{1,0:T(8,128)(2,1)S(1)}, u32[]{:S(2)}, u32[]{:S(2)}) collective-permute-start(bf16[64,2048]{1,0:T(8,128)(2,1)S(1)} %get-tuple-element.192.refs_2_.refs_0_), channel_id=1, source_target_pairs={{0,6},{1,7},{6,4},{7,5},{4,2},{5,3},{10,8},{11,9},{8,14},{9,15},{1... | collective-permute-start | bytes 786440 | tf_op jit(solution)/shard_map/chain4/ppermute | solution.py:288
  15.6 4.1 %collective-permute-start.4 = (bf16[64,2048]{1,0:T(8,128)(2,1)S(1)}, bf16[64,2048]{1,0:T(8,128)(2,1)S(1)}, u32[]{:S(2)}, u32[]{:S(2)}) collective-permute-start(bf16[64,2048]{1,0:T(8,128)(2,1)S(1)} %get-tuple-element.198.refs_3_.refs_1_), channel_id=1, source_target_pairs={{0,6},{1,7},{6,4},{7,5},{4,2},{5,3},{10,8},{11,9},{8,14},{9,15},{1... | collective-permute-start | bytes 786440 | tf_op jit(solution)/shard_map/chain5/ppermute | solution.py:288
  19.7 3.1 %shard_map.35 = (bf16[1024,3584]{1,0:T(8,128)(2,1)S(1)}, f32[8,128]{1,0:T(8,128)S(1)}) custom-call(bf16[4096,3584]{1,0:T(8,128)(2,1)} %x.7, f32[8,128]{1,0:T(8,128)S(1)} %get-tuple-element.195.refs_0_), custom_call_target="tpu_custom_call" | custom-call | tf_op jit(solution)/shard_map/pallas_call | solution.py:84
  26.3 4.1 %collective-permute-start.6 = (bf16[64,2048]{1,0:T(8,128)(2,1)S(1)}, bf16[64,2048]{1,0:T(8,128)(2,1)S(1)}, u32[]{:S(2)}, u32[]{:S(2)}) collective-permute-start(bf16[64,2048]{1,0:T(8,128)(2,1)S(1)} %get-tuple-element.203.refs_5_.refs_3_.refs_1_), channel_id=1, source_target_pairs={{0,6},{1,7},{6,4},{7,5},{4,2},{5,3},{10,8},{11,9},{8,14},{9,15},{1... | collective-permute-start | bytes 786440 | tf_op jit(solution)/shard_map/chain7/ppermute | solution.py:288
  30.3 3.1 %shard_map.38 = (bf16[1024,3584]{1,0:T(8,128)(2,1)S(1)}, f32[8,128]{1,0:T(8,128)S(1)}) custom-call(bf16[4096,3584]{1,0:T(8,128)(2,1)} %x.7, f32[8,128]{1,0:T(8,128)S(1)} %get-tuple-element.200.refs_0_), custom_call_target="tpu_custom_call" | custom-call | tf_op jit(solution)/shard_map/pallas_call | solution.py:84
  36.9 4.1 %collective-permute-start.8 = (bf16[64,2048]{1,0:T(8,128)(2,1)S(1)}, bf16[64,2048]{1,0:T(8,128)(2,1)S(1)}, u32[]{:S(2)}, u32[]{:S(2)}) collective-permute-start(bf16[64,2048]{1,0:T(8,128)(2,1)S(1)} %get-tuple-element.209.refs_5_.refs_3_.refs_1_), channel_id=1, source_target_pairs={{0,6},{1,7},{6,4},{7,5},{4,2},{5,3},{10,8},{11,9},{8,14},{9,15},{1... | collective-permute-start | bytes 786440 | tf_op jit(solution)/shard_map/chain9/ppermute | solution.py:288
  41.0 3.1 %shard_map.41 = (bf16[1024,3584]{1,0:T(8,128)(2,1)S(1)}, f32[8,128]{1,0:T(8,128)S(1)}) custom-call(bf16[4096,3584]{1,0:T(8,128)(2,1)} %x.7, f32[8,128]{1,0:T(8,128)S(1)} %get-tuple-element.205.refs_0_), custom_call_target="tpu_custom_call" | custom-call | tf_op jit(solution)/shard_map/pallas_call | solution.py:84
  45.0 1.9 collective-permute-done.8.refs_1_.refs_7_
  49.1 4.2 %collective-permute-start.7 = (bf16[64,2048]{1,0:T(8,128)(2,1)S(1)}, bf16[64,2048]{1,0:T(8,128)(2,1)S(1)}, u32[]{:S(2)}, u32[]{:S(2)}) collective-permute-start(bf16[64,2048]{1,0:T(8,128)(2,1)S(1)} %get-tuple-element.208.refs_4_.refs_2_.refs_0_), channel_id=1, source_target_pairs={{0,6},{1,7},{6,4},{7,5},{4,2},{5,3},{10,8},{11,9},{8,14},{9,15},{1... | collective-permute-start | bytes 786440 | tf_op jit(solution)/shard_map/chain10/ppermute | solution.py:288
  57.3 3.8 %collective-permute-start.10 = (bf16[64,2048]{1,0:T(8,128)(2,1)S(1)}, bf16[64,2048]{1,0:T(8,128)(2,1)S(1)}, u32[]{:S(2)}, u32[]{:S(2)}) collective-permute-start(bf16[64,2048]{1,0:T(8,128)(2,1)S(1)} %get-tuple-element.213.refs_4_.refs_2_.refs_0_), channel_id=1, source_target_pairs={{0,6},{1,7},{6,4},{7,5},{4,2},{5,3},{10,8},{11,9},{8,14},{9,15},{1... | collective-permute-start | bytes 786440 | tf_op jit(solution)/shard_map/chain12/ppermute | solution.py:288
  61.9 4.1 %collective-permute-start.12 = (bf16[64,2048]{1,0:T(8,128)(2,1)S(1)}, bf16[64,2048]{1,0:T(8,128)(2,1)S(1)}, u32[]{:S(2)}, u32[]{:S(2)}) collective-permute-start(bf16[64,2048]{1,0:T(8,128)(2,1)S(1)} %get-tuple-element.216.refs_5_.refs_3_.refs_1_), channel_id=1, source_target_pairs={{0,6},{1,7},{6,4},{7,5},{4,2},{5,3},{10,8},{11,9},{8,14},{9,15},{1... | collective-permute-start | bytes 786440 | tf_op jit(solution)/shard_map/chain13/ppermute | solution.py:288
  66.4 5.4 %shard_map.49 = (f32[128,3584]{1,0:T(8,128)S(1)}, f32[8,128]{1,0:T(8,128)S(1)}) custom-call(bf16[128,2048]{1,0:T(8,128)(2,1)S(1)} %get-tuple-element.217.mine, bf16[128,2048]{1,0:T(8,128)(2,1)S(1)} %collective-permute-done.11.other, bf16[1024,3584]{1,0:T(8,128)(2,1)S(1)} %get-tuple-element.218.refs_0_, bf16[1024,3584]{1,0:T(8,128)(2,1)S(1)} %get-tuple-element.219.refs_1_, ...), custom_call_target="tpu_custom_call" | custom-call | flops 15032385536 | tf_op jit(solution)/shard_map/pallas_call | solution.py:195
  72.6 2.4 collective-permute-start.13
  75.7 1.9 collective-permute-start.15
  79.0 5.9 %collective-permute-start.22 = (f32[128,3584]{1,0:T(8,128)S(1)}, f32[128,3584]{1,0:T(8,128)S(1)}, u32[]{:S(2)}, u32[]{:S(2)}) collective-permute-start(f32[128,3584]{1,0:T(8,128)S(1)} %get-tuple-element.253), channel_id=1, source_target_pairs={{0,24},{1,25},{2,26},{3,27},{4,28},{5,29},{6,30},{7,31},{8,0},{9,1... | collective-permute-start | bytes 5505032 | tf_op jit(solution)/shard_map/back0/ppermute | solution.py:302
  84.9 5.4 %shard_map.54 = (f32[128,3584]{1,0:T(8,128)S(1)}, f32[8,128]{1,0:T(8,128)S(1)}) custom-call(bf16[128,2048]{1,0:T(8,128)(2,1)S(1)} %get-tuple-element.230.mine, bf16[128,2048]{1,0:T(8,128)(2,1)S(1)} %collective-permute-done.14.other, bf16[1024,3584]{1,0:T(8,128)(2,1)S(1)} %get-tuple-element.218.refs_0_, bf16[1024,3584]{1,0:T(8,128)(2,1)S(1)} %get-tuple-element.219.refs_1_, ...), custom_call_target="tpu_custom_call" | custom-call | flops 15032385536 | tf_op jit(solution)/shard_map/pallas_call | solution.py:195
  94.0 3.6 %collective-permute-start.27 = (f32[128,3584]{1,0:T(8,128)S(1)}, f32[128,3584]{1,0:T(8,128)S(1)}, u32[]{:S(2)}, u32[]{:S(2)}) collective-permute-start(f32[128,3584]{1,0:T(8,128)S(1)} %get-tuple-element.266), channel_id=1, source_target_pairs={{0,24},{1,25},{2,26},{3,27},{4,28},{5,29},{6,30},{7,31},{8,0},{9,1... | collective-permute-start | bytes 5505032 | tf_op jit(solution)/shard_map/back1/ppermute | solution.py:302
  97.6 5.4 %shard_map.59 = (f32[128,3584]{1,0:T(8,128)S(1)}, f32[8,128]{1,0:T(8,128)S(1)}) custom-call(bf16[128,2048]{1,0:T(8,128)(2,1)S(1)} %get-tuple-element.237.mine, bf16[128,2048]{1,0:T(8,128)(2,1)S(1)} %collective-permute-done.17.other, bf16[1024,3584]{1,0:T(8,128)(2,1)S(1)} %get-tuple-element.218.refs_0_, bf16[1024,3584]{1,0:T(8,128)(2,1)S(1)} %get-tuple-element.219.refs_1_, ...), custom_call_target="tpu_custom_call" | custom-call | flops 15032385536 | tf_op jit(solution)/shard_map/pallas_call | solution.py:195
  103.1 2.3 collective-permute-start.21
  105.3 2.8 %collective-permute-start.23 = (bf16[64,2048]{1,0:T(8,128)(2,1)S(1)}, bf16[64,2048]{1,0:T(8,128)(2,1)S(1)}, u32[]{:S(2)}, u32[]{:S(2)}) collective-permute-start(bf16[64,2048]{1,0:T(8,128)(2,1)S(1)} %get-tuple-element.245.refs_7_.refs_5_.refs_3_.refs_1_), channel_id=1, source_target_pairs={{0,6},{1,7},{6,4},{7,5},{4,2},{5,3},{10,8},{11,9},{8,14},{9,15},{1... | collective-permute-start | bytes 786440 | tf_op jit(solution)/shard_map/chain19/ppermute | solution.py:288
  108.3 2.2 collective-permute-start.19
  110.5 5.4 %shard_map.63 = (f32[128,3584]{1,0:T(8,128)S(1)}, f32[8,128]{1,0:T(8,128)S(1)}) custom-call(bf16[128,2048]{1,0:T(8,128)(2,1)S(1)} %get-tuple-element.248.mine, bf16[128,2048]{1,0:T(8,128)(2,1)S(1)} %collective-permute-done.20.other, bf16[1024,3584]{1,0:T(8,128)(2,1)S(1)} %get-tuple-element.218.refs_0_, bf16[1024,3584]{1,0:T(8,128)(2,1)S(1)} %get-tuple-element.219.refs_1_, ...), custom_call_target="tpu_custom_call" | custom-call | flops 15032385536 | tf_op jit(solution)/shard_map/pallas_call | solution.py:195
  118.1 4.4 %collective-permute-start.25 = (bf16[64,2048]{1,0:T(8,128)(2,1)S(1)}, bf16[64,2048]{1,0:T(8,128)(2,1)S(1)}, u32[]{:S(2)}, u32[]{:S(2)}) collective-permute-start(bf16[64,2048]{1,0:T(8,128)(2,1)S(1)} %get-tuple-element.257.refs_7_.refs_5_.refs_3_.refs_1_), channel_id=1, source_target_pairs={{0,6},{1,7},{6,4},{7,5},{4,2},{5,3},{10,8},{11,9},{8,14},{9,15},{1... | collective-permute-start | bytes 786440 | tf_op jit(solution)/shard_map/chain21/ppermute | solution.py:288
  124.1 5.4 %shard_map.69 = (f32[128,3584]{1,0:T(8,128)S(1)}, f32[8,128]{1,0:T(8,128)S(1)}) custom-call(bf16[128,2048]{1,0:T(8,128)(2,1)S(1)} %get-tuple-element.247.mine, bf16[128,2048]{1,0:T(8,128)(2,1)S(1)} %collective-permute-done.19.other, bf16[1024,3584]{1,0:T(8,128)(2,1)S(1)} %get-tuple-element.218.refs_0_, bf16[1024,3584]{1,0:T(8,128)(2,1)S(1)} %get-tuple-element.219.refs_1_, ...), custom_call_target="tpu_custom_call" | custom-call | flops 15032385536 | tf_op jit(solution)/shard_map/pallas_call | solution.py:195
  131.5 2.0 collective-permute-start.32
  137.1 5.6 %shard_map.75 = (f32[128,3584]{1,0:T(8,128)S(1)}, f32[8,128]{1,0:T(8,128)S(1)}) custom-call(bf16[128,2048]{1,0:T(8,128)(2,1)S(1)} %get-tuple-element.264.mine, bf16[128,2048]{1,0:T(8,128)(2,1)S(1)} %collective-permute-done.26.other, bf16[1024,3584]{1,0:T(8,128)(2,1)S(1)} %get-tuple-element.218.refs_0_, bf16[1024,3584]{1,0:T(8,128)(2,1)S(1)} %get-tuple-element.219.refs_1_, ...), custom_call_target="tpu_custom_call" | custom-call | flops 15032385536 | tf_op jit(solution)/shard_map/pallas_call | solution.py:195
  142.8 2.2 collective-permute-start.31
  145.1 2.5 collective-permute-start.33
  148.5 5.4 %shard_map.79 = (f32[128,3584]{1,0:T(8,128)S(1)}, f32[8,128]{1,0:T(8,128)S(1)}) custom-call(bf16[128,2048]{1,0:T(8,128)(2,1)S(1)} %get-tuple-element.275.mine, bf16[128,2048]{1,0:T(8,128)(2,1)S(1)} %collective-permute-done.30.other, bf16[1024,3584]{1,0:T(8,128)(2,1)S(1)} %get-tuple-element.218.refs_0_, bf16[1024,3584]{1,0:T(8,128)(2,1)S(1)} %get-tuple-element.219.refs_1_, ...), custom_call_target="tpu_custom_call" | custom-call | flops 15032385536 | tf_op jit(solution)/shard_map/pallas_call | solution.py:195
  155.4 2.1 collective-permute-start.35
  157.6 4.1 %collective-permute-start.36 = (bf16[64,2048]{1,0:T(8,128)(2,1)S(1)}, bf16[64,2048]{1,0:T(8,128)(2,1)S(1)}, u32[]{:S(2)}, u32[]{:S(2)}) collective-permute-start(bf16[64,2048]{1,0:T(8,128)(2,1)S(1)} %get-tuple-element.285.refs_7_.refs_5_.refs_3_.refs_1_), channel_id=1, source_target_pairs={{0,6},{1,7},{6,4},{7,5},{4,2},{5,3},{10,8},{11,9},{8,14},{9,15},{1... | collective-permute-start | bytes 786440 | tf_op jit(solution)/shard_map/chain27/ppermute | solution.py:288
  161.8 5.4 %shard_map.85 = (f32[128,3584]{1,0:T(8,128)S(1)}, f32[8,128]{1,0:T(8,128)S(1)}) custom-call(bf16[128,2048]{1,0:T(8,128)(2,1)S(1)} %get-tuple-element.286.mine, bf16[128,2048]{1,0:T(8,128)(2,1)S(1)} %collective-permute-done.34.other, bf16[1024,3584]{1,0:T(8,128)(2,1)S(1)} %get-tuple-element.218.refs_0_, bf16[1024,3584]{1,0:T(8,128)(2,1)S(1)} %get-tuple-element.219.refs_1_, ...), custom_call_target="tpu_custom_call" | custom-call | flops 15032385536 | tf_op jit(solution)/shard_map/pallas_call | solution.py:195
  167.4 1.9 collective-permute-start.41
  170.7 3.4 %collective-permute-start.44 = (f32[128,3584]{1,0:T(8,128)S(1)}, f32[128,3584]{1,0:T(8,128)S(1)}, u32[]{:S(2)}, u32[]{:S(2)}) collective-permute-start(f32[128,3584]{1,0:T(8,128)S(1)} %get-tuple-element.317), channel_id=1, source_target_pairs={{0,24},{1,25},{2,26},{3,27},{4,28},{5,29},{6,30},{7,31},{8,0},{9,1... | collective-permute-start | bytes 5505032 | tf_op jit(solution)/shard_map/back4/ppermute | solution.py:302
  177.3 6.2 %shard_map.91 = (bf16[1024,3584]{1,0:T(8,128)(2,1)}, f32[8,128]{1,0:T(8,128)S(1)}) custom-call(bf16[128,2048]{1,0:T(8,128)(2,1)S(1)} %get-tuple-element.302.mine, bf16[128,2048]{1,0:T(8,128)(2,1)S(1)} %collective-permute-done.40.other, bf16[1024,3584]{1,0:T(8,128)(2,1)S(1)} %get-tuple-element.218.refs_0_, bf16[1024,3584]{1,0:T(8,128)(2,1)S(1)} %get-tuple-element.219.refs_1_, ...), custom_call_target="tpu_custom_call" | custom-call | flops 15032385536 | tf_op jit(solution)/shard_map/pallas_call | solution.py:195
  185.5 2.4 collective-permute-start.51
  187.9 6.2 %shard_map.93 = (bf16[1024,3584]{1,0:T(8,128)(2,1)}, f32[8,128]{1,0:T(8,128)S(1)}) custom-call(bf16[128,2048]{1,0:T(8,128)(2,1)S(1)} %get-tuple-element.300.mine, bf16[128,2048]{1,0:T(8,128)(2,1)S(1)} %collective-permute-done.39.other, bf16[1024,3584]{1,0:T(8,128)(2,1)S(1)} %get-tuple-element.218.refs_0_, ...), custom_call_target="tpu_custom_call", output_to_operand_aliasing={{0}: (7, {})} | custom-call | flops 15032385536 | tf_op jit(solution)/shard_map/pallas_call | solution.py:195
  197.1 6.2 %shard_map.96 = (bf16[1024,3584]{1,0:T(8,128)(2,1)}, f32[8,128]{1,0:T(8,128)S(1)}) custom-call(bf16[128,2048]{1,0:T(8,128)(2,1)S(1)} %get-tuple-element.298.mine, bf16[128,2048]{1,0:T(8,128)(2,1)S(1)} %collective-permute-done.38.other, bf16[1024,3584]{1,0:T(8,128)(2,1)S(1)} %get-tuple-element.218.refs_0_, ...), custom_call_target="tpu_custom_call", output_to_operand_aliasing={{0}: (7, {})} | custom-call | flops 15032385536 | tf_op jit(solution)/shard_map/pallas_call | solution.py:195
  208.7 6.2 %shard_map.102 = (bf16[1024,3584]{1,0:T(8,128)(2,1)}, f32[8,128]{1,0:T(8,128)S(1)}) custom-call(bf16[128,2048]{1,0:T(8,128)(2,1)S(1)} %get-tuple-element.322.mine, bf16[128,2048]{1,0:T(8,128)(2,1)S(1)} %collective-permute-done.47.other, bf16[1024,3584]{1,0:T(8,128)(2,1)S(1)} %get-tuple-element.218.refs_0_, ...), custom_call_target="tpu_custom_call", output_to_operand_aliasing={{0}: (7, {})} | custom-call | flops 15032385536 | tf_op jit(solution)/shard_map/pallas_call | solution.py:195
  216.8 4.0 %collective-permute-start.59 = (f32[128,3584]{1,0:T(8,128)S(1)}, f32[128,3584]{1,0:T(8,128)S(1)}, u32[]{:S(2)}, u32[]{:S(2)}) collective-permute-start(f32[128,3584]{1,0:T(8,128)S(1)} %get-tuple-element.357), channel_id=1, source_target_pairs={{0,24},{1,25},{2,26},{3,27},{4,28},{5,29},{6,30},{7,31},{8,0},{9,1... | collective-permute-start | bytes 5505032 | tf_op jit(solution)/shard_map/back6/ppermute | solution.py:302
  224.9 6.2 %shard_map.108 = (bf16[1024,3584]{1,0:T(8,128)(2,1)}, f32[8,128]{1,0:T(8,128)S(1)}) custom-call(bf16[128,2048]{1,0:T(8,128)(2,1)S(1)} %get-tuple-element.331.mine, bf16[128,2048]{1,0:T(8,128)(2,1)S(1)} %collective-permute-done.50.other, bf16[1024,3584]{1,0:T(8,128)(2,1)S(1)} %get-tuple-element.218.refs_0_, ...), custom_call_target="tpu_custom_call", output_to_operand_aliasing={{0}: (7, {})} | custom-call | flops 15032385536 | tf_op jit(solution)/shard_map/pallas_call | solution.py:195
  236.8 6.2 %shard_map.112 = (bf16[1024,3584]{1,0:T(8,128)(2,1)}, f32[8,128]{1,0:T(8,128)S(1)}) custom-call(bf16[128,2048]{1,0:T(8,128)(2,1)S(1)} %get-tuple-element.344.mine, bf16[128,2048]{1,0:T(8,128)(2,1)S(1)} %collective-permute-done.54.other, bf16[1024,3584]{1,0:T(8,128)(2,1)S(1)} %get-tuple-element.218.refs_0_, ...), custom_call_target="tpu_custom_call", output_to_operand_aliasing={{0}: (7, {})} | custom-call | flops 15032385536 | tf_op jit(solution)/shard_map/pallas_call | solution.py:195
  245.0 2.3 collective-permute-done.58.other
  247.3 6.2 %shard_map.116 = (bf16[1024,3584]{1,0:T(8,128)(2,1)}, f32[8,128]{1,0:T(8,128)S(1)}) custom-call(bf16[128,2048]{1,0:T(8,128)(2,1)S(1)} %get-tuple-element.356.mine, bf16[128,2048]{1,0:T(8,128)(2,1)S(1)} %collective-permute-done.58.other, bf16[1024,3584]{1,0:T(8,128)(2,1)S(1)} %get-tuple-element.218.refs_0_, ...), custom_call_target="tpu_custom_call", output_to_operand_aliasing={{0}: (7, {})} | custom-call | flops 15032385536 | tf_op jit(solution)/shard_map/pallas_call | solution.py:195
  253.5 5.0 %collective-permute-done.56.other = bf16[128,2048]{1,0:T(8,128)(2,1)S(1)} collective-permute-done((bf16[128,2048]{1,0:T(8,128)(2,1)S(1)}, bf16[128,2048]{1,0:T(8,128)(2,1)S(1)}, u32[]{:S(2)}, u32[]{:S(2)}) %collective-permute-start.56) | collective-permute-done | bytes 524320 | tf_op jit(solution)/shard_map/swap15/ppermute | solution.py:310
  259.5 6.2 %shard_map.117 = (bf16[1024,3584]{1,0:T(8,128)(2,1)}, f32[8,128]{1,0:T(8,128)}) custom-call(bf16[128,2048]{1,0:T(8,128)(2,1)S(1)} %get-tuple-element.354.mine, bf16[128,2048]{1,0:T(8,128)(2,1)S(1)} %collective-permute-done.56.other, bf16[1024,3584]{1,0:T(8,128)(2,1)S(1)} %get-tuple-element.218.refs_0_, ...), custom_call_target="tpu_custom_call", output_to_operand_aliasing={{0}: (7, {})} | custom-call | flops 15032385536 | tf_op jit(solution)/shard_map/pallas_call | solution.py:195
  (162 shorter events, 67.1 us)
Async XLA Ops:
  10.0 12.8 %collective-permute-start.1 = (bf16[64,2048]{1,0:T(8,128)(2,1)S(1)}, bf16[64,2048]{1,0:T(8,128)(2,1)S(1)}, u32[]{:S(2)}, u32[]{:S(2)}) collective-permute-start(bf16[64,2048]{1,0:T(8,128)(2,1)S(1)} %get-tuple-element.192.refs_2_.refs_0_), channel_id=1, source_target_pairs={{0,6},{1,7},{6,4},{7,5},{4,2},{5,3},{10,8},{11,9},{8,14},{9,15},{1... | collective-permute-start | bytes 786440 | tf_op jit(solution)/shard_map/chain4/ppermute | solution.py:288
  47.8 18.6 %collective-permute-start.11 = (bf16[128,2048]{1,0:T(8,128)(2,1)S(1)}, bf16[128,2048]{1,0:T(8,128)(2,1)S(1)}, u32[]{:S(2)}, u32[]{:S(2)}) collective-permute-start(bf16[128,2048]{1,0:T(8,128)(2,1)S(1)} %get-tuple-element.217.mine), channel_id=1, source_target_pairs={{0,1},{1,0},{2,3},{3,2},{4,5},{5,4},{6,7},{7,6},{8,9},{9,8},{10,11... | collective-permute-start | bytes 1572872 | tf_op jit(solution)/shard_map/swap1/ppermute | solution.py:310
  57.3 14.5 %collective-permute-start.10 = (bf16[64,2048]{1,0:T(8,128)(2,1)S(1)}, bf16[64,2048]{1,0:T(8,128)(2,1)S(1)}, u32[]{:S(2)}, u32[]{:S(2)}) collective-permute-start(bf16[64,2048]{1,0:T(8,128)(2,1)S(1)} %get-tuple-element.213.refs_4_.refs_2_.refs_0_), channel_id=1, source_target_pairs={{0,6},{1,7},{6,4},{7,5},{4,2},{5,3},{10,8},{11,9},{8,14},{9,15},{1... | collective-permute-start | bytes 786440 | tf_op jit(solution)/shard_map/chain12/ppermute | solution.py:288
  61.9 13.1 %collective-permute-start.12 = (bf16[64,2048]{1,0:T(8,128)(2,1)S(1)}, bf16[64,2048]{1,0:T(8,128)(2,1)S(1)}, u32[]{:S(2)}, u32[]{:S(2)}) collective-permute-start(bf16[64,2048]{1,0:T(8,128)(2,1)S(1)} %get-tuple-element.216.refs_5_.refs_3_.refs_1_), channel_id=1, source_target_pairs={{0,6},{1,7},{6,4},{7,5},{4,2},{5,3},{10,8},{11,9},{8,14},{9,15},{1... | collective-permute-start | bytes 786440 | tf_op jit(solution)/shard_map/chain13/ppermute | solution.py:288
  66.1 18.9 %collective-permute-start.14 = (bf16[128,2048]{1,0:T(8,128)(2,1)S(1)}, bf16[128,2048]{1,0:T(8,128)(2,1)S(1)}, u32[]{:S(2)}, u32[]{:S(2)}) collective-permute-start(bf16[128,2048]{1,0:T(8,128)(2,1)S(1)} %get-tuple-element.230.mine), channel_id=1, source_target_pairs={{0,1},{1,0},{2,3},{3,2},{4,5},{5,4},{6,7},{7,6},{8,9},{9,8},{10,11... | collective-permute-start | bytes 1572872 | tf_op jit(solution)/shard_map/swap2/ppermute | solution.py:310
  72.6 17.8 %collective-permute-start.13 = (bf16[64,2048]{1,0:T(8,128)(2,1)S(1)}, bf16[64,2048]{1,0:T(8,128)(2,1)S(1)}, u32[]{:S(2)}, u32[]{:S(2)}) collective-permute-start(bf16[64,2048]{1,0:T(8,128)(2,1)S(1)} %get-tuple-element.225.refs_4_.refs_2_.refs_0_), channel_id=1, source_target_pairs={{0,6},{1,7},{6,4},{7,5},{4,2},{5,3},{10,8},{11,9},{8,14},{9,15},{1... | collective-permute-start | bytes 786440 | tf_op jit(solution)/shard_map/chain14/ppermute | solution.py:288
  75.7 15.5 %collective-permute-start.15 = (bf16[64,2048]{1,0:T(8,128)(2,1)S(1)}, bf16[64,2048]{1,0:T(8,128)(2,1)S(1)}, u32[]{:S(2)}, u32[]{:S(2)}) collective-permute-start(bf16[64,2048]{1,0:T(8,128)(2,1)S(1)} %get-tuple-element.229.refs_5_.refs_3_.refs_1_), channel_id=1, source_target_pairs={{0,6},{1,7},{6,4},{7,5},{4,2},{5,3},{10,8},{11,9},{8,14},{9,15},{1... | collective-permute-start | bytes 786440 | tf_op jit(solution)/shard_map/chain15/ppermute | solution.py:288
  77.7 16.2 %collective-permute-start.17 = (bf16[128,2048]{1,0:T(8,128)(2,1)S(1)}, bf16[128,2048]{1,0:T(8,128)(2,1)S(1)}, u32[]{:S(2)}, u32[]{:S(2)}) collective-permute-start(bf16[128,2048]{1,0:T(8,128)(2,1)S(1)} %get-tuple-element.237.mine), channel_id=1, source_target_pairs={{0,1},{1,0},{2,3},{3,2},{4,5},{5,4},{6,7},{7,6},{8,9},{9,8},{10,11... | collective-permute-start | bytes 1572872 | tf_op jit(solution)/shard_map/swap3/ppermute | solution.py:310
  79.0 38.9 %collective-permute-start.22 = (f32[128,3584]{1,0:T(8,128)S(1)}, f32[128,3584]{1,0:T(8,128)S(1)}, u32[]{:S(2)}, u32[]{:S(2)}) collective-permute-start(f32[128,3584]{1,0:T(8,128)S(1)} %get-tuple-element.253), channel_id=1, source_target_pairs={{0,24},{1,25},{2,26},{3,27},{4,28},{5,29},{6,30},{7,31},{8,0},{9,1... | collective-permute-start | bytes 5505032 | tf_op jit(solution)/shard_map/back0/ppermute | solution.py:302
  91.1 11.9 %collective-permute-start.16 = (bf16[64,2048]{1,0:T(8,128)(2,1)S(1)}, bf16[64,2048]{1,0:T(8,128)(2,1)S(1)}, u32[]{:S(2)}, u32[]{:S(2)}) collective-permute-start(bf16[64,2048]{1,0:T(8,128)(2,1)S(1)} %get-tuple-element.234.refs_4_.refs_2_.refs_0_), channel_id=1, source_target_pairs={{0,6},{1,7},{6,4},{7,5},{4,2},{5,3},{10,8},{11,9},{8,14},{9,15},{1... | collective-permute-start | bytes 786440 | tf_op jit(solution)/shard_map/chain16/ppermute | solution.py:288
  92.0 13.4 %collective-permute-start.18 = (bf16[64,2048]{1,0:T(8,128)(2,1)S(1)}, bf16[64,2048]{1,0:T(8,128)(2,1)S(1)}, u32[]{:S(2)}, u32[]{:S(2)}) collective-permute-start(bf16[64,2048]{1,0:T(8,128)(2,1)S(1)} %get-tuple-element.236.refs_5_.refs_3_.refs_1_), channel_id=1, source_target_pairs={{0,6},{1,7},{6,4},{7,5},{4,2},{5,3},{10,8},{11,9},{8,14},{9,15},{1... | collective-permute-start | bytes 786440 | tf_op jit(solution)/shard_map/chain17/ppermute | solution.py:288
  92.2 16.1 %collective-permute-start.20 = (bf16[128,2048]{1,0:T(8,128)(2,1)S(1)}, bf16[128,2048]{1,0:T(8,128)(2,1)S(1)}, u32[]{:S(2)}, u32[]{:S(2)}) collective-permute-start(bf16[128,2048]{1,0:T(8,128)(2,1)S(1)} %get-tuple-element.248.mine), channel_id=1, source_target_pairs={{0,1},{1,0},{2,3},{3,2},{4,5},{5,4},{6,7},{7,6},{8,9},{9,8},{10,11... | collective-permute-start | bytes 1572872 | tf_op jit(solution)/shard_map/swap4/ppermute | solution.py:310
  94.0 41.5 %collective-permute-start.27 = (f32[128,3584]{1,0:T(8,128)S(1)}, f32[128,3584]{1,0:T(8,128)S(1)}, u32[]{:S(2)}, u32[]{:S(2)}) collective-permute-start(f32[128,3584]{1,0:T(8,128)S(1)} %get-tuple-element.266), channel_id=1, source_target_pairs={{0,24},{1,25},{2,26},{3,27},{4,28},{5,29},{6,30},{7,31},{8,0},{9,1... | collective-permute-start | bytes 5505032 | tf_op jit(solution)/shard_map/back1/ppermute | solution.py:302
  103.1 12.9 %collective-permute-start.21 = (bf16[64,2048]{1,0:T(8,128)(2,1)S(1)}, bf16[64,2048]{1,0:T(8,128)(2,1)S(1)}, u32[]{:S(2)}, u32[]{:S(2)}) collective-permute-start(bf16[64,2048]{1,0:T(8,128)(2,1)S(1)} %get-tuple-element.243.refs_6_.refs_4_.refs_2_.refs_0_), channel_id=1, source_target_pairs={{0,6},{1,7},{6,4},{7,5},{4,2},{5,3},{10,8},{11,9},{8,14},{9,15},{1... | collective-permute-start | bytes 786440 | tf_op jit(solution)/shard_map/chain18/ppermute | solution.py:288
  105.3 12.7 %collective-permute-start.23 = (bf16[64,2048]{1,0:T(8,128)(2,1)S(1)}, bf16[64,2048]{1,0:T(8,128)(2,1)S(1)}, u32[]{:S(2)}, u32[]{:S(2)}) collective-permute-start(bf16[64,2048]{1,0:T(8,128)(2,1)S(1)} %get-tuple-element.245.refs_7_.refs_5_.refs_3_.refs_1_), channel_id=1, source_target_pairs={{0,6},{1,7},{6,4},{7,5},{4,2},{5,3},{10,8},{11,9},{8,14},{9,15},{1... | collective-permute-start | bytes 786440 | tf_op jit(solution)/shard_map/chain19/ppermute | solution.py:288
  108.3 15.8 %collective-permute-start.19 = (bf16[128,2048]{1,0:T(8,128)(2,1)S(1)}, bf16[128,2048]{1,0:T(8,128)(2,1)S(1)}, u32[]{:S(2)}, u32[]{:S(2)}) collective-permute-start(bf16[128,2048]{1,0:T(8,128)(2,1)S(1)} %get-tuple-element.247.mine), channel_id=1, source_target_pairs={{0,1},{1,0},{2,3},{3,2},{4,5},{5,4},{6,7},{7,6},{8,9},{9,8},{10,11... | collective-permute-start | bytes 1572872 | tf_op jit(solution)/shard_map/swap5/ppermute | solution.py:310
  116.0 13.5 %collective-permute-start.24 = (bf16[64,2048]{1,0:T(8,128)(2,1)S(1)}, bf16[64,2048]{1,0:T(8,128)(2,1)S(1)}, u32[]{:S(2)}, u32[]{:S(2)}) collective-permute-start(bf16[64,2048]{1,0:T(8,128)(2,1)S(1)} %get-tuple-element.251.refs_6_.refs_4_.refs_2_.refs_0_), channel_id=1, source_target_pairs={{0,6},{1,7},{6,4},{7,5},{4,2},{5,3},{10,8},{11,9},{8,14},{9,15},{1... | collective-permute-start | bytes 786440 | tf_op jit(solution)/shard_map/chain20/ppermute | solution.py:288
  118.1 15.4 %collective-permute-start.25 = (bf16[64,2048]{1,0:T(8,128)(2,1)S(1)}, bf16[64,2048]{1,0:T(8,128)(2,1)S(1)}, u32[]{:S(2)}, u32[]{:S(2)}) collective-permute-start(bf16[64,2048]{1,0:T(8,128)(2,1)S(1)} %get-tuple-element.257.refs_7_.refs_5_.refs_3_.refs_1_), channel_id=1, source_target_pairs={{0,6},{1,7},{6,4},{7,5},{4,2},{5,3},{10,8},{11,9},{8,14},{9,15},{1... | collective-permute-start | bytes 786440 | tf_op jit(solution)/shard_map/chain21/ppermute | solution.py:288
  122.6 13.4 %collective-permute-start.26 = (bf16[128,2048]{1,0:T(8,128)(2,1)S(1)}, bf16[128,2048]{1,0:T(8,128)(2,1)S(1)}, u32[]{:S(2)}, u32[]{:S(2)}) collective-permute-start(bf16[128,2048]{1,0:T(8,128)(2,1)S(1)} %get-tuple-element.264.mine), channel_id=1, source_target_pairs={{0,1},{1,0},{2,3},{3,2},{4,5},{5,4},{6,7},{7,6},{8,9},{9,8},{10,11... | collective-permute-start | bytes 1572872 | tf_op jit(solution)/shard_map/swap6/ppermute | solution.py:310
  129.6 13.2 %collective-permute-start.28 = (bf16[64,2048]{1,0:T(8,128)(2,1)S(1)}, bf16[64,2048]{1,0:T(8,128)(2,1)S(1)}, u32[]{:S(2)}, u32[]{:S(2)}) collective-permute-start(bf16[64,2048]{1,0:T(8,128)(2,1)S(1)} %get-tuple-element.261.refs_6_.refs_4_.refs_2_.refs_0_), channel_id=1, source_target_pairs={{0,6},{1,7},{6,4},{7,5},{4,2},{5,3},{10,8},{11,9},{8,14},{9,15},{1... | collective-permute-start | bytes 786440 | tf_op jit(solution)/shard_map/chain22/ppermute | solution.py:288
  131.5 23.9 %collective-permute-start.32 = (f32[128,3584]{1,0:T(8,128)S(1)}, f32[128,3584]{1,0:T(8,128)S(1)}, u32[]{:S(2)}, u32[]{:S(2)}) collective-permute-start(f32[128,3584]{1,0:T(8,128)S(1)} %get-tuple-element.281), channel_id=1, source_target_pairs={{0,24},{1,25},{2,26},{3,27},{4,28},{5,29},{6,30},{7,31},{8,0},{9,1... | collective-permute-start | bytes 5505032 | tf_op jit(solution)/shard_map/back2/ppermute | solution.py:302
  133.6 11.4 %collective-permute-start.29 = (bf16[64,2048]{1,0:T(8,128)(2,1)S(1)}, bf16[64,2048]{1,0:T(8,128)(2,1)S(1)}, u32[]{:S(2)}, u32[]{:S(2)}) collective-permute-start(bf16[64,2048]{1,0:T(8,128)(2,1)S(1)} %get-tuple-element.263.refs_7_.refs_5_.refs_3_.refs_1_), channel_id=1, source_target_pairs={{0,6},{1,7},{6,4},{7,5},{4,2},{5,3},{10,8},{11,9},{8,14},{9,15},{1... | collective-permute-start | bytes 786440 | tf_op jit(solution)/shard_map/chain23/ppermute | solution.py:288
  135.7 12.7 %collective-permute-start.30 = (bf16[128,2048]{1,0:T(8,128)(2,1)S(1)}, bf16[128,2048]{1,0:T(8,128)(2,1)S(1)}, u32[]{:S(2)}, u32[]{:S(2)}) collective-permute-start(bf16[128,2048]{1,0:T(8,128)(2,1)S(1)} %get-tuple-element.275.mine), channel_id=1, source_target_pairs={{0,1},{1,0},{2,3},{3,2},{4,5},{5,4},{6,7},{7,6},{8,9},{9,8},{10,11... | collective-permute-start | bytes 1572872 | tf_op jit(solution)/shard_map/swap7/ppermute | solution.py:310
  136.0 38.2 %collective-permute-start.37 = (f32[128,3584]{1,0:T(8,128)S(1)}, f32[128,3584]{1,0:T(8,128)S(1)}, u32[]{:S(2)}, u32[]{:S(2)}) collective-permute-start(f32[128,3584]{1,0:T(8,128)S(1)} %get-tuple-element.294), channel_id=1, source_target_pairs={{0,24},{1,25},{2,26},{3,27},{4,28},{5,29},{6,30},{7,31},{8,0},{9,1... | collective-permute-start | bytes 5505032 | tf_op jit(solution)/shard_map/back3/ppermute | solution.py:302
  145.1 12.5 %collective-permute-start.33 = (bf16[64,2048]{1,0:T(8,128)(2,1)S(1)}, bf16[64,2048]{1,0:T(8,128)(2,1)S(1)}, u32[]{:S(2)}, u32[]{:S(2)}) collective-permute-start(bf16[64,2048]{1,0:T(8,128)(2,1)S(1)} %get-tuple-element.274.refs_7_.refs_5_.refs_3_.refs_1_), channel_id=1, source_target_pairs={{0,6},{1,7},{6,4},{7,5},{4,2},{5,3},{10,8},{11,9},{8,14},{9,15},{1... | collective-permute-start | bytes 786440 | tf_op jit(solution)/shard_map/chain25/ppermute | solution.py:288
  148.3 13.5 %collective-permute-start.34 = (bf16[128,2048]{1,0:T(8,128)(2,1)S(1)}, bf16[128,2048]{1,0:T(8,128)(2,1)S(1)}, u32[]{:S(2)}, u32[]{:S(2)}) collective-permute-start(bf16[128,2048]{1,0:T(8,128)(2,1)S(1)} %get-tuple-element.286.mine), channel_id=1, source_target_pairs={{0,1},{1,0},{2,3},{3,2},{4,5},{5,4},{6,7},{7,6},{8,9},{9,8},{10,11... | collective-permute-start | bytes 1572872 | tf_op jit(solution)/shard_map/swap8/ppermute | solution.py:310
  154.0 22.3 %collective-permute-start.40 = (bf16[128,2048]{1,0:T(8,128)(2,1)S(1)}, bf16[128,2048]{1,0:T(8,128)(2,1)S(1)}, u32[]{:S(2)}, u32[]{:S(2)}) collective-permute-start(bf16[128,2048]{1,0:T(8,128)(2,1)S(1)} %get-tuple-element.302.mine), channel_id=1, source_target_pairs={{0,1},{1,0},{2,3},{3,2},{4,5},{5,4},{6,7},{7,6},{8,9},{9,8},{10,11... | collective-permute-start | bytes 1572872 | tf_op jit(solution)/shard_map/swap0/ppermute | solution.py:310
  155.4 11.9 %collective-permute-start.35 = (bf16[64,2048]{1,0:T(8,128)(2,1)S(1)}, bf16[64,2048]{1,0:T(8,128)(2,1)S(1)}, u32[]{:S(2)}, u32[]{:S(2)}) collective-permute-start(bf16[64,2048]{1,0:T(8,128)(2,1)S(1)} %get-tuple-element.279.refs_6_.refs_4_.refs_2_.refs_0_), channel_id=1, source_target_pairs={{0,6},{1,7},{6,4},{7,5},{4,2},{5,3},{10,8},{11,9},{8,14},{9,15},{1... | collective-permute-start | bytes 786440 | tf_op jit(solution)/shard_map/chain26/ppermute | solution.py:288
  157.6 13.1 %collective-permute-start.36 = (bf16[64,2048]{1,0:T(8,128)(2,1)S(1)}, bf16[64,2048]{1,0:T(8,128)(2,1)S(1)}, u32[]{:S(2)}, u32[]{:S(2)}) collective-permute-start(bf16[64,2048]{1,0:T(8,128)(2,1)S(1)} %get-tuple-element.285.refs_7_.refs_5_.refs_3_.refs_1_), channel_id=1, source_target_pairs={{0,6},{1,7},{6,4},{7,5},{4,2},{5,3},{10,8},{11,9},{8,14},{9,15},{1... | collective-permute-start | bytes 786440 | tf_op jit(solution)/shard_map/chain27/ppermute | solution.py:288
  167.4 16.1 %collective-permute-start.41 = (bf16[64,2048]{1,0:T(8,128)(2,1)S(1)}, bf16[64,2048]{1,0:T(8,128)(2,1)S(1)}, u32[]{:S(2)}, u32[]{:S(2)}) collective-permute-start(bf16[64,2048]{1,0:T(8,128)(2,1)S(1)} %get-tuple-element.290.refs_6_.refs_4_.refs_2_.refs_0_), channel_id=1, source_target_pairs={{0,6},{1,7},{6,4},{7,5},{4,2},{5,3},{10,8},{11,9},{8,14},{9,15},{1... | collective-permute-start | bytes 786440 | tf_op jit(solution)/shard_map/chain28/ppermute | solution.py:288
  169.3 16.2 %collective-permute-start.39 = (bf16[128,2048]{1,0:T(8,128)(2,1)S(1)}, bf16[128,2048]{1,0:T(8,128)(2,1)S(1)}, u32[]{:S(2)}, u32[]{:S(2)}) collective-permute-start(bf16[128,2048]{1,0:T(8,128)(2,1)S(1)} %get-tuple-element.300.mine), channel_id=1, source_target_pairs={{0,1},{1,0},{2,3},{3,2},{4,5},{5,4},{6,7},{7,6},{8,9},{9,8},{10,11... | collective-permute-start | bytes 1572872 | tf_op jit(solution)/shard_map/swap9/ppermute | solution.py:310
  170.7 34.6 %collective-permute-start.44 = (f32[128,3584]{1,0:T(8,128)S(1)}, f32[128,3584]{1,0:T(8,128)S(1)}, u32[]{:S(2)}, u32[]{:S(2)}) collective-permute-start(f32[128,3584]{1,0:T(8,128)S(1)} %get-tuple-element.317), channel_id=1, source_target_pairs={{0,24},{1,25},{2,26},{3,27},{4,28},{5,29},{6,30},{7,31},{8,0},{9,1... | collective-permute-start | bytes 5505032 | tf_op jit(solution)/shard_map/back4/ppermute | solution.py:302
  174.2 20.0 %collective-permute-start.42 = (bf16[64,2048]{1,0:T(8,128)(2,1)S(1)}, bf16[64,2048]{1,0:T(8,128)(2,1)S(1)}, u32[]{:S(2)}, u32[]{:S(2)}) collective-permute-start(bf16[64,2048]{1,0:T(8,128)(2,1)S(1)} %get-tuple-element.292.refs_7_.refs_5_.refs_3_.refs_1_), channel_id=1, source_target_pairs={{0,6},{1,7},{6,4},{7,5},{4,2},{5,3},{10,8},{11,9},{8,14},{9,15},{1... | collective-permute-start | bytes 786440 | tf_op jit(solution)/shard_map/chain29/ppermute | solution.py:288
  176.3 20.0 %collective-permute-start.38 = (bf16[128,2048]{1,0:T(8,128)(2,1)S(1)}, bf16[128,2048]{1,0:T(8,128)(2,1)S(1)}, u32[]{:S(2)}, u32[]{:S(2)}) collective-permute-start(bf16[128,2048]{1,0:T(8,128)(2,1)S(1)} %get-tuple-element.298.mine), channel_id=1, source_target_pairs={{0,1},{1,0},{2,3},{3,2},{4,5},{5,4},{6,7},{7,6},{8,9},{9,8},{10,11... | collective-permute-start | bytes 1572872 | tf_op jit(solution)/shard_map/swap10/ppermute | solution.py:310
  183.6 19.7 %collective-permute-start.43 = (bf16[64,2048]{1,0:T(8,128)(2,1)S(1)}, bf16[64,2048]{1,0:T(8,128)(2,1)S(1)}, u32[]{:S(2)}, u32[]{:S(2)}) collective-permute-start(bf16[64,2048]{1,0:T(8,128)(2,1)S(1)} %get-tuple-element.309.refs_6_.refs_4_.refs_2_.refs_0_), channel_id=1, source_target_pairs={{0,6},{1,7},{6,4},{7,5},{4,2},{5,3},{10,8},{11,9},{8,14},{9,15},{1... | collective-permute-start | bytes 786440 | tf_op jit(solution)/shard_map/chain30/ppermute | solution.py:288
  185.5 37.3 %collective-permute-start.51 = (f32[128,3584]{1,0:T(8,128)S(1)}, f32[128,3584]{1,0:T(8,128)S(1)}, u32[]{:S(2)}, u32[]{:S(2)}) collective-permute-start(f32[128,3584]{1,0:T(8,128)S(1)} %get-tuple-element.335), channel_id=1, source_target_pairs={{0,24},{1,25},{2,26},{3,27},{4,28},{5,29},{6,30},{7,31},{8,0},{9,1... | collective-permute-start | bytes 5505032 | tf_op jit(solution)/shard_map/back5/ppermute | solution.py:302
  196.3 12.4 %collective-permute-start.47 = (bf16[128,2048]{1,0:T(8,128)(2,1)S(1)}, bf16[128,2048]{1,0:T(8,128)(2,1)S(1)}, u32[]{:S(2)}, u32[]{:S(2)}) collective-permute-start(bf16[128,2048]{1,0:T(8,128)(2,1)S(1)} %get-tuple-element.322.mine), channel_id=1, source_target_pairs={{0,1},{1,0},{2,3},{3,2},{4,5},{5,4},{6,7},{7,6},{8,9},{9,8},{10,11... | collective-permute-start | bytes 1572872 | tf_op jit(solution)/shard_map/swap11/ppermute | solution.py:310
  203.4 11.5 %collective-permute-start.46 = (bf16[64,2048]{1,0:T(8,128)(2,1)S(1)}, bf16[64,2048]{1,0:T(8,128)(2,1)S(1)}, u32[]{:S(2)}, u32[]{:S(2)}) collective-permute-start(bf16[64,2048]{1,0:T(8,128)(2,1)S(1)} %get-tuple-element.315.refs_6_.refs_4_.refs_2_.refs_0_), channel_id=1, source_target_pairs={{0,6},{1,7},{6,4},{7,5},{4,2},{5,3},{10,8},{11,9},{8,14},{9,15},{1... | collective-permute-start | bytes 786440 | tf_op jit(solution)/shard_map/chain32/ppermute | solution.py:288
  205.4 15.5 %collective-permute-start.48 = (bf16[64,2048]{1,0:T(8,128)(2,1)S(1)}, bf16[64,2048]{1,0:T(8,128)(2,1)S(1)}, u32[]{:S(2)}, u32[]{:S(2)}) collective-permute-start(bf16[64,2048]{1,0:T(8,128)(2,1)S(1)} %get-tuple-element.321.refs_7_.refs_5_.refs_3_.refs_1_), channel_id=1, source_target_pairs={{0,6},{1,7},{6,4},{7,5},{4,2},{5,3},{10,8},{11,9},{8,14},{9,15},{1... | collective-permute-start | bytes 786440 | tf_op jit(solution)/shard_map/chain33/ppermute | solution.py:288
  207.5 16.5 %collective-permute-start.50 = (bf16[128,2048]{1,0:T(8,128)(2,1)S(1)}, bf16[128,2048]{1,0:T(8,128)(2,1)S(1)}, u32[]{:S(2)}, u32[]{:S(2)}) collective-permute-start(bf16[128,2048]{1,0:T(8,128)(2,1)S(1)} %get-tuple-element.331.mine), channel_id=1, source_target_pairs={{0,1},{1,0},{2,3},{3,2},{4,5},{5,4},{6,7},{7,6},{8,9},{9,8},{10,11... | collective-permute-start | bytes 1572872 | tf_op jit(solution)/shard_map/swap12/ppermute | solution.py:310
  214.9 16.2 %collective-permute-start.49 = (bf16[64,2048]{1,0:T(8,128)(2,1)S(1)}, bf16[64,2048]{1,0:T(8,128)(2,1)S(1)}, u32[]{:S(2)}, u32[]{:S(2)}) collective-permute-start(bf16[64,2048]{1,0:T(8,128)(2,1)S(1)} %get-tuple-element.328.refs_6_.refs_4_.refs_2_), channel_id=1, source_target_pairs={{0,6},{1,7},{6,4},{7,5},{4,2},{5,3},{10,8},{11,9},{8,14},{9,15},{1... | collective-permute-start | bytes 786440 | tf_op jit(solution)/shard_map/chain34/ppermute | solution.py:288
  216.8 30.5 %collective-permute-start.59 = (f32[128,3584]{1,0:T(8,128)S(1)}, f32[128,3584]{1,0:T(8,128)S(1)}, u32[]{:S(2)}, u32[]{:S(2)}) collective-permute-start(f32[128,3584]{1,0:T(8,128)S(1)} %get-tuple-element.357), channel_id=1, source_target_pairs={{0,24},{1,25},{2,26},{3,27},{4,28},{5,29},{6,30},{7,31},{8,0},{9,1... | collective-permute-start | bytes 5505032 | tf_op jit(solution)/shard_map/back6/ppermute | solution.py:302
  220.9 12.2 %collective-permute-start.52 = (bf16[64,2048]{1,0:T(8,128)(2,1)S(1)}, bf16[64,2048]{1,0:T(8,128)(2,1)S(1)}, u32[]{:S(2)}, u32[]{:S(2)}) collective-permute-start(bf16[64,2048]{1,0:T(8,128)(2,1)S(1)} %get-tuple-element.330.refs_7_.refs_5_.refs_3_), channel_id=1, source_target_pairs={{0,6},{1,7},{6,4},{7,5},{4,2},{5,3},{10,8},{11,9},{8,14},{9,15},{1... | collective-permute-start | bytes 786440 | tf_op jit(solution)/shard_map/chain35/ppermute | solution.py:288
  223.0 12.7 %collective-permute-start.54 = (bf16[128,2048]{1,0:T(8,128)(2,1)S(1)}, bf16[128,2048]{1,0:T(8,128)(2,1)S(1)}, u32[]{:S(2)}, u32[]{:S(2)}) collective-permute-start(bf16[128,2048]{1,0:T(8,128)(2,1)S(1)} %get-tuple-element.344.mine), channel_id=1, source_target_pairs={{0,1},{1,0},{2,3},{3,2},{4,5},{5,4},{6,7},{7,6},{8,9},{9,8},{10,11... | collective-permute-start | bytes 1572872 | tf_op jit(solution)/shard_map/swap13/ppermute | solution.py:310
  224.0 35.5 %collective-permute-start.57 = (f32[128,3584]{1,0:T(8,128)S(1)}, f32[128,3584]{1,0:T(8,128)S(1)}, u32[]{:S(2)}, u32[]{:S(2)}) collective-permute-start(f32[128,3584]{1,0:T(8,128)S(1)} %get-tuple-element.355), channel_id=1, source_target_pairs={{0,24},{1,25},{2,26},{3,27},{4,28},{5,29},{6,30},{7,31},{8,0},{9,1... | collective-permute-start | bytes 5505032 | tf_op jit(solution)/shard_map/back7/ppermute | solution.py:302
  231.2 11.8 %collective-permute-start.53 = (bf16[64,2048]{1,0:T(8,128)(2,1)S(1)}, bf16[64,2048]{1,0:T(8,128)(2,1)S(1)}, u32[]{:S(2)}, u32[]{:S(2)}) collective-permute-start(bf16[64,2048]{1,0:T(8,128)(2,1)S(1)} %get-tuple-element.341.refs_6_.refs_4_), channel_id=1, source_target_pairs={{0,6},{1,7},{6,4},{7,5},{4,2},{5,3},{10,8},{11,9},{8,14},{9,15},{1... | collective-permute-start | bytes 786440 | tf_op jit(solution)/shard_map/chain36/ppermute | solution.py:288
  235.6 11.7 %collective-permute-start.58 = (bf16[128,2048]{1,0:T(8,128)(2,1)S(1)}, bf16[128,2048]{1,0:T(8,128)(2,1)S(1)}, u32[]{:S(2)}, u32[]{:S(2)}) collective-permute-start(bf16[128,2048]{1,0:T(8,128)(2,1)S(1)} %get-tuple-element.356.mine), channel_id=1, source_target_pairs={{0,1},{1,0},{2,3},{3,2},{4,5},{5,4},{6,7},{7,6},{8,9},{9,8},{10,11... | collective-permute-start | bytes 1572872 | tf_op jit(solution)/shard_map/swap14/ppermute | solution.py:310
  243.6 15.0 %collective-permute-start.56 = (bf16[128,2048]{1,0:T(8,128)(2,1)S(1)}, bf16[128,2048]{1,0:T(8,128)(2,1)S(1)}, u32[]{:S(2)}, u32[]{:S(2)}) collective-permute-start(bf16[128,2048]{1,0:T(8,128)(2,1)S(1)} %get-tuple-element.354.mine), channel_id=1, source_target_pairs={{0,1},{1,0},{2,3},{3,2},{4,5},{5,4},{6,7},{7,6},{8,9},{9,8},{10,11... | collective-permute-start | bytes 1572872 | tf_op jit(solution)/shard_map/swap15/ppermute | solution.py:310
  (12 other events, 117.7 us)
